TPU v7x, 128 devices: a whole 4x4x4 slice. The times are simulated.
128 devices in a mesh: rows: 32 (over y, x_lo, z), cols: 4 (over x_hi, core).
Axes of the slice: x: 4 (x_hi: 2, x_lo: 2; x = x_hi * 2 + x_lo), y: 4, z: 4, core: 2. Of those that a mesh axis runs over, the one named last changes fastest.
Arguments:
- features_in: bfloat16 [1024, 512, 128], P('rows', 'cols'), may hold values from -6 to 6
- cotangent: bfloat16 [1024, 512, 128], P('rows', 'cols'), may hold values from -6 to 6
- depth_kernels: bfloat16 [8, 9, 128], replicated, may hold values from -2 to 2
- point_weights: bfloat16 [8, 128, 128], replicated, may hold values from -0.5 to 0.5
- coarse_weight: bfloat16 [128, 128], replicated, may hold values from -4 to 4
Outputs:
- output: bfloat16 [1024, 512, 128], P('rows', 'cols')
- input_grad: bfloat16 [1024, 512, 128], P('rows', 'cols')
- weight_grads: float32 [9, 128, 128], P(None, 'rows')
All inputs are finite; a program needn't handle non-finite values.
Results may differ from a plain program's by a relative error of at most 0.039.
Values may be sent and summed in bfloat16 or wider, within the bound.
No kernel may reach another device: no remote copies, remote signals or barrier semaphores. Data moves between devices by JAX's collectives and lax.ppermute only.
A program may use at most 128 MiB of HBM per device.

v0:
```python
import jax
import jax.numpy as jnp
from jax import lax
from jax.sharding import PartitionSpec as P

STRIDE = 8


def extended(cells, sides, width):
    for axis, dim in sides:
        count = lax.axis_size(axis)
        ends = count - 1
        head = lax.slice_in_dim(cells, 0, width, axis=dim)
        tail = lax.slice_in_dim(cells, cells.shape[dim] - width, cells.shape[dim], axis=dim)
        cells = jnp.concatenate(
            [
                lax.ppermute(tail, axis, [(i, (i + 1) % count) for i in range(ends)]),
                cells,
                lax.ppermute(head, axis, [((i + 1) % count, i) for i in range(ends)]),
            ],
            axis=dim,
        )
    return cells


def gelu_tanh(value):
    return jax.nn.gelu(value, approximate=True)


def taps(padded, kernel, dilate, base, height, breadth, sign):
    total = jnp.zeros((height, breadth, padded.shape[2]), jnp.float32)
    for shift_row in (-1, 0, 1):
        for shift_col in (-1, 0, 1):
            index = (shift_row + 1) * 3 + (shift_col + 1)
            start_row = base + sign * shift_row * dilate
            start_col = base + sign * shift_col * dilate
            piece = padded[start_row : start_row + height, start_col : start_col + breadth, :]
            total = total + kernel[index].astype(jnp.float32) * piece.astype(jnp.float32)
    return total


def pointwise(hidden, weight):
    height, breadth, channels = hidden.shape
    mixed = jnp.dot(hidden.reshape(-1, channels), weight, preferred_element_type=jnp.float32)
    return mixed.reshape(height, breadth, channels)


def local(features_in, cotangent, depth_kernels, point_weights, coarse_weight):
    height, breadth, channels = features_in.shape
    layers = depth_kernels.shape[0]
    contract = (((0,), (0,)), ((), ()))
    preacts = []
    hiddens = []
    x_now = features_in
    for layer in range(layers):
        dilate = 2 ** (layer % 4)
        padded = extended(x_now, (("rows", 0), ("cols", 1)), dilate)
        preact = taps(padded, depth_kernels[layer], dilate, dilate, height, breadth, 1)
        hidden = gelu_tanh(preact).astype(jnp.bfloat16)
        x_now = (x_now.astype(jnp.float32) + pointwise(hidden, point_weights[layer])).astype(
            jnp.bfloat16
        )
        preacts.append(preact)
        hiddens.append(hidden)
    blocks = (height // STRIDE, STRIDE, breadth // STRIDE, STRIDE, channels)
    pooled = features_in.astype(jnp.float32).reshape(blocks).mean(axis=(1, 3)).astype(jnp.bfloat16)
    coarse = jnp.dot(
        pooled.reshape(-1, channels), coarse_weight, preferred_element_type=jnp.float32
    )
    coarse = coarse.reshape(height // STRIDE, 1, breadth // STRIDE, 1, channels)
    output = (
        (x_now.astype(jnp.float32).reshape(blocks) + coarse)
        .reshape(height, breadth, channels)
        .astype(jnp.bfloat16)
    )
    block_cot = cotangent.astype(jnp.float32).reshape(blocks).sum(axis=(1, 3)).astype(jnp.bfloat16)
    coarse_grad = lax.dot_general(
        pooled.reshape(-1, channels),
        block_cot.reshape(-1, channels),
        contract,
        preferred_element_type=jnp.float32,
    )
    back = jnp.dot(
        block_cot.reshape(-1, channels), coarse_weight.T, preferred_element_type=jnp.float32
    ) / (STRIDE * STRIDE)
    back = back.reshape(height // STRIDE, 1, breadth // STRIDE, 1, channels)
    upstream = cotangent.astype(jnp.float32)
    grads = [None] * layers
    for layer in range(layers - 1, -1, -1):
        dilate = 2 ** (layer % 4)
        up_b = upstream.astype(jnp.bfloat16).reshape(-1, channels)
        grads[layer] = lax.dot_general(
            hiddens[layer].reshape(-1, channels), up_b, contract, preferred_element_type=jnp.float32
        )
        hid_grad = jnp.dot(
            up_b, point_weights[layer].T, preferred_element_type=jnp.float32
        ).reshape(height, breadth, channels)
        pull = jax.vjp(gelu_tanh, preacts[layer])[1]
        pre_grad = pull(hid_grad)[0]
        padded = extended(pre_grad.astype(jnp.bfloat16), (("rows", 0), ("cols", 1)), dilate).astype(
            pre_grad.dtype
        )
        upstream = upstream + taps(
            padded, depth_kernels[layer], dilate, dilate, height, breadth, -1
        )
    input_grad = (
        (upstream.reshape(blocks) + back).reshape(height, breadth, channels).astype(jnp.bfloat16)
    )
    partial_grads = jnp.stack(grads + [coarse_grad])
    summed = lax.psum(partial_grads.astype(jnp.bfloat16), "cols")
    weight_grads = lax.psum_scatter(summed, "rows", scatter_dimension=1, tiled=True).astype(
        jnp.float32
    )
    return (output, input_grad, weight_grads)


def solution(mesh):
    in_specs = (P("rows", "cols", None), P("rows", "cols", None), P(), P(), P())
    out_specs = (P("rows", "cols", None), P("rows", "cols", None), P(None, "rows", None))
    return jax.shard_map(local, mesh=mesh, in_specs=in_specs, out_specs=out_specs, check_vma=False)
```

profile of v0, /device:TPU:1, one launch (start us, length us, event | category | flops | bytes accessed | tf_op | source)
XLA Modules:
  0.0 729.9 jit_solution(10321325402022438136)
XLA Ops:
  17.4 6.5 collective-permute-start.2
  74.8 4.9 collective-permute-done.11
  101.8 5.3 collective-permute-done.15
  125.7 4.6 collective-permute-done.19
  158.9 4.7 collective-permute-start.24
  185.2 4.7 collective-permute-start.28
  202.3 5.5 collective-permute-done.31
  213.6 4.7 collective-permute-start.32
  230.7 5.5 collective-permute-done.35
  239.9 4.6 collective-permute-start.36
  255.6 4.7 collective-permute-done.39
  264.5 4.6 collective-permute-start.40
  279.5 4.6 collective-permute-done.43
  288.4 4.7 collective-permute-start.44
  303.1 4.6 collective-permute-done.47
  312.2 4.7 collective-permute-start.48
  329.5 5.3 collective-permute-done.51
  339.2 4.6 collective-permute-start.52
  356.0 4.8 collective-permute-done.55
  366.7 4.6 collective-permute-start.56
  404.6 4.7 collective-permute-start.60
  414.9 6.0 collective-permute-start.62
  432.5 266.3 %all-reduce.3.cloned.1.call-done = bf16[9,128,128]{2,1,0:T(8,128)(2,1)} async-done(((bf16[9,128,128]{2,1,0:T(8,128)(2,1)}), bf16[9,128,128]{2,1,0:T(8,128)(2,1)}) %all-reduce.3.cloned.1.call-update) | async-done | bytes 294928
  699.5 22.4 %psum.8 = bf16[9,4,128]{2,1,0:T(4,128)(2,1)S(1)} all-reduce(bf16[9,4,128]{2,1,0:T(4,128)(2,1)S(1)} %constant_dynamic-slice_fusion), channel_id=1, replica_groups=mesh['rows'=32,'cols'=4] {'cols'}, use_global_device_ids=true, to_apply=%region_2.0 | all-reduce | flops 4608 | bytes 18432 | tf_op jit(solution)/shard_map/psum | solution.py:110
  (372 shorter events, 315.0 us)
Async XLA Ops:
  7.2 691.6 %all-reduce.3.cloned.1.call-start = ((), (), s32[]{:S(2)}) async-start(), calls=%async_computation | async-start | bytes 589824
  17.4 8.6 %collective-permute-start.2 = (bf16[34,1,128]{2,1,0:T(2,128)(2,1)S(1)}, bf16[34,1,128]{2,1,0:T(2,128)(2,1)S(1)}, u32[]{:S(2)}, u32[]{:S(2)}) collective-permute-start(bf16[34,1,128]{2,1,0:T(2,128)(2,1)S(1)} %get-tuple-element.47), channel_id=1, source_target_pairs={{0,1},{1,2},{2,3},{4,5},{5,6},{6,7},{8,9},{9,10},{10,11},{12,13},{... | collective-permute-start | bytes 26120 | tf_op jit(solution)/shard_map/ppermute | solution.py:17
  72.9 6.8 collective-permute-start.11
  85.4 7.0 collective-permute-start.12
  89.1 7.4 %collective-permute-start.13 = (bf16[8,128,128]{2,1,0:T(8,128)(2,1)S(1)}, bf16[8,128,128]{2,1,0:T(8,128)(2,1)S(1)}, u32[]{:S(2)}, u32[]{:S(2)}) collective-permute-start(bf16[8,128,128]{2,1,0:T(8,128)(2,1)S(1)} %get-tuple-element.74), channel_id=1, source_target_pairs={{4,0},{8,4},{12,8},{16,12},{20,16},{24,20},{28,24},{32,28},{36,32}... | collective-permute-start | bytes 786440 | tf_op jit(solution)/shard_map/ppermute | solution.py:19
  99.6 7.4 %collective-permute-start.15 = (bf16[48,8,128]{2,1,0:T(8,128)(2,1)S(1)}, bf16[48,8,128]{2,1,0:T(8,128)(2,1)S(1)}, u32[]{:S(2)}, u32[]{:S(2)}) collective-permute-start(bf16[48,8,128]{2,1,0:T(8,128)(2,1)S(1)} %get-tuple-element.14), channel_id=1, source_target_pairs={{1,0},{2,1},{3,2},{5,4},{6,5},{7,6},{9,8},{10,9},{11,10},{13,12},{... | collective-permute-start | bytes 294920 | tf_op jit(solution)/shard_map/ppermute | solution.py:19
  172.7 6.8 collective-permute-start.27
  185.2 7.9 %collective-permute-start.28 = (bf16[8,128,128]{2,1,0:T(8,128)(2,1)S(1)}, bf16[8,128,128]{2,1,0:T(8,128)(2,1)S(1)}, u32[]{:S(2)}, u32[]{:S(2)}) collective-permute-start(bf16[8,128,128]{2,1,0:T(8,128)(2,1)S(1)} %get-tuple-element.65), channel_id=1, source_target_pairs={{0,4},{4,8},{8,12},{12,16},{16,20},{20,24},{24,28},{28,32},{32,36}... | collective-permute-start | bytes 786440 | tf_op jit(solution)/shard_map/ppermute | solution.py:17
  189.9 7.4 %collective-permute-start.29 = (bf16[8,128,128]{2,1,0:T(8,128)(2,1)S(1)}, bf16[8,128,128]{2,1,0:T(8,128)(2,1)S(1)}, u32[]{:S(2)}, u32[]{:S(2)}) collective-permute-start(bf16[8,128,128]{2,1,0:T(8,128)(2,1)S(1)} %get-tuple-element.66), channel_id=1, source_target_pairs={{4,0},{8,4},{12,8},{16,12},{20,16},{24,20},{28,24},{32,28},{36,32}... | collective-permute-start | bytes 786440 | tf_op jit(solution)/shard_map/ppermute | solution.py:19
  200.4 7.4 %collective-permute-start.31 = (bf16[48,8,128]{2,1,0:T(8,128)(2,1)S(1)}, bf16[48,8,128]{2,1,0:T(8,128)(2,1)S(1)}, u32[]{:S(2)}, u32[]{:S(2)}) collective-permute-start(bf16[48,8,128]{2,1,0:T(8,128)(2,1)S(1)} %get-tuple-element.10), channel_id=1, source_target_pairs={{1,0},{2,1},{3,2},{5,4},{6,5},{7,6},{9,8},{10,9},{11,10},{13,12},{... | collective-permute-start | bytes 294920 | tf_op jit(solution)/shard_map/ppermute | solution.py:19
  213.6 7.9 %collective-permute-start.32 = (bf16[8,128,128]{2,1,0:T(8,128)(2,1)S(1)}, bf16[8,128,128]{2,1,0:T(8,128)(2,1)S(1)}, u32[]{:S(2)}, u32[]{:S(2)}) collective-permute-start(bf16[8,128,128]{2,1,0:T(8,128)(2,1)S(1)} %get-tuple-element.63), channel_id=1, source_target_pairs={{0,4},{4,8},{8,12},{12,16},{16,20},{20,24},{24,28},{28,32},{32,36}... | collective-permute-start | bytes 786440 | tf_op jit(solution)/shard_map/ppermute | solution.py:17
  218.3 7.4 %collective-permute-start.33 = (bf16[8,128,128]{2,1,0:T(8,128)(2,1)S(1)}, bf16[8,128,128]{2,1,0:T(8,128)(2,1)S(1)}, u32[]{:S(2)}, u32[]{:S(2)}) collective-permute-start(bf16[8,128,128]{2,1,0:T(8,128)(2,1)S(1)} %get-tuple-element.64), channel_id=1, source_target_pairs={{4,0},{8,4},{12,8},{16,12},{20,16},{24,20},{28,24},{32,28},{36,32}... | collective-permute-start | bytes 786440 | tf_op jit(solution)/shard_map/ppermute | solution.py:19
  228.7 7.4 %collective-permute-start.35 = (bf16[48,8,128]{2,1,0:T(8,128)(2,1)S(1)}, bf16[48,8,128]{2,1,0:T(8,128)(2,1)S(1)}, u32[]{:S(2)}, u32[]{:S(2)}) collective-permute-start(bf16[48,8,128]{2,1,0:T(8,128)(2,1)S(1)} %get-tuple-element.6), channel_id=1, source_target_pairs={{1,0},{2,1},{3,2},{5,4},{6,5},{7,6},{9,8},{10,9},{11,10},{13,12},{... | collective-permute-start | bytes 294920 | tf_op jit(solution)/shard_map/ppermute | solution.py:19
  253.5 6.8 collective-permute-start.39
  312.2 7.9 %collective-permute-start.48 = (bf16[8,128,128]{2,1,0:T(8,128)(2,1)S(1)}, bf16[8,128,128]{2,1,0:T(8,128)(2,1)S(1)}, u32[]{:S(2)}, u32[]{:S(2)}) collective-permute-start(bf16[8,128,128]{2,1,0:T(8,128)(2,1)S(1)} %get-tuple-element.55), channel_id=1, source_target_pairs={{0,4},{4,8},{8,12},{12,16},{16,20},{20,24},{24,28},{28,32},{32,36}... | collective-permute-start | bytes 786440 | tf_op jit(solution)/shard_map/ppermute | solution.py:17
  316.8 7.4 %collective-permute-start.49 = (bf16[8,128,128]{2,1,0:T(8,128)(2,1)S(1)}, bf16[8,128,128]{2,1,0:T(8,128)(2,1)S(1)}, u32[]{:S(2)}, u32[]{:S(2)}) collective-permute-start(bf16[8,128,128]{2,1,0:T(8,128)(2,1)S(1)} %get-tuple-element.56), channel_id=1, source_target_pairs={{4,0},{8,4},{12,8},{16,12},{20,16},{24,20},{28,24},{32,28},{36,32}... | collective-permute-start | bytes 786440 | tf_op jit(solution)/shard_map/ppermute | solution.py:19
  327.3 7.4 %collective-permute-start.51 = (bf16[48,8,128]{2,1,0:T(8,128)(2,1)S(1)}, bf16[48,8,128]{2,1,0:T(8,128)(2,1)S(1)}, u32[]{:S(2)}, u32[]{:S(2)}) collective-permute-start(bf16[48,8,128]{2,1,0:T(8,128)(2,1)S(1)} %get-tuple-element.4), channel_id=1, source_target_pairs={{1,0},{2,1},{3,2},{5,4},{6,5},{7,6},{9,8},{10,9},{11,10},{13,12},{... | collective-permute-start | bytes 294920 | tf_op jit(solution)/shard_map/ppermute | solution.py:19
  339.2 6.9 collective-permute-start.52
  353.7 7.1 collective-permute-start.55
  366.7 8.0 %collective-permute-start.56 = (bf16[2,128,128]{2,1,0:T(8,128)(2,1)S(1)}, bf16[2,128,128]{2,1,0:T(8,128)(2,1)S(1)}, u32[]{:S(2)}, u32[]{:S(2)}) collective-permute-start(bf16[2,128,128]{2,1,0:T(8,128)(2,1)S(1)} %get-tuple-element.51), channel_id=1, source_target_pairs={{0,4},{4,8},{8,12},{12,16},{16,20},{20,24},{24,28},{28,32},{32,36}... | collective-permute-start | bytes 196616 | tf_op jit(solution)/shard_map/ppermute | solution.py:17
  376.6 8.3 %collective-permute-start.58 = (bf16[36,2,128]{2,1,0:T(2,128)(2,1)S(1)}, bf16[36,2,128]{2,1,0:T(2,128)(2,1)S(1)}, u32[]{:S(2)}, u32[]{:S(2)}) collective-permute-start(bf16[36,2,128]{2,1,0:T(2,128)(2,1)S(1)} %get-tuple-element.27), channel_id=1, source_target_pairs={{0,1},{1,2},{2,3},{4,5},{5,6},{6,7},{8,9},{9,10},{10,11},{12,13},{... | collective-permute-start | bytes 55304 | tf_op jit(solution)/shard_map/ppermute | solution.py:17
  404.6 6.9 collective-permute-start.60
  414.9 9.0 %collective-permute-start.62 = (bf16[34,1,128]{2,1,0:T(2,128)(2,1)}, bf16[34,1,128]{2,1,0:T(2,128)(2,1)}, u32[]{:S(2)}, u32[]{:S(2)}) collective-permute-start(bf16[34,1,128]{2,1,0:T(2,128)(2,1)} %get-tuple-element.39), channel_id=1, source_target_pairs={{0,1},{1,2},{2,3},{4,5},{5,6},{6,7},{8,9},{9,10},{10,11},{12,13},{... | collective-permute-start | bytes 26120 | tf_op jit(solution)/shard_map/ppermute | solution.py:17
  420.9 6.9 collective-permute-start.63
  (121 other events, 1982.1 us)
Sparse Core Ops, SparseCore 0:
  423.9 274.8 all-reduce.2
where the time goes:
time: 740 us; the launch traced here: 730 us
  waiting for transfers between devices  408 us (55%)
  starting transfers between devices  177 us (24%)
  other arithmetic  58.5 us (8%)
  matrix products  32.4 us (4%)
  blocking collectives  22.4 us (3%)
  between operations  17.4 us (2%)
  local copies, waits for them, and re-layouts  13.3 us (2%)
    unnamed x2, waiting for transfers between devices  266 us
    ppermute x32, waiting for transfers between devices, extended(): lax.ppermute(head, axis, [((i + 1) % count, i) for i in range(ends)])  132 us
    ppermute x32, starting transfers between devices, extended(): lax.ppermute(tail, axis, [(i, (i + 1) % count) for i in range(ends)])  125 us
    ppermute x32, starting transfers between devices, extended(): lax.ppermute(head, axis, [((i + 1) % count, i) for i in range(ends)])  52.7 us
    add x8, other arithmetic, taps(): total + kernel[index].astype(jnp.float32) * piece.astype(jnp.float32)  23 us
    psum x1, blocking collectives, local(): summed = lax.psum(partial_grads.astype(jnp.bfloat16), 'cols')  22.4 us
  transfers between devices with their start and end apart: 65, of which 41 were waited for; matrix products, arithmetic and copies ran while one was open for 2% of the time, Pallas kernels for 0%

commit v1 on v0

v1 whole, which is shorter than its diff:
```python
import functools

import jax
import jax.numpy as jnp
from jax import lax
from jax.experimental import pallas as pl
from jax.experimental.pallas import tpu as pltpu
from jax.sharding import PartitionSpec as P

STRIDE = 8
F32 = jnp.float32
BF = jnp.bfloat16
C0 = 0.7978845608028654
C1 = 0.7978845608028654 * 0.044715

ROWS, COLS, CH = 32, 128, 128
RH, CHALO = 15, 16
WIDE = COLS + 2 * CHALO
PAD = 8

HALO = (14, 12, 8, 0)
SPAN = ((0, 160), (0, 160), (8, 152), (16, 144))
DHALO = (2, 4, 8, 0)
DSPAN = ((8, 152), (8, 152), (8, 152), (16, 144))
BLOCK = (15, 14, 16, 16)

VMEM = pl.BlockSpec(memory_space=pltpu.VMEM)
SMEM = pl.BlockSpec(memory_space=pltpu.SMEM)
ANY = pl.BlockSpec(memory_space=pl.ANY)


def sds(shape, dtype):
    return jax.ShapeDtypeStruct(shape, dtype)


def gelu_parts(half, want_slope):
    square = half * half
    t = jnp.tanh(half * (2 * C0 + 8 * C1 * square))
    half_t = half * t
    hidden = half + half_t
    if not want_slope:
        return hidden, None
    slope = (0.5 + 0.5 * t) + (half - half_t * t) * (C0 + 12 * C1 * square)
    return hidden, slope


def rows_of(kernel, scale):
    return [jnp.broadcast_to(kernel[t : t + 1, :] * scale, (8, CH))[None] for t in range(9)]


def tap_sum(src, row, col, width, dilate, sign, taps, which, start=None):
    total = start
    for i in which:
        for j in (-1, 0, 1):
            at = col + sign * j * dilate
            piece = src[row + sign * i * dilate, at : at + width, :].reshape(width // 8, 8, CH)
            piece = piece * taps[(i + 1) * 3 + j + 1]
            total = piece if total is None else total + piece
    return total


def chunks(low, high, size):
    out = []
    while low < high:
        out.append((low, min(size, high - low)))
        low += size
    return out


def clear_outside(ref, edges, rows_top, rows_bottom, col_left, col_right):
    count = ref.shape[0]
    breadth = ref.shape[1]

    @pl.when(edges[0] == 1)
    def _():
        ref[0:rows_top] = jnp.zeros((rows_top, breadth, CH), F32)

    @pl.when(edges[1] == 1)
    def _():
        ref[count - rows_bottom : count] = jnp.zeros((rows_bottom, breadth, CH), F32)

    @pl.when(edges[2] == 1)
    def _():
        ref[:, col_left : col_left + CHALO] = jnp.zeros((count, CHALO, CH), F32)

    @pl.when(edges[3] == 1)
    def _():
        ref[:, col_right : col_right + CHALO] = jnp.zeros((count, CHALO, CH), F32)


def grad_of(hidden, upstream):
    return lax.dot_general(
        hidden.reshape(-1, CH),
        upstream.reshape(-1, CH),
        (((0,), (0,)), ((), ())),
        preferred_element_type=F32,
    )


def forward_kernel(last, *refs):
    refs = list(refs)
    take = lambda n: [refs.pop(0) for _ in range(n)]
    edges, own, left, right, top, bottom, kernels, weights = take(8)
    if last:
        coarse, cot, back_weight = take(3)
        out, pre, pre_left, pre_right, grad = take(5)
        kept = take(3 + 3)
    else:
        x_out, x_left, x_right = take(3)
        kept = take(4 + 4)
    count = len(kept) // 2
    hid_out, slope_out = kept[:count], kept[count:]
    x_bufs = take(2)
    h_bufs = take(4)
    hid_two = take(1)[0]
    slopes = take(4)
    sem = take(1)[0]
    own_buf = take(1)[0]

    def build(r, _):
        x_bufs[0][RH + r, PAD : PAD + 16] = left[r].astype(F32)
        x_bufs[0][RH + r, PAD + 16 : PAD + 144] = own[r].astype(F32)
        x_bufs[0][RH + r, PAD + 144 : PAD + 160] = right[r].astype(F32)
        return 0

    lax.fori_loop(0, ROWS, build, 0)

    def build_ends(r, _):
        x_bufs[0][r, PAD : PAD + WIDE] = top[r].astype(F32)
        x_bufs[0][RH + ROWS + r, PAD : PAD + WIDE] = bottom[r].astype(F32)
        return 0

    lax.fori_loop(0, RH, build_ends, 0)

    copies = []
    for layer in range(4):
        dilate = 2**layer
        halo = HALO[layer]
        low, high = SPAN[layer]
        breadth = high - low
        dhalo = DHALO[layer]
        dlow, dhigh = DSPAN[layer]
        src, dst = x_bufs[layer % 2], x_bufs[(layer + 1) % 2]
        h_buf, slope_buf = h_bufs[layer], slopes[layer]
        taps = rows_of(kernels[layer], 0.5)

        def act_rows(r, number, want_slope, own_rows):
            for q in range(number):
                hid_parts, slope_parts = [], []
                for c, width in chunks(low, high, 32):
                    half = tap_sum(
                        src, RH + r + q, PAD + c, width, dilate, 1, taps, (-1, 0, 1)
                    )
                    hidden, slope = gelu_parts(half, want_slope)
                    hid_parts.append(hidden.reshape(width, CH))
                    if want_slope:
                        slope_parts.append(slope.reshape(width, CH))
                hidden = jnp.concatenate(hid_parts, 0)
                h_buf[halo + r + q] = hidden.astype(BF)
                if layer == 2 and own_rows:
                    hid_two[r + q] = hidden[8:136].astype(BF)
                if want_slope:
                    slope = jnp.concatenate(slope_parts, 0)
                    slope_buf[dhalo + r + q] = slope[dlow - low : dhigh - low].astype(BF)

        number = 4
        outer = halo - dhalo
        if outer:
            each = outer // number

            def outer_body(it, _):
                r = jnp.where(it < each, it * number - halo, ROWS + dhalo + (it - each) * number)
                act_rows(r, number, False, False)
                return 0

            lax.fori_loop(0, 2 * each, outer_body, 0)
        if layer == 2:

            def ring_body(it, _):
                r = jnp.where(it < 2, it * number - halo, ROWS + (it - 2) * number)
                act_rows(r, number, True, False)
                return 0

            lax.fori_loop(0, 4, ring_body, 0)
            first, rows_here = 0, ROWS
        else:
            first, rows_here = -dhalo, ROWS + 2 * dhalo

        def inner_body(it, _):
            act_rows(first + it * number, number, True, True)
            return 0

        lax.fori_loop(0, rows_here // number, inner_body, 0)

        if layer < count:
            if layer == 2:
                hid_src = hid_two
            else:
                hid_src = h_buf.at[pl.ds(halo, ROWS), pl.ds(16 - low, COLS)]
            copies.append(pltpu.make_async_copy(hid_src, hid_out[layer], sem.at[layer]))
            copies.append(pltpu.make_async_copy(slope_buf, slope_out[layer], sem.at[4 + layer]))
            copies[-1].start()
            copies[-2].start()

        step = BLOCK[layer]
        total = ROWS + 2 * halo

        def mix_body(it, _):
            at = it * step
            mixed = jnp.dot(
                h_buf[pl.ds(at, step)].reshape(step * breadth, CH),
                weights[layer],
                preferred_element_type=F32,
            ).reshape(step, breadth, CH)
            rows = pl.ds(RH - halo + at, step)
            value = src[rows, PAD + low : PAD + high] + mixed
            if layer < 3:
                dst[rows, PAD + low : PAD + high] = value
            elif last:
                for q in range(step // STRIDE):
                    extra = coarse[it * (step // STRIDE) + q][:, None, :]
                    part = value[q * STRIDE : (q + 1) * STRIDE].reshape(STRIDE, -1, STRIDE, CH)
                    part = (part + extra[None]).reshape(STRIDE, COLS, CH)
                    own_buf[pl.ds(at + q * STRIDE, STRIDE)] = part.astype(BF)
            else:
                value = value.astype(BF)
                own_buf[pl.ds(at, step)] = value
                x_left[pl.ds(at, step)] = value[:, :CHALO]
                x_right[pl.ds(at, step)] = value[:, COLS - CHALO :]
            return 0

        lax.fori_loop(0, total // step, mix_body, 0)
        if layer < 3:
            clear_outside(dst, edges, RH, RH, PAD, PAD + 16 + COLS)

    result = out if last else x_out
    copies.append(pltpu.make_async_copy(own_buf, result, sem.at[8]))
    copies[-1].start()
    if last:
        total = jnp.zeros((CH, CH), F32)
        for b in range(2):
            rows = slice(16 * b, 16 * b + 16)
            up = cot[rows]
            total = total + grad_of(h_bufs[3][rows], up)
            pulled = jnp.dot(up.reshape(-1, CH), back_weight[...], preferred_element_type=F32)
            value = pulled.reshape(16, COLS, CH) * slopes[3][rows].astype(F32)
            value = value.astype(BF)
            pre[rows] = value
            pre_left[rows] = value[:, :CHALO]
            pre_right[rows] = value[:, COLS - CHALO :]
        grad[...] = total
    for copy in copies:
        copy.wait()


def forward(last, edges, own, left, right, top, bottom, kernels, weights, extra=()):
    count = 3 if last else 4
    block = sds((ROWS, COLS, CH), BF)
    strip = sds((ROWS, CHALO, CH), BF)
    hid_shapes = [block] * count
    slope_shapes = [
        sds((ROWS + 2 * DHALO[k], DSPAN[k][1] - DSPAN[k][0], CH), BF) for k in range(4)
    ]
    if last:
        outs = [block, block, strip, strip, sds((CH, CH), F32)]
        specs = [ANY] + [VMEM] * 4
    else:
        outs = [block, strip, strip]
        specs = [ANY, VMEM, VMEM]
    outs = outs + hid_shapes + slope_shapes[:count]
    specs = specs + [ANY] * (2 * count)
    scratch = [pltpu.VMEM((ROWS + 2 * RH, WIDE + 2 * PAD, CH), F32)] * 2
    scratch += [
        pltpu.VMEM((ROWS + 2 * HALO[k], SPAN[k][1] - SPAN[k][0], CH), BF) for k in range(4)
    ]
    scratch += [pltpu.VMEM((ROWS, COLS, CH), BF)]
    scratch += [pltpu.VMEM(s.shape, BF) for s in slope_shapes]
    scratch += [pltpu.SemaphoreType.DMA((9,)), pltpu.VMEM((ROWS, COLS, CH), BF)]
    return pl.pallas_call(
        functools.partial(forward_kernel, last),
        out_shape=outs,
        in_specs=[SMEM] + [VMEM] * (7 + len(extra)),
        out_specs=specs,
        scratch_shapes=scratch,
        compiler_params=pltpu.CompilerParams(vmem_limit_bytes=52 * 2**20),
        cost_estimate=pl.CostEstimate(
            flops=4 * 2 * 8000 * CH * CH, bytes_accessed=12 * 2**20, transcendentals=0
        ),
        name="forward_last" if last else "forward_first",
    )(edges, own, left, right, top, bottom, kernels, weights, *extra)


def pool_kernel(feature, cot, weight, weight_t, coarse, back, grad):
    total = None
    for b in range(ROWS // STRIDE):
        rows = slice(STRIDE * b, STRIDE * (b + 1))

        def block_sum(ref):
            value = ref[STRIDE * b].astype(F32)
            for r in range(1, STRIDE):
                value = value + ref[STRIDE * b + r].astype(F32)
            return value.reshape(COLS // STRIDE, STRIDE, CH).sum(axis=1)

        pooled = (block_sum(feature) * (1.0 / (STRIDE * STRIDE))).astype(BF)
        block_cot = block_sum(cot).astype(BF)
        coarse[b] = jnp.dot(pooled, weight[...], preferred_element_type=F32)
        back[b] = jnp.dot(block_cot, weight_t[...], preferred_element_type=F32) * (
            1.0 / (STRIDE * STRIDE)
        )
        part = grad_of(pooled, block_cot)
        total = part if total is None else total + part
    grad[...] = total


def pool(feature, cot, weight):
    small = sds((ROWS // STRIDE, COLS // STRIDE, CH), F32)
    return pl.pallas_call(
        pool_kernel,
        out_shape=[small, small, sds((CH, CH), F32)],
        in_specs=[VMEM] * 4,
        out_specs=[VMEM] * 3,
        compiler_params=pltpu.CompilerParams(vmem_limit_bytes=16 * 2**20),
        cost_estimate=pl.CostEstimate(flops=10**8, bytes_accessed=2 * 2**20, transcendentals=0),
        name="pool",
    )(feature, cot, weight, weight.T)


BASE = 8


def ends_kernel(pre, pre_left, pre_right, base, base_left, base_right, kernel, up, down, buf):
    taps = rows_of(kernel, 1.0)

    def build(r, _):
        buf[r, 0:16] = pre_left[r].astype(F32)
        buf[r, 16:144] = pre[r].astype(F32)
        buf[r, 144:160] = pre_right[r].astype(F32)
        return 0

    lax.fori_loop(0, ROWS, build, 0)
    zeros = jnp.zeros((8, CH), F32)

    def one(r, which):
        parts = []
        for c, width in chunks(8, 152, 32):
            parts.append(tap_sum(buf, r, c, width, 8, -1, taps, which).reshape(width, CH))
        middle = jnp.concatenate(parts, 0)
        ends = jnp.concatenate(
            [
                base_left[r].astype(F32)[8:16],
                base[r].astype(F32),
                base_right[r].astype(F32)[0:8],
            ],
            0,
        )
        return jnp.concatenate([zeros, middle + ends, zeros], 0).astype(BF)

    def body(r, _):
        up[r] = one(r, (-1, 0))
        down[r] = one(ROWS - 7 + r, (0, 1))
        return 0

    lax.fori_loop(0, 7, body, 0)

    def body_pre(r, _):
        up[7 + r] = buf[r].astype(BF)
        down[7 + r] = buf[ROWS - 8 + r].astype(BF)
        return 0

    lax.fori_loop(0, 8, body_pre, 0)


def ends(pre, pre_left, pre_right, base, base_left, base_right, kernel):
    strip = sds((RH, WIDE, CH), BF)
    return pl.pallas_call(
        ends_kernel,
        out_shape=[strip, strip],
        in_specs=[VMEM] * 7,
        out_specs=[VMEM] * 2,
        scratch_shapes=[pltpu.VMEM((ROWS, WIDE, CH), F32)],
        compiler_params=pltpu.CompilerParams(vmem_limit_bytes=24 * 2**20),
        cost_estimate=pl.CostEstimate(flops=10**8, bytes_accessed=6 * 2**20, transcendentals=0),
        name="ends",
    )(pre, pre_left, pre_right, base, base_left, base_right, kernel)


UHALO = 7
UWIDE = COLS + 16


def backward_kernel(last, *refs):
    refs = list(refs)
    take = lambda n: [refs.pop(0) for _ in range(n)]
    edges, pre, pre_left, pre_right, base, base_left, base_right, top, bottom = take(9)
    kernels, weights_t = take(2)
    count = 3 if last else 4
    if last:
        back = take(1)[0]
    slope_in = take(count)
    hid_in = take(count)
    if last:
        out, grads = take(2)
    else:
        up_out, pre_out, strip_left, strip_right, grads = take(5)
    buf, ups = take(2)
    slopes = take(count)
    hids = take(count)
    sem = take(1)[0]

    copies = []
    for k in range(count):
        copies.append(
            (
                pltpu.make_async_copy(slope_in[k], slopes[k], sem.at[2 * k]),
                pltpu.make_async_copy(hid_in[k], hids[k], sem.at[2 * k + 1]),
            )
        )
        copies[-1][0].start()
        copies[-1][1].start()

    def build(r, _):
        buf[BASE + r, 0:16] = pre_left[r].astype(F32)
        buf[BASE + r, 16:144] = pre[r].astype(F32)
        buf[BASE + r, 144:160] = pre_right[r].astype(F32)
        ups[UHALO + r, 0:8] = base_left[r].astype(F32)[8:16]
        ups[UHALO + r, 8:136] = base[r].astype(F32)
        ups[UHALO + r, 136:144] = base_right[r].astype(F32)[0:8]
        return 0

    lax.fori_loop(0, ROWS, build, 0)

    def build_pre(r, _):
        buf[r] = top[7 + r].astype(F32)
        buf[BASE + ROWS + r] = bottom[7 + r].astype(F32)
        return 0

    lax.fori_loop(0, 8, build_pre, 0)

    def build_ups(r, _):
        ups[r] = top[r].astype(F32)[8:152]
        ups[UHALO + ROWS + r] = bottom[r].astype(F32)[8:152]
        return 0

    lax.fori_loop(0, 7, build_ups, 0)

    def add_taps(r, low, high, dilate, taps, which, extra=None):
        for c, width in chunks(low, high, 32):
            start = ups[UHALO + r, c - 8 : c - 8 + width].reshape(width // 8, 8, CH)
            total = tap_sum(buf, BASE + r, c, width, dilate, -1, taps, which, start)
            if extra is not None:
                total = total + extra[(c - low) // 8 : (c - low + width) // 8][:, None, :]
                out[r, c - low : c - low + width] = total.reshape(width, CH).astype(BF)
            else:
                ups[UHALO + r, c - 8 : c - 8 + width] = total.reshape(width, CH)

    taps = rows_of(kernels[3], 1.0)

    def first_body(it, _):
        for q in range(2):
            add_taps(2 * it + q, 8, 152, 8, taps, (-1, 0, 1))
        return 0

    lax.fori_loop(0, ROWS // 2, first_body, 0)

    def first_ends(r, _):
        add_taps(r - 7, 8, 152, 8, taps, (-1,))
        add_taps(ROWS + r, 8, 152, 8, taps, (1,))
        return 0

    lax.fori_loop(0, 7, first_ends, 0)

    for k, layer in enumerate((2, 1, 0)):
        dilate = 2**layer
        halo = (1, 3, 7)[layer]
        copies[k][0].wait()
        copies[k][1].wait()
        step = (ROWS + 2 * halo) // 2
        skip = DHALO[layer] - halo

        def pull_body(it, _):
            at = it * step
            up = ups[pl.ds(UHALO - halo + at, step)].astype(BF)
            pulled = jnp.dot(
                up.reshape(step * UWIDE, CH), weights_t[layer], preferred_element_type=F32
            ).reshape(step, UWIDE, CH)
            slope = slopes[k][pl.ds(skip + at, step)].astype(F32)
            buf[pl.ds(BASE - halo + at, step), 8:152] = pulled * slope
            return 0

        lax.fori_loop(0, 2, pull_body, 0)
        clear_outside(buf, edges, 8, 8, 0, 16 + COLS)
        total = jnp.zeros((CH, CH), F32)
        for b in range(2):
            up = ups[UHALO + 16 * b : UHALO + 16 * b + 16, 8:136].astype(BF)
            total = total + grad_of(hids[k][16 * b : 16 * b + 16], up)
        grads[k] = total

        taps = rows_of(kernels[layer], 1.0)
        reach = (0, 1, 3)[layer]
        low, high = ((16, 144), (8, 152), (8, 152))[layer]

        def tap_body(it, _):
            for q in range(2):
                r = 2 * it + q - reach
                if last and layer == 0:
                    add_taps(r, low, high, dilate, taps, (-1, 0, 1), back[r // STRIDE])
                else:
                    add_taps(r, low, high, dilate, taps, (-1, 0, 1))
            return 0

        if layer == 1:
            lax.fori_loop(0, (ROWS + 2) // 2, tap_body, 0)
        else:
            lax.fori_loop(0, (ROWS + 2 * reach) // 2, tap_body, 0)

    if not last:
        copies[3][0].wait()
        copies[3][1].wait()
        total = jnp.zeros((CH, CH), F32)
        for b in range(2):
            rows = slice(16 * b, 16 * b + 16)
            value = ups[UHALO + 16 * b : UHALO + 16 * b + 16, 8:136]
            up_out[rows] = value
            up = value.astype(BF)
            total = total + grad_of(hids[3][rows], up)
            pulled = jnp.dot(up.reshape(-1, CH), weights_t[3], preferred_element_type=F32)
            value = (pulled.reshape(16, COLS, CH) * slopes[3][rows].astype(F32)).astype(BF)
            pre_out[rows] = value
            strip_left[rows, 0:16] = value[:, :CHALO]
            strip_left[rows, 16:32] = up[:, :CHALO]
            strip_right[rows, 0:16] = value[:, COLS - CHALO :]
            strip_right[rows, 16:32] = up[:, COLS - CHALO :]
        grads[3] = total


def backward(last, edges, pre, sides, base, base_sides, ends_in, kernels, weights_t, slopes, hids, back=()):
    count = len(slopes)
    block = sds((ROWS, COLS, CH), BF)
    if last:
        outs = [block, sds((count, CH, CH), F32)]
    else:
        strip = sds((ROWS, 2 * CHALO, CH), BF)
        outs = [sds((ROWS, COLS, CH), F32), block, strip, strip, sds((count, CH, CH), F32)]
    scratch = [
        pltpu.VMEM((ROWS + 16, WIDE, CH), F32),
        pltpu.VMEM((ROWS + 2 * UHALO, UWIDE, CH), F32),
    ]
    scratch += [pltpu.VMEM(a.shape, BF) for a in slopes]
    scratch += [pltpu.VMEM(a.shape, BF) for a in hids]
    scratch += [pltpu.SemaphoreType.DMA((2 * count,))]
    args = (edges, pre, *sides, base, *base_sides, *ends_in, kernels, weights_t, *back)
    return pl.pallas_call(
        functools.partial(backward_kernel, last),
        out_shape=outs,
        in_specs=[SMEM] + [VMEM] * (len(args) - 1) + [ANY] * (2 * count),
        out_specs=[VMEM] * len(outs),
        scratch_shapes=scratch,
        compiler_params=pltpu.CompilerParams(vmem_limit_bytes=52 * 2**20),
        cost_estimate=pl.CostEstimate(
            flops=7 * 2 * 5000 * CH * CH, bytes_accessed=14 * 2**20, transcendentals=0
        ),
        name="backward_last" if last else "backward_first",
    )(*args, *slopes, *hids)


def exchange(to_before, to_after, axis):
    ends_at = lax.axis_size(axis) - 1
    forth = [(i, i + 1) for i in range(ends_at)]
    back = [(i + 1, i) for i in range(ends_at)]
    return lax.ppermute(to_after, axis, forth), lax.ppermute(to_before, axis, back)


def row_strips(own, left, right):
    wide = lambda s: jnp.concatenate([left[s], own[s], right[s]], axis=1)
    return wide(slice(0, RH)), wide(slice(ROWS - RH, ROWS))


def local(features_in, cotangent, depth_kernels, point_weights, coarse_weight):
    row, col = lax.axis_index("rows"), lax.axis_index("cols")
    row_end, col_end = lax.axis_size("rows") - 1, lax.axis_size("cols") - 1
    edges = jnp.stack([row == 0, row == row_end, col == 0, col == col_end]).astype(jnp.int32)
    kernels = depth_kernels.astype(F32)
    weights_t = jnp.swapaxes(point_weights, 1, 2)

    side = lambda s: jnp.concatenate([features_in[:, s], cotangent[:, s]], axis=1)
    from_left, from_right = exchange(
        side(slice(0, CHALO)), side(slice(COLS - CHALO, COLS)), "cols"
    )
    left, right = from_left[:, :CHALO], from_right[:, :CHALO]
    cot_left, cot_right = from_left[:, CHALO:], from_right[:, CHALO:]
    top, bottom = exchange(*row_strips(features_in, left, right), "rows")
    coarse, back, coarse_grad = pool(features_in, cotangent, coarse_weight)
    x_mid, x_left, x_right, *kept = forward(
        False, edges, features_in, left, right, top, bottom, kernels[:4], point_weights[:4]
    )
    hid_low, slope_low = kept[:4], kept[4:]
    left, right = exchange(x_left, x_right, "cols")
    top, bottom = exchange(*row_strips(x_mid, left, right), "rows")
    output, pre, pre_left, pre_right, grad_top, *kept = forward(
        True, edges, x_mid, left, right, top, bottom, kernels[4:], point_weights[4:],
        (coarse, cotangent, weights_t[7]),
    )
    hid_high, slope_high = kept[:3], kept[3:]

    sides = exchange(pre_left, pre_right, "cols")
    base_sides = (cot_left, cot_right)
    rows_in = exchange(*ends(pre, *sides, cotangent, *base_sides, kernels[7]), "rows")
    order = lambda things: [things[2], things[1], things[0]]
    upstream, pre, strip_left, strip_right, grad_mid = backward(
        False, edges, pre, sides, cotangent, base_sides, rows_in,
        kernels[4:], jnp.concatenate([weights_t[4:7], weights_t[3:4]]),
        order(slope_high) + [slope_low[3]], order(hid_high) + [hid_low[3]],
    )
    got_left, got_right = exchange(strip_left, strip_right, "cols")
    sides = (got_left[:, :CHALO], got_right[:, :CHALO])
    base_sides = (got_left[:, CHALO:], got_right[:, CHALO:])
    rows_in = exchange(*ends(pre, *sides, upstream, *base_sides, kernels[3]), "rows")
    input_grad, grad_low = backward(
        True, edges, pre, sides, upstream, base_sides, rows_in,
        kernels[:4], weights_t[:3], order(slope_low), order(hid_low), (back,),
    )

    grads = [grad_low[2], grad_low[1], grad_low[0], grad_mid[3], grad_mid[2], grad_mid[1]]
    grads = jnp.stack(grads + [grad_mid[0], grad_top, coarse_grad], axis=1).astype(BF)
    shares = lax.all_to_all(grads, ("rows", "cols"), 0, 0, tiled=True)
    summed = shares.astype(F32).sum(axis=0)
    weight_grads = lax.all_gather(summed[:, None, :], "cols", axis=1, tiled=True)
    return (output, input_grad, weight_grads)


def solution(mesh):
    in_specs = (P("rows", "cols", None), P("rows", "cols", None), P(), P(), P())
    out_specs = (P("rows", "cols", None), P("rows", "cols", None), P(None, "rows", None))
    return jax.shard_map(local, mesh=mesh, in_specs=in_specs, out_specs=out_specs, check_vma=False)
```

time: 740 us -> 239 us (0.32); the launches traced: 730 us -> 238 us
  waiting for transfers between devices: 408 us -> 66.7 us
  starting transfers between devices: 177 us -> 42.6 us
  Pallas kernels: 0 us -> 80.3 us
  other arithmetic: 58.5 us -> 2.16 us
  matrix products: 32.4 us -> 0 us
  between operations: 17.4 us -> 1.19 us
  blocking collectives: 22.4 us -> 33 us
    unnamed x2 -> x0, waiting for transfers between devices: 266 us -> none
    ppermute x64 -> x16, starting transfers between devices: 177 us -> 42.6 us  [the longest x8 28.2 us: exchange(): lax.ppermute(to_after, axis, forth)]
    pallas_call x0 -> x7, Pallas kernels: none -> 80.3 us  [the longest x2 46.9 us: forward(): pl.pallas_call(functools.partial(forward_kernel, last), out_shape=outs, i...]
    ppermute x64 -> x16, waiting for transfers between devices: 142 us -> 66.7 us  [the longest x8 38.3 us: exchange(): lax.ppermute(to_before, axis, back)]
    add x15 -> x0, other arithmetic: 37.3 us -> none  [the longest x8 23 us: taps(): total + kernel[index].astype(jnp.float32) * piece.astype(jnp.float32)]
    dot_general x27 -> x0, matrix products: 32.4 us -> none  [the longest x8 14.7 us: local(): jnp.dot(up_b, point_weights[layer].T, preferred_element_type=jnp.float32)]
    all_to_all x0 -> x1, blocking collectives: none -> 25.5 us  [local(): shares = lax.all_to_all(grads, ('rows', 'cols'), 0, 0, tiled=True)]
    psum x1 -> x0, blocking collectives: 22.4 us -> none  [local(): summed = lax.psum(partial_grads.astype(jnp.bfloat16), 'cols')]
  transfers between devices with their start and end apart: 65 -> 16, of which waited for: 41 -> 14; matrix products, arithmetic and copies ran while one was open for 2% -> 3% of each run, Pallas kernels for 0% -> 0%
where the time goes in v1:
time: 239 us; the launch traced here: 238 us
  Pallas kernels  80.3 us (34%)
  waiting for transfers between devices  66.7 us (28%)
  starting transfers between devices  42.6 us (18%)
  blocking collectives  33 us (14%)
  local copies, waits for them, and re-layouts  12.1 us (5%)
    pallas_call x2, Pallas kernels, forward(): pl.pallas_call(functools.partial(forward_kernel, last), out_shape=outs, i...  46.9 us
    ppermute x8, waiting for transfers between devices, exchange(): lax.ppermute(to_before, axis, back)  38.3 us
    pallas_call x2, Pallas kernels, backward(): pl.pallas_call(functools.partial(backward_kernel, last), out_shape=outs,...  31.1 us
    ppermute x8, waiting for transfers between devices, exchange(): lax.ppermute(to_after, axis, forth)  28.4 us
    ppermute x8, starting transfers between devices, exchange(): lax.ppermute(to_after, axis, forth)  28.2 us
    all_to_all x1, blocking collectives, local(): shares = lax.all_to_all(grads, ('rows', 'cols'), 0, 0, tiled=True)  25.5 us
    ppermute x8, starting transfers between devices, exchange(): lax.ppermute(to_before, axis, back)  14.4 us
    all_gather x1, blocking collectives, local(): lax.all_gather(summed[:, None, :], 'cols', axis=1, tiled=True)  7.52 us
  transfers between devices with their start and end apart: 16, of which 14 were waited for; matrix products, arithmetic and copies ran while one was open for 3% of the time, Pallas kernels for 0%

profile of v1, /device:TPU:1, one launch (start us, length us, event | category | flops | bytes accessed | tf_op | source)
XLA Modules:
  0.0 238.1 jit_solution(12512539705453312933)
XLA Ops:
  1.9 6.0 %collective-permute-start = (bf16[32,32,128]{2,1,0:T(8,128)(2,1)S(1)}, bf16[32,32,128]{2,1,0:T(8,128)(2,1)S(1)}, u32[]{:S(2)}, u32[]{:S(2)}) collective-permute-start(bf16[32,32,128]{2,1,0:T(8,128)(2,1)S(1)} %pad_maximum_fusion.4), channel_id=1, source_target_pairs={{0,1},{1,2},{2,3},{4,5},{5,6},{6,7},{8,9},{9,10},{10,11},{12,13},{... | collective-permute-start | bytes 786440 | tf_op jit(solution)/shard_map/ppermute | solution.py:570
  11.3 6.1 %collective-permute-done.1 = bf16[32,32,128]{2,1,0:T(8,128)(2,1)S(1)} collective-permute-done((bf16[32,32,128]{2,1,0:T(8,128)(2,1)S(1)}, bf16[32,32,128]{2,1,0:T(8,128)(2,1)S(1)}, u32[]{:S(2)}, u32[]{:S(2)}) %collective-permute-start.1) | collective-permute-done | bytes 262176 | tf_op jit(solution)/shard_map/ppermute | solution.py:570
  17.4 3.6 %collective-permute-start.2 = (bf16[15,160,128]{2,1,0:T(8,128)(2,1)S(1)}, bf16[15,160,128]{2,1,0:T(8,128)(2,1)S(1)}, u32[]{:S(2)}, u32[]{:S(2)}) collective-permute-start(bf16[15,160,128]{2,1,0:T(8,128)(2,1)S(1)} %pad_maximum_fusion), channel_id=1, source_target_pairs={{0,4},{4,8},{8,12},{12,16},{16,20},{20,24},{24,28},{28,32},{32,36}... | collective-permute-start | bytes 1843208 | tf_op jit(solution)/shard_map/ppermute | solution.py:570
  23.5 5.8 %collective-permute-done.2.refs_4_ = bf16[15,160,128]{2,1,0:T(8,128)(2,1)S(1)} collective-permute-done((bf16[15,160,128]{2,1,0:T(8,128)(2,1)S(1)}, bf16[15,160,128]{2,1,0:T(8,128)(2,1)S(1)}, u32[]{:S(2)}, u32[]{:S(2)}) %collective-permute-start.2) | collective-permute-done | bytes 614432 | tf_op jit(solution)/shard_map/ppermute | solution.py:570
  29.3 4.2 %collective-permute-done.3.refs_5_ = bf16[15,160,128]{2,1,0:T(8,128)(2,1)S(1)} collective-permute-done((bf16[15,160,128]{2,1,0:T(8,128)(2,1)S(1)}, bf16[15,160,128]{2,1,0:T(8,128)(2,1)S(1)}, u32[]{:S(2)}, u32[]{:S(2)}) %collective-permute-start.3) | collective-permute-done | bytes 614432 | tf_op jit(solution)/shard_map/ppermute | solution.py:570
  33.5 22.6 %forward_first.1 = (bf16[32,128,128]{2,1,0:T(8,128)(2,1)}, bf16[32,16,128]{2,1,0:T(8,128)(2,1)S(1)}, bf16[32,16,128]{2,1,0:T(8,128)(2,1)S(1)}, bf16[32,128,128]{...) custom-call(s32[4]{0:T(128)S(1)} %add_convert_fusion.refs_0_, ...), custom_call_target="tpu_custom_call" | custom-call | flops 1048576000 | bytes 12582912 | tf_op jit(solution)/shard_map/forward_first/pallas_call | solution.py:279
  61.7 4.1 %collective-permute-done.5.refs_3_ = bf16[32,16,128]{2,1,0:T(8,128)(2,1)S(1)} collective-permute-done((bf16[32,16,128]{2,1,0:T(8,128)(2,1)S(1)}, bf16[32,16,128]{2,1,0:T(8,128)(2,1)S(1)}, u32[]{:S(2)}, u32[]{:S(2)}) %collective-permute-start.5) | collective-permute-done | bytes 131104 | tf_op jit(solution)/shard_map/ppermute | solution.py:570
  66.7 5.4 %collective-permute-start.6 = (bf16[15,160,128]{2,1,0:T(8,128)(2,1)}, bf16[15,160,128]{2,1,0:T(8,128)(2,1)S(1)}, u32[]{:S(2)}, u32[]{:S(2)}) collective-permute-start(bf16[15,160,128]{2,1,0:T(8,128)(2,1)} %pad_maximum_fusion.2), channel_id=1, source_target_pairs={{0,4},{4,8},{8,12},{12,16},{16,20},{20,24},{24,28},{28,32},{32,36}... | collective-permute-start | bytes 1843208 | tf_op jit(solution)/shard_map/ppermute | solution.py:570
  77.2 4.8 %collective-permute-done.6.refs_4_ = bf16[15,160,128]{2,1,0:T(8,128)(2,1)S(1)} collective-permute-done((bf16[15,160,128]{2,1,0:T(8,128)(2,1)}, bf16[15,160,128]{2,1,0:T(8,128)(2,1)S(1)}, u32[]{:S(2)}, u32[]{:S(2)}) %collective-permute-start.6) | collective-permute-done | bytes 614432 | tf_op jit(solution)/shard_map/ppermute | solution.py:570
  82.0 5.0 %collective-permute-done.7.refs_5_ = bf16[15,160,128]{2,1,0:T(8,128)(2,1)} collective-permute-done((bf16[15,160,128]{2,1,0:T(8,128)(2,1)}, bf16[15,160,128]{2,1,0:T(8,128)(2,1)}, u32[]{:S(2)}, u32[]{:S(2)}) %collective-permute-start.7) | collective-permute-done | bytes 614432 | tf_op jit(solution)/shard_map/ppermute | solution.py:570
  87.0 24.3 %forward_last.1 = (bf16[32,128,128]{2,1,0:T(8,128)(2,1)}, bf16[32,128,128]{2,1,0:T(8,128)(2,1)}, bf16[32,16,128]{2,1,0:T(8,128)(2,1)S(1)}, bf16[32,16,128]{2,1,0...) custom-call(s32[4]{0:T(128)S(1)} %add_convert_fusion.refs_0_, ...), custom_call_target="tpu_custom_call" | custom-call | flops 1048576000 | bytes 12582912 | tf_op jit(solution)/shard_map/forward_last/pallas_call | solution.py:279
  116.4 4.8 %collective-permute-done.9.pre_right.refs_3_ = bf16[32,16,128]{2,1,0:T(8,128)(2,1)S(1)} collective-permute-done((bf16[32,16,128]{2,1,0:T(8,128)(2,1)S(1)}, bf16[32,16,128]{2,1,0:T(8,128)(2,1)S(1)}, u32[]{:S(2)}, u32[]{:S(2)}) %collective-permute-start.9) | collective-permute-done | bytes 131104 | tf_op jit(solution)/shard_map/ppermute | solution.py:570
  123.3 3.5 %collective-permute-start.10 = (bf16[15,160,128]{2,1,0:T(8,128)(2,1)S(1)}, bf16[15,160,128]{2,1,0:T(8,128)(2,1)S(1)}, u32[]{:S(2)}, u32[]{:S(2)}) collective-permute-start(bf16[15,160,128]{2,1,0:T(8,128)(2,1)S(1)} %get-tuple-element.47), channel_id=1, source_target_pairs={{0,4},{4,8},{8,12},{12,16},{16,20},{20,24},{24,28},{28,32},{32,36}... | collective-permute-start | bytes 1843208 | tf_op jit(solution)/shard_map/ppermute | solution.py:570
  128.4 8.3 %collective-permute-done.10.refs_7_ = bf16[15,160,128]{2,1,0:T(8,128)(2,1)S(1)} collective-permute-done((bf16[15,160,128]{2,1,0:T(8,128)(2,1)S(1)}, bf16[15,160,128]{2,1,0:T(8,128)(2,1)S(1)}, u32[]{:S(2)}, u32[]{:S(2)}) %collective-permute-start.10) | collective-permute-done | bytes 614432 | tf_op jit(solution)/shard_map/ppermute | solution.py:570
  136.7 4.1 %collective-permute-done.11.refs_8_ = bf16[15,160,128]{2,1,0:T(8,128)(2,1)S(1)} collective-permute-done((bf16[15,160,128]{2,1,0:T(8,128)(2,1)S(1)}, bf16[15,160,128]{2,1,0:T(8,128)(2,1)S(1)}, u32[]{:S(2)}, u32[]{:S(2)}) %collective-permute-start.11) | collective-permute-done | bytes 614432 | tf_op jit(solution)/shard_map/ppermute | solution.py:570
  141.6 15.8 %backward_first.1 = (f32[32,128,128]{2,1,0:T(8,128)}, bf16[32,128,128]{2,1,0:T(8,128)(2,1)}, bf16[32,32,128]{2,1,0:T(8,128)(2,1)S(1)}, bf16[32,32,128]{2,1,0:T(8,128)(2,1)S(1)}, f32[4,128,128]{2,1,0:T(8,128)S(1)}) custom-call(s32[4]{0:T(128)S(1)} %add_convert_fusion.refs_0_, bf16[32,128,128]{2,1,0:T(8,128)(2,1)} %get-tuple-element.44.pre.refs_1_, ...), custom_call_target="tpu_custom_call" | custom-call | flops 1146880000 | bytes 14680064 | tf_op jit(solution)/shard_map/backward_first/pallas_call | solution.py:552
  159.6 2.4 %collective-permute-start.13 = (bf16[32,32,128]{2,1,0:T(8,128)(2,1)S(1)}, bf16[32,32,128]{2,1,0:T(8,128)(2,1)S(1)}, u32[]{:S(2)}, u32[]{:S(2)}) collective-permute-start(bf16[32,32,128]{2,1,0:T(8,128)(2,1)S(1)} %get-tuple-element.59), channel_id=1, source_target_pairs={{1,0},{2,1},{3,2},{5,4},{6,5},{7,6},{9,8},{10,9},{11,10},{13,12},{... | collective-permute-start | bytes 786440 | tf_op jit(solution)/shard_map/ppermute | solution.py:570
  162.9 5.9 %collective-permute-done.13 = bf16[32,32,128]{2,1,0:T(8,128)(2,1)S(1)} collective-permute-done((bf16[32,32,128]{2,1,0:T(8,128)(2,1)S(1)}, bf16[32,32,128]{2,1,0:T(8,128)(2,1)S(1)}, u32[]{:S(2)}, u32[]{:S(2)}) %collective-permute-start.13) | collective-permute-done | bytes 262176 | tf_op jit(solution)/shard_map/ppermute | solution.py:570
  171.2 3.6 %collective-permute-start.14 = (bf16[15,160,128]{2,1,0:T(8,128)(2,1)S(1)}, bf16[15,160,128]{2,1,0:T(8,128)(2,1)S(1)}, u32[]{:S(2)}, u32[]{:S(2)}) collective-permute-start(bf16[15,160,128]{2,1,0:T(8,128)(2,1)S(1)} %get-tuple-element.61), channel_id=1, source_target_pairs={{0,4},{4,8},{8,12},{12,16},{16,20},{20,24},{24,28},{28,32},{32,36}... | collective-permute-start | bytes 1843208 | tf_op jit(solution)/shard_map/ppermute | solution.py:570
  176.2 7.5 %collective-permute-done.14.refs_7_ = bf16[15,160,128]{2,1,0:T(8,128)(2,1)S(1)} collective-permute-done((bf16[15,160,128]{2,1,0:T(8,128)(2,1)S(1)}, bf16[15,160,128]{2,1,0:T(8,128)(2,1)S(1)}, u32[]{:S(2)}, u32[]{:S(2)}) %collective-permute-start.14) | collective-permute-done | bytes 614432 | tf_op jit(solution)/shard_map/ppermute | solution.py:570
  183.7 4.1 %collective-permute-done.15.refs_8_ = bf16[15,160,128]{2,1,0:T(8,128)(2,1)S(1)} collective-permute-done((bf16[15,160,128]{2,1,0:T(8,128)(2,1)S(1)}, bf16[15,160,128]{2,1,0:T(8,128)(2,1)S(1)}, u32[]{:S(2)}, u32[]{:S(2)}) %collective-permute-start.15) | collective-permute-done | bytes 614432 | tf_op jit(solution)/shard_map/ppermute | solution.py:570
  188.6 15.3 %backward_last.1 = (bf16[32,128,128]{2,1,0:T(8,128)(2,1)}, f32[3,128,128]{2,1,0:T(8,128)S(1)}) custom-call(s32[4]{0:T(128)S(1)} %add_convert_fusion.refs_0_, bf16[32,128,128]{2,1,0:T(8,128)(2,1)} %get-tuple-element.57.pre.refs_1_, bf16[32,16,128]{2,1,0:T(8,128)(2,1)S(1)} %get-tuple-element.88.pre_left.refs_2_, ...), custom_call_target="tpu_custom_call" | custom-call | flops 1146880000 | bytes 14680064 | tf_op jit(solution)/shard_map/backward_last/pallas_call | solution.py:552
  204.3 25.5 %all_to_all.5 = bf16[128,9,128]{2,1,0:T(8,128)(2,1)S(1)} all-to-all(bf16[128,9,128]{2,1,0:T(8,128)(2,1)S(1)} %copy.14), channel_id=1, replica_groups=mesh['rows'=32,'cols'=4] {'rows','cols'}, dimensions={0} | all-to-all | bytes 589824 | tf_op jit(solution)/shard_map/all_to_all | solution.py:625
  230.0 7.5 %all-gather = f32[9,512]{1,0:T(8,128)S(1)} all-gather(f32[9,128]{1,0:T(8,128)S(1)} %convert_reduce_fusion), channel_id=2, replica_groups=mesh['rows'=32,'cols'=4] {'cols'}, dimensions={1}, use_global_device_ids=true | all-gather | bytes 23040 | tf_op jit(solution)/shard_map/all_gather | solution.py:627
  (90 shorter events, 36.5 us)
Async XLA Ops:
  0.6 9.4 %copy-start.3 = (bf16[32,128,128]{2,1,0:T(8,128)(2,1)S(1)}, bf16[32,128,128]{2,1,0:T(8,128)(2,1)}, u32[]{:S(2)}) copy-start(bf16[32,128,128]{2,1,0:T(8,128)(2,1)} %feature.1) | copy-start | bytes 3145732
  1.9 9.3 %collective-permute-start = (bf16[32,32,128]{2,1,0:T(8,128)(2,1)S(1)}, bf16[32,32,128]{2,1,0:T(8,128)(2,1)S(1)}, u32[]{:S(2)}, u32[]{:S(2)}) collective-permute-start(bf16[32,32,128]{2,1,0:T(8,128)(2,1)S(1)} %pad_maximum_fusion.4), channel_id=1, source_target_pairs={{0,1},{1,2},{2,3},{4,5},{5,6},{6,7},{8,9},{9,10},{10,11},{12,13},{... | collective-permute-start | bytes 786440 | tf_op jit(solution)/shard_map/ppermute | solution.py:570
  8.0 9.3 %collective-permute-start.1 = (bf16[32,32,128]{2,1,0:T(8,128)(2,1)S(1)}, bf16[32,32,128]{2,1,0:T(8,128)(2,1)S(1)}, u32[]{:S(2)}, u32[]{:S(2)}) collective-permute-start(bf16[32,32,128]{2,1,0:T(8,128)(2,1)S(1)} %pad_maximum_fusion.5), channel_id=1, source_target_pairs={{1,0},{2,1},{3,2},{5,4},{6,5},{7,6},{9,8},{10,9},{11,10},{13,12},{... | collective-permute-start | bytes 786440 | tf_op jit(solution)/shard_map/ppermute | solution.py:570
  10.2 12.1 %copy-start.14 = (f32[8,9,128]{2,1,0:T(8,128)}, f32[8,9,128]{2,1,0:T(8,128)S(1)}, u32[]{:S(2)}) copy-start(f32[8,9,128]{2,1,0:T(8,128)S(1)} %copy_convert_fusion) | copy-start | bytes 110596
  17.3 5.0 %copy-start.13 = (bf16[32,32,128]{2,1,0:T(8,128)(2,1)}, bf16[32,32,128]{2,1,0:T(8,128)(2,1)S(1)}, u32[]{:S(2)}) copy-start(bf16[32,32,128]{2,1,0:T(8,128)(2,1)S(1)} %collective-permute-done.1) | copy-start | bytes 786436
  17.4 11.9 %collective-permute-start.2 = (bf16[15,160,128]{2,1,0:T(8,128)(2,1)S(1)}, bf16[15,160,128]{2,1,0:T(8,128)(2,1)S(1)}, u32[]{:S(2)}, u32[]{:S(2)}) collective-permute-start(bf16[15,160,128]{2,1,0:T(8,128)(2,1)S(1)} %pad_maximum_fusion), channel_id=1, source_target_pairs={{0,4},{4,8},{8,12},{12,16},{16,20},{20,24},{24,28},{28,32},{32,36}... | collective-permute-start | bytes 1843208 | tf_op jit(solution)/shard_map/ppermute | solution.py:570
  21.0 12.5 %collective-permute-start.3 = (bf16[15,160,128]{2,1,0:T(8,128)(2,1)S(1)}, bf16[15,160,128]{2,1,0:T(8,128)(2,1)S(1)}, u32[]{:S(2)}, u32[]{:S(2)}) collective-permute-start(bf16[15,160,128]{2,1,0:T(8,128)(2,1)S(1)} %pad_maximum_fusion.1), channel_id=1, source_target_pairs={{4,0},{8,4},{12,8},{16,12},{20,16},{24,20},{28,24},{32,28},{36,32}... | collective-permute-start | bytes 1843208 | tf_op jit(solution)/shard_map/ppermute | solution.py:570
  56.1 5.6 %collective-permute-start.4 = (bf16[32,16,128]{2,1,0:T(8,128)(2,1)S(1)}, bf16[32,16,128]{2,1,0:T(8,128)(2,1)S(1)}, u32[]{:S(2)}, u32[]{:S(2)}) collective-permute-start(bf16[32,16,128]{2,1,0:T(8,128)(2,1)S(1)} %get-tuple-element.40), channel_id=1, source_target_pairs={{0,1},{1,2},{2,3},{4,5},{5,6},{6,7},{8,9},{9,10},{10,11},{12,13},{... | collective-permute-start | bytes 393224 | tf_op jit(solution)/shard_map/ppermute | solution.py:570
  58.0 7.8 %collective-permute-start.5 = (bf16[32,16,128]{2,1,0:T(8,128)(2,1)S(1)}, bf16[32,16,128]{2,1,0:T(8,128)(2,1)S(1)}, u32[]{:S(2)}, u32[]{:S(2)}) collective-permute-start(bf16[32,16,128]{2,1,0:T(8,128)(2,1)S(1)} %get-tuple-element.41), channel_id=1, source_target_pairs={{1,0},{2,1},{3,2},{5,4},{6,5},{7,6},{9,8},{10,9},{11,10},{13,12},{... | collective-permute-start | bytes 393224 | tf_op jit(solution)/shard_map/ppermute | solution.py:570
  65.8 10.2 %copy-start.7 = (bf16[128,128]{1,0:T(8,128)(2,1)S(1)}, bf16[128,128]{1,0:T(8,128)(2,1)}, u32[]{:S(2)}) copy-start(bf16[128,128]{1,0:T(8,128)(2,1)} %weight.1) | copy-start | bytes 98308
  65.8 10.4 %copy-start = (bf16[32,128,128]{2,1,0:T(8,128)(2,1)S(1)}, bf16[32,128,128]{2,1,0:T(8,128)(2,1)}, u32[]{:S(2)}) copy-start(bf16[32,128,128]{2,1,0:T(8,128)(2,1)} %refs_4_.1) | copy-start | bytes 3145732
  65.8 10.4 %copy-start.4 = (bf16[32,128,128]{2,1,0:T(8,128)(2,1)S(1)}, bf16[32,128,128]{2,1,0:T(8,128)(2,1)}, u32[]{:S(2)}) copy-start(bf16[32,128,128]{2,1,0:T(8,128)(2,1)} %feature.1) | copy-start | bytes 3145732
  66.7 15.2 %collective-permute-start.6 = (bf16[15,160,128]{2,1,0:T(8,128)(2,1)}, bf16[15,160,128]{2,1,0:T(8,128)(2,1)S(1)}, u32[]{:S(2)}, u32[]{:S(2)}) collective-permute-start(bf16[15,160,128]{2,1,0:T(8,128)(2,1)} %pad_maximum_fusion.2), channel_id=1, source_target_pairs={{0,4},{4,8},{8,12},{12,16},{16,20},{20,24},{24,28},{28,32},{32,36}... | collective-permute-start | bytes 1843208 | tf_op jit(solution)/shard_map/ppermute | solution.py:570
  73.0 14.0 %collective-permute-start.7 = (bf16[15,160,128]{2,1,0:T(8,128)(2,1)}, bf16[15,160,128]{2,1,0:T(8,128)(2,1)}, u32[]{:S(2)}, u32[]{:S(2)}) collective-permute-start(bf16[15,160,128]{2,1,0:T(8,128)(2,1)} %pad_maximum_fusion.3), channel_id=1, source_target_pairs={{4,0},{8,4},{12,8},{16,12},{20,16},{24,20},{28,24},{32,28},{36,32}... | collective-permute-start | bytes 1843208 | tf_op jit(solution)/shard_map/ppermute | solution.py:570
  87.0 34.2 %copy-start.1 = (bf16[32,128,128]{2,1,0:T(8,128)(2,1)S(1)}, bf16[32,128,128]{2,1,0:T(8,128)(2,1)}, u32[]{:S(2)}) copy-start(bf16[32,128,128]{2,1,0:T(8,128)(2,1)} %refs_4_.1) | copy-start | bytes 3145732
  111.3 5.1 %collective-permute-start.8 = (bf16[32,16,128]{2,1,0:T(8,128)(2,1)S(1)}, bf16[32,16,128]{2,1,0:T(8,128)(2,1)S(1)}, u32[]{:S(2)}, u32[]{:S(2)}) collective-permute-start(bf16[32,16,128]{2,1,0:T(8,128)(2,1)S(1)} %get-tuple-element.45), channel_id=1, source_target_pairs={{0,1},{1,2},{2,3},{4,5},{5,6},{6,7},{8,9},{9,10},{10,11},{12,13},{... | collective-permute-start | bytes 393224 | tf_op jit(solution)/shard_map/ppermute | solution.py:570
  113.4 7.8 %collective-permute-start.9 = (bf16[32,16,128]{2,1,0:T(8,128)(2,1)S(1)}, bf16[32,16,128]{2,1,0:T(8,128)(2,1)S(1)}, u32[]{:S(2)}, u32[]{:S(2)}) collective-permute-start(bf16[32,16,128]{2,1,0:T(8,128)(2,1)S(1)} %get-tuple-element.46), channel_id=1, source_target_pairs={{1,0},{2,1},{3,2},{5,4},{6,5},{7,6},{9,8},{10,9},{11,10},{13,12},{... | collective-permute-start | bytes 393224 | tf_op jit(solution)/shard_map/ppermute | solution.py:570
  123.3 13.4 %collective-permute-start.10 = (bf16[15,160,128]{2,1,0:T(8,128)(2,1)S(1)}, bf16[15,160,128]{2,1,0:T(8,128)(2,1)S(1)}, u32[]{:S(2)}, u32[]{:S(2)}) collective-permute-start(bf16[15,160,128]{2,1,0:T(8,128)(2,1)S(1)} %get-tuple-element.47), channel_id=1, source_target_pairs={{0,4},{4,8},{8,12},{12,16},{16,20},{20,24},{24,28},{28,32},{32,36}... | collective-permute-start | bytes 1843208 | tf_op jit(solution)/shard_map/ppermute | solution.py:570
  126.8 14.0 %collective-permute-start.11 = (bf16[15,160,128]{2,1,0:T(8,128)(2,1)S(1)}, bf16[15,160,128]{2,1,0:T(8,128)(2,1)S(1)}, u32[]{:S(2)}, u32[]{:S(2)}) collective-permute-start(bf16[15,160,128]{2,1,0:T(8,128)(2,1)S(1)} %get-tuple-element.48), channel_id=1, source_target_pairs={{4,0},{8,4},{12,8},{16,12},{20,16},{24,20},{28,24},{32,28},{36,32}... | collective-permute-start | bytes 1843208 | tf_op jit(solution)/shard_map/ppermute | solution.py:570
  157.5 11.3 %copy-start.5 = (bf16[32,128,128]{2,1,0:T(8,128)(2,1)S(1)}, bf16[32,128,128]{2,1,0:T(8,128)(2,1)}, u32[]{:S(2)}) copy-start(bf16[32,128,128]{2,1,0:T(8,128)(2,1)} %get-tuple-element.57.pre.refs_1_) | copy-start | bytes 3145732
  157.5 5.4 %collective-permute-start.12 = (bf16[32,32,128]{2,1,0:T(8,128)(2,1)S(1)}, bf16[32,32,128]{2,1,0:T(8,128)(2,1)S(1)}, u32[]{:S(2)}, u32[]{:S(2)}) collective-permute-start(bf16[32,32,128]{2,1,0:T(8,128)(2,1)S(1)} %get-tuple-element.58), channel_id=1, source_target_pairs={{0,1},{1,2},{2,3},{4,5},{5,6},{6,7},{8,9},{9,10},{10,11},{12,13},{... | collective-permute-start | bytes 786440 | tf_op jit(solution)/shard_map/ppermute | solution.py:570
  159.6 9.2 %collective-permute-start.13 = (bf16[32,32,128]{2,1,0:T(8,128)(2,1)S(1)}, bf16[32,32,128]{2,1,0:T(8,128)(2,1)S(1)}, u32[]{:S(2)}, u32[]{:S(2)}) collective-permute-start(bf16[32,32,128]{2,1,0:T(8,128)(2,1)S(1)} %get-tuple-element.59), channel_id=1, source_target_pairs={{1,0},{2,1},{3,2},{5,4},{6,5},{7,6},{9,8},{10,9},{11,10},{13,12},{... | collective-permute-start | bytes 786440 | tf_op jit(solution)/shard_map/ppermute | solution.py:570
  171.2 12.4 %collective-permute-start.14 = (bf16[15,160,128]{2,1,0:T(8,128)(2,1)S(1)}, bf16[15,160,128]{2,1,0:T(8,128)(2,1)S(1)}, u32[]{:S(2)}, u32[]{:S(2)}) collective-permute-start(bf16[15,160,128]{2,1,0:T(8,128)(2,1)S(1)} %get-tuple-element.61), channel_id=1, source_target_pairs={{0,4},{4,8},{8,12},{12,16},{16,20},{20,24},{24,28},{28,32},{32,36}... | collective-permute-start | bytes 1843208 | tf_op jit(solution)/shard_map/ppermute | solution.py:570
  174.8 13.0 %collective-permute-start.15 = (bf16[15,160,128]{2,1,0:T(8,128)(2,1)S(1)}, bf16[15,160,128]{2,1,0:T(8,128)(2,1)S(1)}, u32[]{:S(2)}, u32[]{:S(2)}) collective-permute-start(bf16[15,160,128]{2,1,0:T(8,128)(2,1)S(1)} %get-tuple-element.62), channel_id=1, source_target_pairs={{4,0},{8,4},{12,8},{16,12},{20,16},{24,20},{28,24},{32,28},{36,32}... | collective-permute-start | bytes 1843208 | tf_op jit(solution)/shard_map/ppermute | solution.py:570
  (8 other events, 14.0 us)

commit v2 on v1

--- a/solution.py
+++ b/solution.py
@@ -20,9 +20,8 @@
 
 HALO = (14, 12, 8, 0)
 SPAN = ((0, 160), (0, 160), (8, 152), (16, 144))
-DHALO = (2, 4, 8, 0)
+DHALO = (2, 3, 8, 0)
 DSPAN = ((8, 152), (8, 152), (8, 152), (16, 144))
-BLOCK = (15, 14, 16, 16)
 
 VMEM = pl.BlockSpec(memory_space=pltpu.VMEM)
 SMEM = pl.BlockSpec(memory_space=pltpu.SMEM)
@@ -71,13 +70,17 @@
     count = ref.shape[0]
     breadth = ref.shape[1]
 
-    @pl.when(edges[0] == 1)
-    def _():
-        ref[0:rows_top] = jnp.zeros((rows_top, breadth, CH), F32)
-
-    @pl.when(edges[1] == 1)
-    def _():
-        ref[count - rows_bottom : count] = jnp.zeros((rows_bottom, breadth, CH), F32)
+    if rows_top:
+
+        @pl.when(edges[0] == 1)
+        def _():
+            ref[0:rows_top] = jnp.zeros((rows_top, breadth, CH), F32)
+
+    if rows_bottom:
+
+        @pl.when(edges[1] == 1)
+        def _():
+            ref[count - rows_bottom : count] = jnp.zeros((rows_bottom, breadth, CH), F32)
 
     @pl.when(edges[2] == 1)
     def _():
@@ -97,33 +100,167 @@
     )
 
 
-def forward_kernel(last, *refs):
+INNER = (0, 2, 6)
+DSKIP = (4, 3, 0)
+
+
+def act_rows(src, taps, layer, r, number, want_slope, h_buf, h_at, slope_buf, slope_at, hid_own, own_at):
+    low, high = SPAN[layer]
+    dlow, dhigh = DSPAN[layer]
+    for q in range(number):
+        hid_parts, slope_parts = [], []
+        for c, width in chunks(low, high, 32):
+            half = tap_sum(src, RH + r + q, PAD + c, width, 2**layer, 1, taps, (-1, 0, 1))
+            hidden, slope = gelu_parts(half, want_slope)
+            hid_parts.append(hidden.reshape(width, CH))
+            if want_slope:
+                slope_parts.append(slope.reshape(width, CH))
+        hidden = jnp.concatenate(hid_parts, 0)
+        h_buf[h_at + q] = hidden.astype(BF)
+        if hid_own is not None:
+            hid_own[own_at + q] = hidden[8:136].astype(BF)
+        if want_slope:
+            slope = jnp.concatenate(slope_parts, 0)
+            slope_buf[slope_at + q] = slope[dlow - low : dhigh - low].astype(BF)
+
+
+def mixed_rows(h_buf, h_at, src, r, step, layer, weights):
+    low, high = SPAN[layer]
+    mixed = jnp.dot(
+        h_buf[pl.ds(h_at, step)].reshape(step * (high - low), CH),
+        weights[layer],
+        preferred_element_type=F32,
+    ).reshape(step, high - low, CH)
+    return src[pl.ds(RH + r, step), PAD + low : PAD + high] + mixed
+
+
+def inner_kernel(*refs):
+    refs = list(refs)
+    take = lambda n: [refs.pop(0) for _ in range(n)]
+    edges, own, left, right, kernels, weights = take(6)
+    hid_out, slope_out, x_out = take(3), take(3), take(3)
+    x_bufs, h_bufs, slopes = take(4), take(3), take(3)
+    hid_two, sem = take(2)
+
+    def build(r, _):
+        x_bufs[0][RH + r, PAD : PAD + 16] = left[r].astype(F32)
+        x_bufs[0][RH + r, PAD + 16 : PAD + 144] = own[r].astype(F32)
+        x_bufs[0][RH + r, PAD + 144 : PAD + 160] = right[r].astype(F32)
+        return 0
+
+    lax.fori_loop(0, ROWS, build, 0)
+    copies = []
+
+    def send(src, dst, slot):
+        copies.append(pltpu.make_async_copy(src, dst, sem.at[slot]))
+        copies[-1].start()
+
+    for layer in range(3):
+        src, dst = x_bufs[layer], x_bufs[layer + 1]
+        h_buf, slope_buf = h_bufs[layer], slopes[layer]
+        low, high = SPAN[layer]
+        edge = INNER[layer]
+        first, number = edge + 1, ROWS - 2 - 2 * edge
+        taps = rows_of(kernels[layer], 0.5)
+        hid_own = hid_two if layer == 2 else None
+
+        def body(it, _):
+            act_rows(
+                src, taps, layer, first + 2 * it, 2, True,
+                h_buf, 2 * it, slope_buf, 2 * it, hid_own, 2 * it,
+            )
+            return 0
+
+        lax.fori_loop(0, number // 2, body, 0)
+        rows = pl.ds(first, number)
+        hid_src = hid_two if layer == 2 else h_buf.at[:, pl.ds(16 - low, COLS)]
+        send(hid_src, hid_out[layer].at[rows], layer)
+        send(slope_buf, slope_out[layer].at[pl.ds(DHALO[layer] + first, number)], 3 + layer)
+
+        step = (15, 13, 18)[layer]
+
+        def mix_body(it, _):
+            at = it * step
+            dst[pl.ds(RH + first + at, step), PAD + low : PAD + high] = mixed_rows(
+                h_buf, at, src, first + at, step, layer, weights
+            )
+            return 0
+
+        lax.fori_loop(0, number // step, mix_body, 0)
+        clear_outside(dst, edges, 0, 0, PAD, PAD + 16 + COLS)
+        depth = (4, 8, 18)[layer]
+        send(dst.at[pl.ds(RH + first, depth)], x_out[layer].at[pl.ds(0, depth)], 6 + layer)
+        if layer < 2:
+            send(
+                dst.at[pl.ds(RH + first + number - depth, depth)],
+                x_out[layer].at[pl.ds(depth, depth)],
+                9 + layer,
+            )
+    for copy in copies:
+        copy.wait()
+
+
+XWIDE = WIDE + 2 * PAD
+SLOPE_SHAPES = [(ROWS + 2 * DHALO[k], DSPAN[k][1] - DSPAN[k][0], CH) for k in range(4)]
+
+
+def inner(edges, own, left, right, kernels, weights):
+    outs = [sds((ROWS, COLS, CH), BF)] * 3
+    outs += [sds(s, BF) for s in SLOPE_SHAPES[:3]]
+    outs += [sds((n, XWIDE, CH), F32) for n in (8, 16, 18)]
+    numbers = [ROWS - 2 - 2 * e for e in INNER]
+    scratch = [pltpu.VMEM((ROWS + 2 * RH, XWIDE, CH), F32)] * 4
+    scratch += [pltpu.VMEM((numbers[k], SPAN[k][1] - SPAN[k][0], CH), BF) for k in range(3)]
+    scratch += [pltpu.VMEM((numbers[k], SLOPE_SHAPES[k][1], CH), BF) for k in range(3)]
+    scratch += [pltpu.VMEM((numbers[2], COLS, CH), BF), pltpu.SemaphoreType.DMA((11,))]
+    return pl.pallas_call(
+        inner_kernel,
+        out_shape=outs,
+        in_specs=[SMEM] + [VMEM] * 5,
+        out_specs=[ANY] * 9,
+        scratch_shapes=scratch,
+        compiler_params=pltpu.CompilerParams(vmem_limit_bytes=52 * 2**20),
+        cost_estimate=pl.CostEstimate(
+            flops=4 * 2 * 3000 * CH * CH, bytes_accessed=12 * 2**20, transcendentals=0
+        ),
+        name="forward_inner",
+    )(edges, own, left, right, kernels, weights)
+
+
+def outer_kernel(last, *refs):
     refs = list(refs)
     take = lambda n: [refs.pop(0) for _ in range(n)]
     edges, own, left, right, top, bottom, kernels, weights = take(8)
     if last:
         coarse, cot, back_weight = take(3)
+    x_in = take(3)
+    take(6)
+    if last:
         out, pre, pre_left, pre_right, grad = take(5)
-        kept = take(3 + 3)
     else:
-        x_out, x_left, x_right = take(3)
-        kept = take(4 + 4)
-    count = len(kept) // 2
-    hid_out, slope_out = kept[:count], kept[count:]
-    x_bufs = take(2)
-    h_bufs = take(4)
-    hid_two = take(1)[0]
-    slopes = take(4)
-    sem = take(1)[0]
-    own_buf = take(1)[0]
-
-    def build(r, _):
+        x_out, x_left, x_right, hid_three, slope_three = take(5)
+    hid_out, slope_out = take(3), take(3)
+    x_bufs, h_bufs, slopes = take(4), take(4), take(4)
+    hid_two, own_buf, sem = take(3)
+
+    loads = []
+    for layer in range(3):
+        first = INNER[layer] + 1
+        depth = (4, 8, 18)[layer]
+        spots = [(first, 0)] if layer == 2 else [(first, 0), (ROWS - first - depth, depth)]
+        for k, (r, at) in enumerate(spots):
+            copy = pltpu.make_async_copy(
+                x_in[layer].at[pl.ds(at, depth)],
+                x_bufs[layer + 1].at[pl.ds(RH + r, depth)],
+                sem.at[20 + 2 * layer + k],
+            )
+            copy.start()
+            loads.append((layer, copy))
+
+    for r in (0, 1, ROWS - 2, ROWS - 1):
         x_bufs[0][RH + r, PAD : PAD + 16] = left[r].astype(F32)
         x_bufs[0][RH + r, PAD + 16 : PAD + 144] = own[r].astype(F32)
         x_bufs[0][RH + r, PAD + 144 : PAD + 160] = right[r].astype(F32)
-        return 0
-
-    lax.fori_loop(0, ROWS, build, 0)
 
     def build_ends(r, _):
         x_bufs[0][r, PAD : PAD + WIDE] = top[r].astype(F32)
@@ -131,111 +268,102 @@
         return 0
 
     lax.fori_loop(0, RH, build_ends, 0)
-
     copies = []
-    for layer in range(4):
-        dilate = 2**layer
-        halo = HALO[layer]
+
+    def send(src, dst, slot):
+        copies.append(pltpu.make_async_copy(src, dst, sem.at[slot]))
+        copies[-1].start()
+
+    for layer in range(3):
+        src, dst = x_bufs[layer], x_bufs[layer + 1]
+        h_buf, slope_buf = h_bufs[layer], slopes[layer]
+        halo, edge, dhalo = HALO[layer], INNER[layer], DHALO[layer]
         low, high = SPAN[layer]
-        breadth = high - low
-        dhalo = DHALO[layer]
-        dlow, dhigh = DSPAN[layer]
-        src, dst = x_bufs[layer % 2], x_bufs[(layer + 1) % 2]
-        h_buf, slope_buf = h_bufs[layer], slopes[layer]
         taps = rows_of(kernels[layer], 0.5)
-
-        def act_rows(r, number, want_slope, own_rows):
-            for q in range(number):
-                hid_parts, slope_parts = [], []
-                for c, width in chunks(low, high, 32):
-                    half = tap_sum(
-                        src, RH + r + q, PAD + c, width, dilate, 1, taps, (-1, 0, 1)
-                    )
-                    hidden, slope = gelu_parts(half, want_slope)
-                    hid_parts.append(hidden.reshape(width, CH))
-                    if want_slope:
-                        slope_parts.append(slope.reshape(width, CH))
-                hidden = jnp.concatenate(hid_parts, 0)
-                h_buf[halo + r + q] = hidden.astype(BF)
-                if layer == 2 and own_rows:
-                    hid_two[r + q] = hidden[8:136].astype(BF)
-                if want_slope:
-                    slope = jnp.concatenate(slope_parts, 0)
-                    slope_buf[dhalo + r + q] = slope[dlow - low : dhigh - low].astype(BF)
-
-        number = 4
-        outer = halo - dhalo
-        if outer:
-            each = outer // number
-
-            def outer_body(it, _):
-                r = jnp.where(it < each, it * number - halo, ROWS + dhalo + (it - each) * number)
-                act_rows(r, number, False, False)
+        hid_own = hid_two if layer == 2 else None
+        skip = DSKIP[layer]
+        kept = 5 - skip
+
+        if skip:
+
+            def far_body(it, _):
+                low_side = it >= skip
+                at = jnp.where(low_side, 15 + 3 * kept + 3 * (it - skip), 3 * it)
+                r = jnp.where(low_side, ROWS - 1 - edge - 15, -halo) + at
+                act_rows(src, taps, layer, r, 3, False, h_buf, at, None, 0, None, 0)
                 return 0
 
-            lax.fori_loop(0, 2 * each, outer_body, 0)
-        if layer == 2:
-
-            def ring_body(it, _):
-                r = jnp.where(it < 2, it * number - halo, ROWS + (it - 2) * number)
-                act_rows(r, number, True, False)
-                return 0
-
-            lax.fori_loop(0, 4, ring_body, 0)
-            first, rows_here = 0, ROWS
+            lax.fori_loop(0, 2 * skip, far_body, 0)
+
+        def near_body(it, _):
+            low_side = it >= kept
+            at = jnp.where(low_side, 15 + 3 * (it - kept), 3 * skip + 3 * it)
+            r = jnp.where(low_side, ROWS - 1 - edge - 15, -halo) + at
+            act_rows(src, taps, layer, r, 3, True, h_buf, at, slope_buf, 3 * it, hid_own, at)
+            return 0
+
+        lax.fori_loop(0, 2 * kept, near_body, 0)
+
+        whole = hid_two if layer == 2 else h_buf
+        cols = pl.ds(0, COLS) if layer == 2 else pl.ds(16 - low, COLS)
+        send(whole.at[pl.ds(halo, edge + 1), cols], hid_out[layer].at[pl.ds(0, edge + 1)], layer)
+        send(
+            whole.at[pl.ds(15, edge + 1), cols],
+            hid_out[layer].at[pl.ds(ROWS - 1 - edge, edge + 1)],
+            3 + layer,
+        )
+        number = 3 * kept
+        send(slope_buf.at[pl.ds(0, number)], slope_out[layer].at[pl.ds(0, number)], 6 + layer)
+        send(
+            slope_buf.at[pl.ds(number, number)],
+            slope_out[layer].at[pl.ds(dhalo + ROWS - 1 - edge, number)],
+            9 + layer,
+        )
+        for which, copy in loads:
+            if which == layer:
+                copy.wait()
+
+        def mix_body(it, _):
+            r = jnp.where(it == 0, -halo, ROWS - 1 - edge)
+            dst[pl.ds(RH + r, 15), PAD + low : PAD + high] = mixed_rows(
+                h_buf, 15 * it, src, r, 15, layer, weights
+            )
+            return 0
+
+        lax.fori_loop(0, 2, mix_body, 0)
+        clear_outside(dst, edges, RH, RH, PAD, PAD + 16 + COLS)
+
+    taps = rows_of(kernels[3], 0.5)
+
+    def last_body(it, _):
+        act_rows(
+            x_bufs[3], taps, 3, 4 * it, 4, True, h_bufs[3], 4 * it, slopes[3], 4 * it, None, 0
+        )
+        return 0
+
+    lax.fori_loop(0, ROWS // 4, last_body, 0)
+    if not last:
+        send(h_bufs[3], hid_three, 12)
+        send(slopes[3], slope_three, 13)
+
+    def last_mix(it, _):
+        at = 16 * it
+        value = mixed_rows(h_bufs[3], at, x_bufs[3], at, 16, 3, weights)
+        if last:
+            for q in range(2):
+                extra = coarse[2 * it + q][:, None, :]
+                part = value[q * STRIDE : (q + 1) * STRIDE].reshape(STRIDE, -1, STRIDE, CH)
+                part = (part + extra[None]).reshape(STRIDE, COLS, CH)
+                own_buf[pl.ds(at + q * STRIDE, STRIDE)] = part.astype(BF)
         else:
-            first, rows_here = -dhalo, ROWS + 2 * dhalo
-
-        def inner_body(it, _):
-            act_rows(first + it * number, number, True, True)
-            return 0
-
-        lax.fori_loop(0, rows_here // number, inner_body, 0)
-
-        if layer < count:
-            if layer == 2:
-                hid_src = hid_two
-            else:
-                hid_src = h_buf.at[pl.ds(halo, ROWS), pl.ds(16 - low, COLS)]
-            copies.append(pltpu.make_async_copy(hid_src, hid_out[layer], sem.at[layer]))
-            copies.append(pltpu.make_async_copy(slope_buf, slope_out[layer], sem.at[4 + layer]))
-            copies[-1].start()
-            copies[-2].start()
-
-        step = BLOCK[layer]
-        total = ROWS + 2 * halo
-
-        def mix_body(it, _):
-            at = it * step
-            mixed = jnp.dot(
-                h_buf[pl.ds(at, step)].reshape(step * breadth, CH),
-                weights[layer],
-                preferred_element_type=F32,
-            ).reshape(step, breadth, CH)
-            rows = pl.ds(RH - halo + at, step)
-            value = src[rows, PAD + low : PAD + high] + mixed
-            if layer < 3:
-                dst[rows, PAD + low : PAD + high] = value
-            elif last:
-                for q in range(step // STRIDE):
-                    extra = coarse[it * (step // STRIDE) + q][:, None, :]
-                    part = value[q * STRIDE : (q + 1) * STRIDE].reshape(STRIDE, -1, STRIDE, CH)
-                    part = (part + extra[None]).reshape(STRIDE, COLS, CH)
-                    own_buf[pl.ds(at + q * STRIDE, STRIDE)] = part.astype(BF)
-            else:
-                value = value.astype(BF)
-                own_buf[pl.ds(at, step)] = value
-                x_left[pl.ds(at, step)] = value[:, :CHALO]
-                x_right[pl.ds(at, step)] = value[:, COLS - CHALO :]
-            return 0
-
-        lax.fori_loop(0, total // step, mix_body, 0)
-        if layer < 3:
-            clear_outside(dst, edges, RH, RH, PAD, PAD + 16 + COLS)
-
-    result = out if last else x_out
-    copies.append(pltpu.make_async_copy(own_buf, result, sem.at[8]))
-    copies[-1].start()
+            value = value.astype(BF)
+            own_buf[pl.ds(at, 16)] = value
+            x_left[pl.ds(at, 16)] = value[:, :CHALO]
+            x_right[pl.ds(at, 16)] = value[:, COLS - CHALO :]
+        return 0
+
+    lax.fori_loop(0, 2, last_mix, 0)
+    send(own_buf, out if last else x_out, 14)
     if last:
         total = jnp.zeros((CH, CH), F32)
         for b in range(2):
@@ -253,41 +381,38 @@
         copy.wait()
 
 
-def forward(last, edges, own, left, right, top, bottom, kernels, weights, extra=()):
-    count = 3 if last else 4
+def outer(last, edges, own, left, right, top, bottom, kernels, weights, begun, extra=()):
     block = sds((ROWS, COLS, CH), BF)
     strip = sds((ROWS, CHALO, CH), BF)
-    hid_shapes = [block] * count
-    slope_shapes = [
-        sds((ROWS + 2 * DHALO[k], DSPAN[k][1] - DSPAN[k][0], CH), BF) for k in range(4)
-    ]
     if last:
         outs = [block, block, strip, strip, sds((CH, CH), F32)]
         specs = [ANY] + [VMEM] * 4
     else:
-        outs = [block, strip, strip]
-        specs = [ANY, VMEM, VMEM]
-    outs = outs + hid_shapes + slope_shapes[:count]
-    specs = specs + [ANY] * (2 * count)
-    scratch = [pltpu.VMEM((ROWS + 2 * RH, WIDE + 2 * PAD, CH), F32)] * 2
-    scratch += [
-        pltpu.VMEM((ROWS + 2 * HALO[k], SPAN[k][1] - SPAN[k][0], CH), BF) for k in range(4)
-    ]
-    scratch += [pltpu.VMEM((ROWS, COLS, CH), BF)]
-    scratch += [pltpu.VMEM(s.shape, BF) for s in slope_shapes]
-    scratch += [pltpu.SemaphoreType.DMA((9,)), pltpu.VMEM((ROWS, COLS, CH), BF)]
+        outs = [block, strip, strip, block, block]
+        specs = [ANY, VMEM, VMEM, ANY, ANY]
+    outs = outs + [sds(a.shape, BF) for a in begun[:6]]
+    specs = specs + [ANY] * 6
+    args = (edges, own, left, right, top, bottom, kernels, weights, *extra, *begun[6:], *begun[:6])
+    scratch = [pltpu.VMEM((ROWS + 2 * RH, XWIDE, CH), F32)] * 4
+    heights = [30, 30, 30, ROWS]
+    scratch += [pltpu.VMEM((heights[k], SPAN[k][1] - SPAN[k][0], CH), BF) for k in range(4)]
+    tall = [6 * (5 - DSKIP[k]) for k in range(3)] + [ROWS]
+    scratch += [pltpu.VMEM((tall[k], SLOPE_SHAPES[k][1], CH), BF) for k in range(4)]
+    scratch += [pltpu.VMEM((30, COLS, CH), BF), pltpu.VMEM((ROWS, COLS, CH), BF)]
+    scratch += [pltpu.SemaphoreType.DMA((26,))]
     return pl.pallas_call(
-        functools.partial(forward_kernel, last),
+        functools.partial(outer_kernel, last),
         out_shape=outs,
-        in_specs=[SMEM] + [VMEM] * (7 + len(extra)),
+        in_specs=[SMEM] + [VMEM] * (7 + len(extra)) + [ANY] * 9,
         out_specs=specs,
         scratch_shapes=scratch,
+        input_output_aliases={len(args) - 6 + k: 5 + k for k in range(6)},
         compiler_params=pltpu.CompilerParams(vmem_limit_bytes=52 * 2**20),
         cost_estimate=pl.CostEstimate(
-            flops=4 * 2 * 8000 * CH * CH, bytes_accessed=12 * 2**20, transcendentals=0
+            flops=4 * 2 * 5000 * CH * CH, bytes_accessed=12 * 2**20, transcendentals=0
         ),
         name="forward_last" if last else "forward_first",
-    )(edges, own, left, right, top, bottom, kernels, weights, *extra)
+    )(*args)
 
 
 def pool_kernel(feature, cot, weight, weight_t, coarse, back, grad):
@@ -590,14 +715,16 @@
     cot_left, cot_right = from_left[:, CHALO:], from_right[:, CHALO:]
     top, bottom = exchange(*row_strips(features_in, left, right), "rows")
     coarse, back, coarse_grad = pool(features_in, cotangent, coarse_weight)
-    x_mid, x_left, x_right, *kept = forward(
-        False, edges, features_in, left, right, top, bottom, kernels[:4], point_weights[:4]
+    begun = inner(edges, features_in, left, right, kernels[:3], point_weights[:3])
+    x_mid, x_left, x_right, hid_three, slope_three, *kept = outer(
+        False, edges, features_in, left, right, top, bottom, kernels[:4], point_weights[:4], begun
     )
-    hid_low, slope_low = kept[:4], kept[4:]
+    hid_low, slope_low = kept[:3] + [hid_three], kept[3:] + [slope_three]
     left, right = exchange(x_left, x_right, "cols")
     top, bottom = exchange(*row_strips(x_mid, left, right), "rows")
-    output, pre, pre_left, pre_right, grad_top, *kept = forward(
-        True, edges, x_mid, left, right, top, bottom, kernels[4:], point_weights[4:],
+    begun = inner(edges, x_mid, left, right, kernels[4:7], point_weights[4:7])
+    output, pre, pre_left, pre_right, grad_top, *kept = outer(
+        True, edges, x_mid, left, right, top, bottom, kernels[4:], point_weights[4:], begun,
         (coarse, cotangent, weights_t[7]),
     )
     hid_high, slope_high = kept[:3], kept[3:]
@@ -621,10 +748,11 @@
     )
 
     grads = [grad_low[2], grad_low[1], grad_low[0], grad_mid[3], grad_mid[2], grad_mid[1]]
-    grads = jnp.stack(grads + [grad_mid[0], grad_top, coarse_grad], axis=1).astype(BF)
-    shares = lax.all_to_all(grads, ("rows", "cols"), 0, 0, tiled=True)
-    summed = shares.astype(F32).sum(axis=0)
-    weight_grads = lax.all_gather(summed[:, None, :], "cols", axis=1, tiled=True)
+    grads = jnp.stack(grads + [grad_mid[0], grad_top, coarse_grad]).astype(BF)
+    shares = lax.all_to_all(grads, "rows", 1, 0, tiled=True)
+    summed = shares.reshape(-1, grads.shape[0], CH * 4).astype(F32).sum(axis=0)
+    parts = lax.all_gather(summed, "cols", axis=0, tiled=False)
+    weight_grads = parts.sum(axis=0).reshape(grads.shape[0], 4, CH)
     return (output, input_grad, weight_grads)
 
 

time: 239 us -> 228 us (0.954)
  waiting for transfers between devices: 66.7 us -> 47.5 us
  Pallas kernels: 80.3 us -> 87.8 us
  blocking collectives: 33 us -> 30.6 us
    ppermute x8, waiting for transfers between devices: 28.4 us -> 16.9 us  [exchange(): lax.ppermute(to_after, axis, forth)]
    ppermute x8, waiting for transfers between devices: 38.3 us -> 30.6 us  [exchange(): lax.ppermute(to_before, axis, back)]
    pallas_call x2 -> x4, Pallas kernels: 46.9 us -> 54.3 us  [the longest x2 31.9 us: outer(): pl.pallas_call(functools.partial(outer_kernel, last), out_shape=outs, in_...]
    unnamed x41 -> x45, local copies, waits for them, and re-layouts: 6.86 us -> 9.2 us
  transfers between devices with their start and end apart: 16 -> 16, of which waited for: 14 -> 10; matrix products, arithmetic and copies ran while one was open for 3% -> 3% of each run, Pallas kernels for 0% -> 10%
where the time goes in v2:
time: 228 us; the launch traced here: 227 us
  Pallas kernels  87.8 us (39%)
  waiting for transfers between devices  47.5 us (21%)
  starting transfers between devices  43.9 us (19%)
  blocking collectives  30.6 us (13%)
  local copies, waits for them, and re-layouts  14.1 us (6%)
    pallas_call x2, Pallas kernels, outer(): pl.pallas_call(functools.partial(outer_kernel, last), out_shape=outs, in_...  31.9 us
    pallas_call x2, Pallas kernels, backward(): pl.pallas_call(functools.partial(backward_kernel, last), out_shape=outs,...  31.2 us
    ppermute x8, waiting for transfers between devices, exchange(): lax.ppermute(to_before, axis, back)  30.6 us
    ppermute x8, starting transfers between devices, exchange(): lax.ppermute(to_after, axis, forth)  29.8 us
    all_to_all x1, blocking collectives, local(): shares = lax.all_to_all(grads, 'rows', 1, 0, tiled=True)  23.9 us
    pallas_call x2, Pallas kernels, inner(): pl.pallas_call(inner_kernel, out_shape=outs, in_specs=[SMEM] + [VMEM] * 5...  22.4 us
    ppermute x8, waiting for transfers between devices, exchange(): lax.ppermute(to_after, axis, forth)  16.9 us
    ppermute x8, starting transfers between devices, exchange(): lax.ppermute(to_before, axis, back)  14.1 us
  transfers between devices with their start and end apart: 16, of which 10 were waited for; matrix products, arithmetic and copies ran while one was open for 3% of the time, Pallas kernels for 10%

profile of v2, /device:TPU:1, one launch (start us, length us, event | category | flops | bytes accessed | tf_op | source)
XLA Modules:
  0.0 227.4 jit_solution(4120990616072182255)
XLA Ops:
  1.9 6.2 %collective-permute-start = (bf16[32,32,128]{2,1,0:T(8,128)(2,1)S(1)}, bf16[32,32,128]{2,1,0:T(8,128)(2,1)S(1)}, u32[]{:S(2)}, u32[]{:S(2)}) collective-permute-start(bf16[32,32,128]{2,1,0:T(8,128)(2,1)S(1)} %pad_maximum_fusion.4), channel_id=1, source_target_pairs={{0,1},{1,2},{2,3},{4,5},{5,6},{6,7},{8,9},{9,10},{10,11},{12,13},{... | collective-permute-start | bytes 786440 | tf_op jit(solution)/shard_map/ppermute | solution.py:695
  11.5 5.8 %collective-permute-done.1 = bf16[32,32,128]{2,1,0:T(8,128)(2,1)S(1)} collective-permute-done((bf16[32,32,128]{2,1,0:T(8,128)(2,1)S(1)}, bf16[32,32,128]{2,1,0:T(8,128)(2,1)S(1)}, u32[]{:S(2)}, u32[]{:S(2)}) %collective-permute-start.1) | collective-permute-done | bytes 262176 | tf_op jit(solution)/shard_map/ppermute | solution.py:695
  17.3 3.6 %collective-permute-start.2 = (bf16[15,160,128]{2,1,0:T(8,128)(2,1)S(1)}, bf16[15,160,128]{2,1,0:T(8,128)(2,1)S(1)}, u32[]{:S(2)}, u32[]{:S(2)}) collective-permute-start(bf16[15,160,128]{2,1,0:T(8,128)(2,1)S(1)} %pad_maximum_fusion), channel_id=1, source_target_pairs={{0,4},{4,8},{8,12},{12,16},{16,20},{20,24},{24,28},{28,32},{32,36}... | collective-permute-start | bytes 1843208 | tf_op jit(solution)/shard_map/ppermute | solution.py:695
  22.4 11.2 %forward_inner.2 = (bf16[32,128,128]{2,1,0:T(8,128)(2,1)}, bf16[32,128,128]{2,1,0:T(8,128)(2,1)}, bf16[32,128,128]{2,1,0:T(8,128)(2,1)}, bf16[36,144,128]{2,1,0:...) custom-call(s32[4]{0:T(128)S(1)} %add_convert_fusion.refs_0_, ...), custom_call_target="tpu_custom_call" | custom-call | flops 393216000 | bytes 12582912 | tf_op jit(solution)/shard_map/forward_inner/pallas_call | solution.py:216
  34.5 15.1 %forward_first.1 = (bf16[32,128,128]{2,1,0:T(8,128)(2,1)}, bf16[32,16,128]{2,1,0:T(8,128)(2,1)S(1)}, bf16[32,16,128]{2,1,0:T(8,128)(2,1)S(1)}, bf16[32,128,128]{...) custom-call(s32[4]{0:T(128)S(1)} %add_convert_fusion.refs_0_, ...), custom_call_target="tpu_custom_call", output_to_operand_aliasing={{5}: (11, {}), {6}: (12, {}), {7}: (13, {}), {8}: (14, {}),... | custom-call | flops 655360000 | bytes 12582912 | tf_op jit(solution)/shard_map/forward_first/pallas_call | solution.py:403
  51.7 2.3 collective-permute-start.5
  55.3 4.2 %collective-permute-done.5.refs_3_ = bf16[32,16,128]{2,1,0:T(8,128)(2,1)S(1)} collective-permute-done((bf16[32,16,128]{2,1,0:T(8,128)(2,1)S(1)}, bf16[32,16,128]{2,1,0:T(8,128)(2,1)S(1)}, u32[]{:S(2)}, u32[]{:S(2)}) %collective-permute-start.5) | collective-permute-done | bytes 131104 | tf_op jit(solution)/shard_map/ppermute | solution.py:695
  60.5 4.1 %collective-permute-start.6 = (bf16[15,160,128]{2,1,0:T(8,128)(2,1)}, bf16[15,160,128]{2,1,0:T(8,128)(2,1)S(1)}, u32[]{:S(2)}, u32[]{:S(2)}) collective-permute-start(bf16[15,160,128]{2,1,0:T(8,128)(2,1)} %pad_maximum_fusion.2), channel_id=1, source_target_pairs={{0,4},{4,8},{8,12},{12,16},{16,20},{20,24},{24,28},{28,32},{32,36}... | collective-permute-start | bytes 1843208 | tf_op jit(solution)/shard_map/ppermute | solution.py:695
  69.7 11.2 %forward_inner.3 = (bf16[32,128,128]{2,1,0:T(8,128)(2,1)}, bf16[32,128,128]{2,1,0:T(8,128)(2,1)}, bf16[32,128,128]{2,1,0:T(8,128)(2,1)}, bf16[36,144,128]{2,1,0:...) custom-call(s32[4]{0:T(128)S(1)} %add_convert_fusion.refs_0_, ...), custom_call_target="tpu_custom_call" | custom-call | flops 393216000 | bytes 12582912 | tf_op jit(solution)/shard_map/forward_inner/pallas_call | solution.py:216
  81.9 16.8 %forward_last.1 = (bf16[32,128,128]{2,1,0:T(8,128)(2,1)}, bf16[32,128,128]{2,1,0:T(8,128)(2,1)}, bf16[32,16,128]{2,1,0:T(8,128)(2,1)S(1)}, bf16[32,16,128]{2,1,0...) custom-call(s32[4]{0:T(128)S(1)} %add_convert_fusion.refs_0_, ...), custom_call_target="tpu_custom_call", output_to_operand_aliasing={{5}: (14, {}), {6}: (15, {}), {7}: (16, {}), {8}: (17, {}),... | custom-call | flops 655360000 | bytes 12582912 | tf_op jit(solution)/shard_map/forward_last/pallas_call | solution.py:403
  100.6 2.4 %collective-permute-start.9 = (bf16[32,16,128]{2,1,0:T(8,128)(2,1)S(1)}, bf16[32,16,128]{2,1,0:T(8,128)(2,1)S(1)}, u32[]{:S(2)}, u32[]{:S(2)}) collective-permute-start(bf16[32,16,128]{2,1,0:T(8,128)(2,1)S(1)} %get-tuple-element.82), channel_id=1, source_target_pairs={{1,0},{2,1},{3,2},{5,4},{6,5},{7,6},{9,8},{10,9},{11,10},{13,12},{... | collective-permute-start | bytes 393224 | tf_op jit(solution)/shard_map/ppermute | solution.py:695
  103.8 4.7 %collective-permute-done.9.pre_right.refs_3_ = bf16[32,16,128]{2,1,0:T(8,128)(2,1)S(1)} collective-permute-done((bf16[32,16,128]{2,1,0:T(8,128)(2,1)S(1)}, bf16[32,16,128]{2,1,0:T(8,128)(2,1)S(1)}, u32[]{:S(2)}, u32[]{:S(2)}) %collective-permute-start.9) | collective-permute-done | bytes 131104 | tf_op jit(solution)/shard_map/ppermute | solution.py:695
  110.5 6.1 %collective-permute-start.10 = (bf16[15,160,128]{2,1,0:T(8,128)(2,1)S(1)}, bf16[15,160,128]{2,1,0:T(8,128)(2,1)S(1)}, u32[]{:S(2)}, u32[]{:S(2)}) collective-permute-start(bf16[15,160,128]{2,1,0:T(8,128)(2,1)S(1)} %get-tuple-element.83), channel_id=1, source_target_pairs={{0,4},{4,8},{8,12},{12,16},{16,20},{20,24},{24,28},{28,32},{32,36}... | collective-permute-start | bytes 1843208 | tf_op jit(solution)/shard_map/ppermute | solution.py:695
  118.0 8.5 %collective-permute-done.10.refs_7_ = bf16[15,160,128]{2,1,0:T(8,128)(2,1)S(1)} collective-permute-done((bf16[15,160,128]{2,1,0:T(8,128)(2,1)S(1)}, bf16[15,160,128]{2,1,0:T(8,128)(2,1)S(1)}, u32[]{:S(2)}, u32[]{:S(2)}) %collective-permute-start.10) | collective-permute-done | bytes 614432 | tf_op jit(solution)/shard_map/ppermute | solution.py:695
  126.5 4.1 %collective-permute-done.11.refs_8_ = bf16[15,160,128]{2,1,0:T(8,128)(2,1)S(1)} collective-permute-done((bf16[15,160,128]{2,1,0:T(8,128)(2,1)S(1)}, bf16[15,160,128]{2,1,0:T(8,128)(2,1)S(1)}, u32[]{:S(2)}, u32[]{:S(2)}) %collective-permute-start.11) | collective-permute-done | bytes 614432 | tf_op jit(solution)/shard_map/ppermute | solution.py:695
  131.5 15.9 %backward_first.1 = (f32[32,128,128]{2,1,0:T(8,128)}, bf16[32,128,128]{2,1,0:T(8,128)(2,1)}, bf16[32,32,128]{2,1,0:T(8,128)(2,1)S(1)}, bf16[32,32,128]{2,1,0:T(8,128)(2,1)S(1)}, f32[4,128,128]{2,1,0:T(8,128)S(1)}) custom-call(s32[4]{0:T(128)S(1)} %add_convert_fusion.refs_0_, bf16[32,128,128]{2,1,0:T(8,128)(2,1)} %get-tuple-element.80.pre.refs_1_, ...), custom_call_target="tpu_custom_call" | custom-call | flops 1146880000 | bytes 14680064 | tf_op jit(solution)/shard_map/backward_first/pallas_call | solution.py:677
  149.5 2.4 %collective-permute-start.13 = (bf16[32,32,128]{2,1,0:T(8,128)(2,1)S(1)}, bf16[32,32,128]{2,1,0:T(8,128)(2,1)S(1)}, u32[]{:S(2)}, u32[]{:S(2)}) collective-permute-start(bf16[32,32,128]{2,1,0:T(8,128)(2,1)S(1)} %get-tuple-element.95), channel_id=1, source_target_pairs={{1,0},{2,1},{3,2},{5,4},{6,5},{7,6},{9,8},{10,9},{11,10},{13,12},{... | collective-permute-start | bytes 786440 | tf_op jit(solution)/shard_map/ppermute | solution.py:695
  152.8 5.9 %collective-permute-done.13 = bf16[32,32,128]{2,1,0:T(8,128)(2,1)S(1)} collective-permute-done((bf16[32,32,128]{2,1,0:T(8,128)(2,1)S(1)}, bf16[32,32,128]{2,1,0:T(8,128)(2,1)S(1)}, u32[]{:S(2)}, u32[]{:S(2)}) %collective-permute-start.13) | collective-permute-done | bytes 262176 | tf_op jit(solution)/shard_map/ppermute | solution.py:695
  161.1 3.7 %collective-permute-start.14 = (bf16[15,160,128]{2,1,0:T(8,128)(2,1)S(1)}, bf16[15,160,128]{2,1,0:T(8,128)(2,1)S(1)}, u32[]{:S(2)}, u32[]{:S(2)}) collective-permute-start(bf16[15,160,128]{2,1,0:T(8,128)(2,1)S(1)} %get-tuple-element.97), channel_id=1, source_target_pairs={{0,4},{4,8},{8,12},{12,16},{16,20},{20,24},{24,28},{28,32},{32,36}... | collective-permute-start | bytes 1843208 | tf_op jit(solution)/shard_map/ppermute | solution.py:695
  166.2 7.5 %collective-permute-done.14.refs_7_ = bf16[15,160,128]{2,1,0:T(8,128)(2,1)S(1)} collective-permute-done((bf16[15,160,128]{2,1,0:T(8,128)(2,1)S(1)}, bf16[15,160,128]{2,1,0:T(8,128)(2,1)S(1)}, u32[]{:S(2)}, u32[]{:S(2)}) %collective-permute-start.14) | collective-permute-done | bytes 614432 | tf_op jit(solution)/shard_map/ppermute | solution.py:695
  173.7 5.7 %collective-permute-done.15.refs_8_ = bf16[15,160,128]{2,1,0:T(8,128)(2,1)S(1)} collective-permute-done((bf16[15,160,128]{2,1,0:T(8,128)(2,1)S(1)}, bf16[15,160,128]{2,1,0:T(8,128)(2,1)S(1)}, u32[]{:S(2)}, u32[]{:S(2)}) %collective-permute-start.15) | collective-permute-done | bytes 614432 | tf_op jit(solution)/shard_map/ppermute | solution.py:695
  180.3 15.3 %backward_last.1 = (bf16[32,128,128]{2,1,0:T(8,128)(2,1)}, f32[3,128,128]{2,1,0:T(8,128)S(1)}) custom-call(s32[4]{0:T(128)S(1)} %add_convert_fusion.refs_0_, bf16[32,128,128]{2,1,0:T(8,128)(2,1)} %get-tuple-element.93.pre.refs_1_, bf16[32,16,128]{2,1,0:T(8,128)(2,1)S(1)} %get-tuple-element.124.pre_left.refs_2_, ...), custom_call_target="tpu_custom_call" | custom-call | flops 1146880000 | bytes 14680064 | tf_op jit(solution)/shard_map/backward_last/pallas_call | solution.py:677
  195.9 23.9 %all_to_all.4 = bf16[9,128,128]{2,0,1:T(8,128)(2,1)S(1)} all-to-all(bf16[9,128,128]{2,0,1:T(8,128)(2,1)S(1)} %copy.33), channel_id=1, replica_groups=mesh['rows'=32,'cols'=4] {'rows'}, dimensions={1} | all-to-all | bytes 589824 | tf_op jit(solution)/shard_map/all_to_all | solution.py:752
  219.9 6.8 %all_gather.7 = f32[4,9,512]{2,1,0:T(8,128)S(1)} all-gather(f32[1,9,512]{2,1,0:T(8,128)S(1)} %all_gather.6), channel_id=1, replica_groups=mesh['rows'=32,'cols'=4] {'cols'}, dimensions={0}, use_global_device_ids=true | all-gather | bytes 92160 | tf_op jit(solution)/shard_map/all_gather | solution.py:754
  (101 shorter events, 32.7 us)
Async XLA Ops:
  0.6 9.4 %copy-start.11 = (bf16[8,128,128]{2,1,0:T(8,128)(2,1)S(1)}, bf16[8,128,128]{2,1,0:T(8,128)(2,1)}, u32[]{:S(2)}) copy-start(bf16[8,128,128]{2,1,0:T(8,128)(2,1)} %param.8) | copy-start | bytes 786436
  1.8 8.9 %copy-start.2 = (bf16[32,128,128]{2,1,0:T(8,128)(2,1)S(1)}, bf16[32,128,128]{2,1,0:T(8,128)(2,1)}, u32[]{:S(2)}) copy-start(bf16[32,128,128]{2,1,0:T(8,128)(2,1)} %feature.1) | copy-start | bytes 3145732
  1.9 9.6 %collective-permute-start = (bf16[32,32,128]{2,1,0:T(8,128)(2,1)S(1)}, bf16[32,32,128]{2,1,0:T(8,128)(2,1)S(1)}, u32[]{:S(2)}, u32[]{:S(2)}) collective-permute-start(bf16[32,32,128]{2,1,0:T(8,128)(2,1)S(1)} %pad_maximum_fusion.4), channel_id=1, source_target_pairs={{0,1},{1,2},{2,3},{4,5},{5,6},{6,7},{8,9},{9,10},{10,11},{12,13},{... | collective-permute-start | bytes 786440 | tf_op jit(solution)/shard_map/ppermute | solution.py:695
  8.1 9.2 %collective-permute-start.1 = (bf16[32,32,128]{2,1,0:T(8,128)(2,1)S(1)}, bf16[32,32,128]{2,1,0:T(8,128)(2,1)S(1)}, u32[]{:S(2)}, u32[]{:S(2)}) collective-permute-start(bf16[32,32,128]{2,1,0:T(8,128)(2,1)S(1)} %pad_maximum_fusion.5), channel_id=1, source_target_pairs={{1,0},{2,1},{3,2},{5,4},{6,5},{7,6},{9,8},{10,9},{11,10},{13,12},{... | collective-permute-start | bytes 786440 | tf_op jit(solution)/shard_map/ppermute | solution.py:695
  11.4 9.6 %copy-start.16 = (f32[8,9,128]{2,1,0:T(8,128)}, f32[8,9,128]{2,1,0:T(8,128)S(1)}, u32[]{:S(2)}) copy-start(f32[8,9,128]{2,1,0:T(8,128)S(1)} %copy_convert_fusion) | copy-start | bytes 110596
  17.3 17.2 %collective-permute-start.2 = (bf16[15,160,128]{2,1,0:T(8,128)(2,1)S(1)}, bf16[15,160,128]{2,1,0:T(8,128)(2,1)S(1)}, u32[]{:S(2)}, u32[]{:S(2)}) collective-permute-start(bf16[15,160,128]{2,1,0:T(8,128)(2,1)S(1)} %pad_maximum_fusion), channel_id=1, source_target_pairs={{0,4},{4,8},{8,12},{12,16},{16,20},{20,24},{24,28},{28,32},{32,36}... | collective-permute-start | bytes 1843208 | tf_op jit(solution)/shard_map/ppermute | solution.py:695
  21.0 13.5 %collective-permute-start.3 = (bf16[15,160,128]{2,1,0:T(8,128)(2,1)S(1)}, bf16[15,160,128]{2,1,0:T(8,128)(2,1)S(1)}, u32[]{:S(2)}, u32[]{:S(2)}) collective-permute-start(bf16[15,160,128]{2,1,0:T(8,128)(2,1)S(1)} %pad_maximum_fusion.1), channel_id=1, source_target_pairs={{4,0},{8,4},{12,8},{16,12},{20,16},{24,20},{28,24},{32,28},{36,32}... | collective-permute-start | bytes 1843208 | tf_op jit(solution)/shard_map/ppermute | solution.py:695
  49.7 5.6 %collective-permute-start.4 = (bf16[32,16,128]{2,1,0:T(8,128)(2,1)S(1)}, bf16[32,16,128]{2,1,0:T(8,128)(2,1)S(1)}, u32[]{:S(2)}, u32[]{:S(2)}) collective-permute-start(bf16[32,16,128]{2,1,0:T(8,128)(2,1)S(1)} %get-tuple-element.67), channel_id=1, source_target_pairs={{0,1},{1,2},{2,3},{4,5},{5,6},{6,7},{8,9},{9,10},{10,11},{12,13},{... | collective-permute-start | bytes 393224 | tf_op jit(solution)/shard_map/ppermute | solution.py:695
  51.7 7.8 %collective-permute-start.5 = (bf16[32,16,128]{2,1,0:T(8,128)(2,1)S(1)}, bf16[32,16,128]{2,1,0:T(8,128)(2,1)S(1)}, u32[]{:S(2)}, u32[]{:S(2)}) collective-permute-start(bf16[32,16,128]{2,1,0:T(8,128)(2,1)S(1)} %get-tuple-element.68), channel_id=1, source_target_pairs={{1,0},{2,1},{3,2},{5,4},{6,5},{7,6},{9,8},{10,9},{11,10},{13,12},{... | collective-permute-start | bytes 393224 | tf_op jit(solution)/shard_map/ppermute | solution.py:695
  59.6 9.0 %copy-start.9 = (bf16[128,128]{1,0:T(8,128)(2,1)S(1)}, bf16[128,128]{1,0:T(8,128)(2,1)}, u32[]{:S(2)}) copy-start(bf16[128,128]{1,0:T(8,128)(2,1)} %weight.1) | copy-start | bytes 98308
  59.6 9.1 %copy-start = (bf16[32,128,128]{2,1,0:T(8,128)(2,1)S(1)}, bf16[32,128,128]{2,1,0:T(8,128)(2,1)}, u32[]{:S(2)}) copy-start(bf16[32,128,128]{2,1,0:T(8,128)(2,1)} %refs_4_.1) | copy-start | bytes 3145732
  59.6 9.1 %copy-start.3 = (bf16[32,128,128]{2,1,0:T(8,128)(2,1)S(1)}, bf16[32,128,128]{2,1,0:T(8,128)(2,1)}, u32[]{:S(2)}) copy-start(bf16[32,128,128]{2,1,0:T(8,128)(2,1)} %feature.1) | copy-start | bytes 3145732
  60.5 21.3 %collective-permute-start.6 = (bf16[15,160,128]{2,1,0:T(8,128)(2,1)}, bf16[15,160,128]{2,1,0:T(8,128)(2,1)S(1)}, u32[]{:S(2)}, u32[]{:S(2)}) collective-permute-start(bf16[15,160,128]{2,1,0:T(8,128)(2,1)} %pad_maximum_fusion.2), channel_id=1, source_target_pairs={{0,4},{4,8},{8,12},{12,16},{16,20},{20,24},{24,28},{28,32},{32,36}... | collective-permute-start | bytes 1843208 | tf_op jit(solution)/shard_map/ppermute | solution.py:695
  65.5 16.4 %collective-permute-start.7 = (bf16[15,160,128]{2,1,0:T(8,128)(2,1)}, bf16[15,160,128]{2,1,0:T(8,128)(2,1)}, u32[]{:S(2)}, u32[]{:S(2)}) collective-permute-start(bf16[15,160,128]{2,1,0:T(8,128)(2,1)} %pad_maximum_fusion.3), channel_id=1, source_target_pairs={{4,0},{8,4},{12,8},{16,12},{20,16},{24,20},{28,24},{32,28},{36,32}... | collective-permute-start | bytes 1843208 | tf_op jit(solution)/shard_map/ppermute | solution.py:695
  81.9 26.5 %copy-start.1 = (bf16[32,128,128]{2,1,0:T(8,128)(2,1)S(1)}, bf16[32,128,128]{2,1,0:T(8,128)(2,1)}, u32[]{:S(2)}) copy-start(bf16[32,128,128]{2,1,0:T(8,128)(2,1)} %refs_4_.1) | copy-start | bytes 3145732
  98.7 5.1 %collective-permute-start.8 = (bf16[32,16,128]{2,1,0:T(8,128)(2,1)S(1)}, bf16[32,16,128]{2,1,0:T(8,128)(2,1)S(1)}, u32[]{:S(2)}, u32[]{:S(2)}) collective-permute-start(bf16[32,16,128]{2,1,0:T(8,128)(2,1)S(1)} %get-tuple-element.81), channel_id=1, source_target_pairs={{0,1},{1,2},{2,3},{4,5},{5,6},{6,7},{8,9},{9,10},{10,11},{12,13},{... | collective-permute-start | bytes 393224 | tf_op jit(solution)/shard_map/ppermute | solution.py:695
  100.6 7.8 %collective-permute-start.9 = (bf16[32,16,128]{2,1,0:T(8,128)(2,1)S(1)}, bf16[32,16,128]{2,1,0:T(8,128)(2,1)S(1)}, u32[]{:S(2)}, u32[]{:S(2)}) collective-permute-start(bf16[32,16,128]{2,1,0:T(8,128)(2,1)S(1)} %get-tuple-element.82), channel_id=1, source_target_pairs={{1,0},{2,1},{3,2},{5,4},{6,5},{7,6},{9,8},{10,9},{11,10},{13,12},{... | collective-permute-start | bytes 393224 | tf_op jit(solution)/shard_map/ppermute | solution.py:695
  110.5 16.0 %collective-permute-start.10 = (bf16[15,160,128]{2,1,0:T(8,128)(2,1)S(1)}, bf16[15,160,128]{2,1,0:T(8,128)(2,1)S(1)}, u32[]{:S(2)}, u32[]{:S(2)}) collective-permute-start(bf16[15,160,128]{2,1,0:T(8,128)(2,1)S(1)} %get-tuple-element.83), channel_id=1, source_target_pairs={{0,4},{4,8},{8,12},{12,16},{16,20},{20,24},{24,28},{28,32},{32,36}... | collective-permute-start | bytes 1843208 | tf_op jit(solution)/shard_map/ppermute | solution.py:695
  116.6 14.0 %collective-permute-start.11 = (bf16[15,160,128]{2,1,0:T(8,128)(2,1)S(1)}, bf16[15,160,128]{2,1,0:T(8,128)(2,1)S(1)}, u32[]{:S(2)}, u32[]{:S(2)}) collective-permute-start(bf16[15,160,128]{2,1,0:T(8,128)(2,1)S(1)} %get-tuple-element.84), channel_id=1, source_target_pairs={{4,0},{8,4},{12,8},{16,12},{20,16},{24,20},{28,24},{32,28},{36,32}... | collective-permute-start | bytes 1843208 | tf_op jit(solution)/shard_map/ppermute | solution.py:695
  147.4 11.3 %copy-start.6 = (bf16[32,128,128]{2,1,0:T(8,128)(2,1)S(1)}, bf16[32,128,128]{2,1,0:T(8,128)(2,1)}, u32[]{:S(2)}) copy-start(bf16[32,128,128]{2,1,0:T(8,128)(2,1)} %get-tuple-element.93.pre.refs_1_) | copy-start | bytes 3145732
  147.4 5.4 %collective-permute-start.12 = (bf16[32,32,128]{2,1,0:T(8,128)(2,1)S(1)}, bf16[32,32,128]{2,1,0:T(8,128)(2,1)S(1)}, u32[]{:S(2)}, u32[]{:S(2)}) collective-permute-start(bf16[32,32,128]{2,1,0:T(8,128)(2,1)S(1)} %get-tuple-element.94), channel_id=1, source_target_pairs={{0,1},{1,2},{2,3},{4,5},{5,6},{6,7},{8,9},{9,10},{10,11},{12,13},{... | collective-permute-start | bytes 786440 | tf_op jit(solution)/shard_map/ppermute | solution.py:695
  149.5 9.2 %collective-permute-start.13 = (bf16[32,32,128]{2,1,0:T(8,128)(2,1)S(1)}, bf16[32,32,128]{2,1,0:T(8,128)(2,1)S(1)}, u32[]{:S(2)}, u32[]{:S(2)}) collective-permute-start(bf16[32,32,128]{2,1,0:T(8,128)(2,1)S(1)} %get-tuple-element.95), channel_id=1, source_target_pairs={{1,0},{2,1},{3,2},{5,4},{6,5},{7,6},{9,8},{10,9},{11,10},{13,12},{... | collective-permute-start | bytes 786440 | tf_op jit(solution)/shard_map/ppermute | solution.py:695
  161.1 12.6 %collective-permute-start.14 = (bf16[15,160,128]{2,1,0:T(8,128)(2,1)S(1)}, bf16[15,160,128]{2,1,0:T(8,128)(2,1)S(1)}, u32[]{:S(2)}, u32[]{:S(2)}) collective-permute-start(bf16[15,160,128]{2,1,0:T(8,128)(2,1)S(1)} %get-tuple-element.97), channel_id=1, source_target_pairs={{0,4},{4,8},{8,12},{12,16},{16,20},{20,24},{24,28},{28,32},{32,36}... | collective-permute-start | bytes 1843208 | tf_op jit(solution)/shard_map/ppermute | solution.py:695
  164.9 14.5 %collective-permute-start.15 = (bf16[15,160,128]{2,1,0:T(8,128)(2,1)S(1)}, bf16[15,160,128]{2,1,0:T(8,128)(2,1)S(1)}, u32[]{:S(2)}, u32[]{:S(2)}) collective-permute-start(bf16[15,160,128]{2,1,0:T(8,128)(2,1)S(1)} %get-tuple-element.98), channel_id=1, source_target_pairs={{4,0},{8,4},{12,8},{16,12},{20,16},{24,20},{28,24},{32,28},{36,32}... | collective-permute-start | bytes 1843208 | tf_op jit(solution)/shard_map/ppermute | solution.py:695
  (10 other events, 13.0 us)

commit v3 on v2

v3 whole, which is shorter than its diff:
```python
import functools

import jax
import jax.numpy as jnp
from jax import lax
from jax.experimental import pallas as pl
from jax.experimental.pallas import tpu as pltpu
from jax.sharding import PartitionSpec as P

STRIDE = 8
F32 = jnp.float32
BF = jnp.bfloat16
C0 = 0.7978845608028654
C1 = 0.7978845608028654 * 0.044715

ROWS, COLS, CH = 32, 128, 128
RH, CHALO = 15, 16
WIDE = COLS + 2 * CHALO
PAD = 8

HALO = (14, 12, 8, 0)
SIDES = (32, 16)
SPANS = (
    ((0, 192), (0, 192), (8, 184), (16, 176)),
    ((0, 160), (0, 160), (8, 152), (16, 144)),
)
DHALO = (2, 3, 8, 0)
DSIDE = (16, 16, 8, 0)

VMEM = pl.BlockSpec(memory_space=pltpu.VMEM)
SMEM = pl.BlockSpec(memory_space=pltpu.SMEM)
ANY = pl.BlockSpec(memory_space=pl.ANY)


def sds(shape, dtype):
    return jax.ShapeDtypeStruct(shape, dtype)


def gelu_parts(half, want_slope):
    square = half * half
    t = jnp.tanh(half * (BF(2 * C0) + BF(8 * C1) * square))
    half_t = half * t
    hidden = half + half_t
    if not want_slope:
        return hidden, None
    slope = (BF(0.5) + BF(0.5) * t) + (half - half_t * t) * (BF(C0) + BF(12 * C1) * square)
    return hidden, slope


def rows_of(kernel, scale):
    return [jnp.broadcast_to(kernel[t : t + 1, :] * scale, (8, CH))[None] for t in range(9)]


def tap_sum(src, row, col, width, dilate, sign, taps, which, start=None):
    total = start
    for i in which:
        for j in (-1, 0, 1):
            at = col + sign * j * dilate
            piece = src[row + sign * i * dilate, at : at + width, :].reshape(width // 8, 8, CH)
            piece = piece * taps[(i + 1) * 3 + j + 1]
            total = piece if total is None else total + piece
    return total


def chunks(low, high, size):
    out = []
    while low < high:
        out.append((low, min(size, high - low)))
        low += size
    return out


def grad_of(hidden, upstream):
    return lax.dot_general(
        hidden.reshape(-1, CH),
        upstream.reshape(-1, CH),
        (((0,), (0,)), ((), ())),
        preferred_element_type=F32,
    )


INNER = (0, 2, 6)
DSKIP = (4, 3, 0)


def act_rows(src, taps, seg, layer, r, number, want_slope, h_buf, h_at, slope_buf, slope_at, hid_own):
    low, high = SPANS[seg][layer]
    first = SIDES[seg] - DSIDE[layer] - low
    for q in range(number):
        parts = []
        for c, width in chunks(low, high, 32):
            half = tap_sum(src, RH + r + q, PAD + c, width, 2**layer, 1, taps, (-1, 0, 1))
            parts.append(gelu_parts(half.reshape(width, CH).astype(BF), want_slope))
        hidden = jnp.concatenate([p[0] for p in parts], 0)
        h_buf[h_at + q] = hidden
        if hid_own is not None:
            own = hidden.astype(F32)[SIDES[seg] - low : SIDES[seg] - low + COLS]
            hid_own[h_at + q] = own.astype(BF)
        if want_slope:
            slope = jnp.concatenate([p[1] for p in parts], 0)
            slope_buf[slope_at + q] = slope[first : first + COLS + 2 * DSIDE[layer]]


def mixed_rows(h_buf, h_at, src, r, step, seg, layer, weights):
    low, high = SPANS[seg][layer]
    mixed = jnp.dot(
        h_buf[pl.ds(h_at, step)].reshape(step * (high - low), CH),
        weights[layer],
        preferred_element_type=F32,
    ).reshape(step, high - low, CH)
    return src[pl.ds(RH + r, step), PAD + low : PAD + high] + mixed


def fill_row(buf, row, at, pieces, r):
    for piece in pieces:
        width = piece.shape[1]
        buf[row, at : at + width] = piece[r].astype(F32)
        at += width


def clear_columns(ref, edges, seg):
    side = SIDES[seg]
    count = ref.shape[0]

    @pl.when(edges[2] == 1)
    def _():
        ref[:, PAD : PAD + side] = jnp.zeros((count, side, CH), F32)

    @pl.when(edges[3] == 1)
    def _():
        ref[:, PAD + side + COLS : PAD + 2 * side + COLS] = jnp.zeros((count, side, CH), F32)


def clear_rows(ref, edges, number):
    count, breadth = ref.shape[0], ref.shape[1]

    @pl.when(edges[0] == 1)
    def _():
        ref[0:number] = jnp.zeros((number, breadth, CH), F32)

    @pl.when(edges[1] == 1)
    def _():
        ref[count - number : count] = jnp.zeros((number, breadth, CH), F32)


def inner_kernel(seg, *refs):
    refs = list(refs)
    take = lambda n: [refs.pop(0) for _ in range(n)]
    edges = take(1)[0]
    pieces = take(1 if seg else 3)
    kernels, weights = take(2)
    hid_out, slope_out, x_out = take(3), take(3), take(3)
    x_bufs, h_bufs, slopes = take(4), take(3), take(3)
    hid_two, sem = take(2)

    def build(r, _):
        fill_row(x_bufs[0], RH + r, PAD, pieces, r)
        return 0

    lax.fori_loop(0, ROWS, build, 0)
    copies = []

    def send(src, dst, slot):
        copies.append(pltpu.make_async_copy(src, dst, sem.at[slot]))
        copies[-1].start()

    for layer in range(3):
        src, dst = x_bufs[layer], x_bufs[layer + 1]
        h_buf, slope_buf = h_bufs[layer], slopes[layer]
        low, high = SPANS[seg][layer]
        edge = INNER[layer]
        first, number = edge + 1, ROWS - 2 - 2 * edge
        taps = rows_of(kernels[layer], 0.5)
        hid_own = hid_two if layer == 2 else None

        def body(it, _):
            act_rows(
                src, taps, seg, layer, first + 2 * it, 2, True,
                h_buf, 2 * it, slope_buf, 2 * it, hid_own,
            )
            return 0

        lax.fori_loop(0, number // 2, body, 0)
        rows = pl.ds(first, number)
        hid_src = hid_two if layer == 2 else h_buf.at[:, pl.ds(SIDES[seg] - low, COLS)]
        send(hid_src, hid_out[layer].at[rows], layer)
        send(slope_buf, slope_out[layer].at[pl.ds(DHALO[layer] + first, number)], 3 + layer)

        step = (15, 13, 9)[layer]

        def mix_body(it, _):
            at = it * step
            dst[pl.ds(RH + first + at, step), PAD + low : PAD + high] = mixed_rows(
                h_buf, at, src, first + at, step, seg, layer, weights
            )
            return 0

        lax.fori_loop(0, number // step, mix_body, 0)
        clear_columns(dst, edges, seg)
        depth = (4, 8, 18)[layer]
        send(dst.at[pl.ds(RH + first, depth)], x_out[layer].at[pl.ds(0, depth)], 6 + layer)
        if layer < 2:
            send(
                dst.at[pl.ds(RH + first + number - depth, depth)],
                x_out[layer].at[pl.ds(depth, depth)],
                9 + layer,
            )
    for copy in copies:
        copy.wait()


SLOPE_SHAPES = [(ROWS + 2 * DHALO[k], COLS + 2 * DSIDE[k], CH) for k in range(4)]


def x_wide(seg):
    return COLS + 2 * SIDES[seg] + 2 * PAD


def inner(seg, edges, pieces, kernels, weights):
    outs = [sds((ROWS, COLS, CH), BF)] * 3
    outs += [sds(s, BF) for s in SLOPE_SHAPES[:3]]
    outs += [sds((n, x_wide(seg), CH), F32) for n in (8, 16, 18)]
    numbers = [ROWS - 2 - 2 * e for e in INNER]
    breadth = [b - a for a, b in SPANS[seg]]
    scratch = [pltpu.VMEM((ROWS + 2 * RH, x_wide(seg), CH), F32)] * 4
    scratch += [pltpu.VMEM((numbers[k], breadth[k], CH), BF) for k in range(3)]
    scratch += [pltpu.VMEM((numbers[k], SLOPE_SHAPES[k][1], CH), BF) for k in range(3)]
    scratch += [pltpu.VMEM((numbers[2], COLS, CH), BF), pltpu.SemaphoreType.DMA((11,))]
    return pl.pallas_call(
        functools.partial(inner_kernel, seg),
        out_shape=outs,
        in_specs=[SMEM] + [VMEM] * (2 + len(pieces)),
        out_specs=[ANY] * 9,
        scratch_shapes=scratch,
        compiler_params=pltpu.CompilerParams(vmem_limit_bytes=52 * 2**20),
        cost_estimate=pl.CostEstimate(
            flops=4 * 2 * 3000 * CH * CH, bytes_accessed=12 * 2**20, transcendentals=0
        ),
        name="inner_last" if seg else "inner_first",
    )(edges, *pieces, kernels, weights)


def outer_kernel(seg, *refs):
    refs = list(refs)
    take = lambda n: [refs.pop(0) for _ in range(n)]
    edges = take(1)[0]
    pieces = take(1 if seg else 3)
    top, bottom, kernels, weights = take(4)
    if seg:
        coarse, cot, back_weight = take(3)
    x_in = take(3)
    take(6)
    if seg:
        out, pre, strip_left, strip_right, grad = take(5)
    else:
        x_out, hid_three, slope_three = take(3)
    hid_out, slope_out = take(3), take(3)
    x_bufs, h_bufs, slopes = take(4), take(4), take(4)
    hid_two, own_buf, sem = take(3)
    side = SIDES[seg]

    loads = []
    for layer in range(3):
        first = INNER[layer] + 1
        depth = (4, 8, 18)[layer]
        spots = [(first, 0)] if layer == 2 else [(first, 0), (ROWS - first - depth, depth)]
        for k, (r, at) in enumerate(spots):
            copy = pltpu.make_async_copy(
                x_in[layer].at[pl.ds(at, depth)],
                x_bufs[layer + 1].at[pl.ds(RH + r, depth)],
                sem.at[20 + 2 * layer + k],
            )
            copy.start()
            loads.append((layer, copy))

    for r in (0, 1, ROWS - 2, ROWS - 1):
        fill_row(x_bufs[0], RH + r, PAD, pieces, r)

    def build_ends(r, _):
        fill_row(x_bufs[0], r, PAD, [top], r)
        fill_row(x_bufs[0], RH + ROWS + r, PAD, [bottom], r)
        return 0

    lax.fori_loop(0, RH, build_ends, 0)
    copies = []

    def send(src, dst, slot):
        copies.append(pltpu.make_async_copy(src, dst, sem.at[slot]))
        copies[-1].start()

    for layer in range(3):
        src, dst = x_bufs[layer], x_bufs[layer + 1]
        h_buf, slope_buf = h_bufs[layer], slopes[layer]
        halo, edge, dhalo = HALO[layer], INNER[layer], DHALO[layer]
        low, high = SPANS[seg][layer]
        taps = rows_of(kernels[layer], 0.5)
        hid_own = hid_two if layer == 2 else None
        skip = DSKIP[layer]
        kept = 5 - skip

        if skip:

            def far_body(it, _):
                low_side = it >= skip
                at = jnp.where(low_side, 15 + 3 * kept + 3 * (it - skip), 3 * it)
                r = jnp.where(low_side, ROWS - 1 - edge - 15, -halo) + at
                act_rows(src, taps, seg, layer, r, 3, False, h_buf, at, None, 0, None)
                return 0

            lax.fori_loop(0, 2 * skip, far_body, 0)

        def near_body(it, _):
            low_side = it >= kept
            at = jnp.where(low_side, 15 + 3 * (it - kept), 3 * skip + 3 * it)
            r = jnp.where(low_side, ROWS - 1 - edge - 15, -halo) + at
            act_rows(src, taps, seg, layer, r, 3, True, h_buf, at, slope_buf, 3 * it, hid_own)
            return 0

        lax.fori_loop(0, 2 * kept, near_body, 0)

        whole = hid_two if layer == 2 else h_buf
        cols = pl.ds(0, COLS) if layer == 2 else pl.ds(side - low, COLS)
        send(whole.at[pl.ds(halo, edge + 1), cols], hid_out[layer].at[pl.ds(0, edge + 1)], layer)
        send(
            whole.at[pl.ds(15, edge + 1), cols],
            hid_out[layer].at[pl.ds(ROWS - 1 - edge, edge + 1)],
            3 + layer,
        )
        number = 3 * kept
        send(slope_buf.at[pl.ds(0, number)], slope_out[layer].at[pl.ds(0, number)], 6 + layer)
        send(
            slope_buf.at[pl.ds(number, number)],
            slope_out[layer].at[pl.ds(dhalo + ROWS - 1 - edge, number)],
            9 + layer,
        )
        for which, copy in loads:
            if which == layer:
                copy.wait()

        def mix_body(it, _):
            r = jnp.where(it == 0, -halo, ROWS - 1 - edge)
            dst[pl.ds(RH + r, 15), PAD + low : PAD + high] = mixed_rows(
                h_buf, 15 * it, src, r, 15, seg, layer, weights
            )
            return 0

        lax.fori_loop(0, 2, mix_body, 0)
        clear_rows(dst, edges, RH)
        clear_columns(dst, edges, seg)

    taps = rows_of(kernels[3], 0.5)

    def last_body(it, _):
        act_rows(
            x_bufs[3], taps, seg, 3, 4 * it, 4, True, h_bufs[3], 4 * it, slopes[3], 4 * it, None
        )
        return 0

    lax.fori_loop(0, ROWS // 4, last_body, 0)
    if not seg:
        send(h_bufs[3].at[:, pl.ds(CHALO, COLS)], hid_three, 12)
        send(slopes[3], slope_three, 13)

    def last_mix(it, _):
        at = 16 * it
        value = mixed_rows(h_bufs[3], at, x_bufs[3], at, 16, seg, 3, weights)
        if seg:
            for q in range(2):
                extra = coarse[2 * it + q][:, None, :]
                part = value[q * STRIDE : (q + 1) * STRIDE].reshape(STRIDE, -1, STRIDE, CH)
                part = (part + extra[None]).reshape(STRIDE, COLS, CH)
                own_buf[pl.ds(at + q * STRIDE, STRIDE)] = part.astype(BF)
        else:
            own_buf[pl.ds(at, 16)] = value.astype(BF)
        return 0

    lax.fori_loop(0, 2, last_mix, 0)
    if seg:
        send(own_buf, out, 14)
        total = jnp.zeros((CH, CH), F32)
        edge_cols = []
        for b in range(2):
            rows = slice(16 * b, 16 * b + 16)
            up = cot[rows]
            total = total + grad_of(h_bufs[3][rows], up)
            pulled = jnp.dot(up.reshape(-1, CH), back_weight[...], preferred_element_type=F32)
            value = pulled.reshape(16, COLS, CH) * slopes[3][rows].astype(F32)
            value = value.astype(BF)
            pre[rows] = value
            strip_left[rows] = value[:, :CHALO]
            strip_right[rows] = value[:, COLS - CHALO :]
            edge_cols.append(up.astype(F32))
        pack_edges(strip_left, strip_right, edge_cols)
        grad[...] = total
    else:
        zeros = jnp.zeros((ROWS, CHALO, CH), BF)

        @pl.when(edges[2] == 1)
        def _():
            own_buf[:, 0:CHALO] = zeros

        @pl.when(edges[3] == 1)
        def _():
            own_buf[:, CHALO + COLS : WIDE] = zeros

        send(own_buf, x_out, 14)
    for copy in copies:
        copy.wait()


def pack_edges(strip_left, strip_right, halves):
    first, second = halves
    strip_left[ROWS : ROWS + 16] = jnp.concatenate([first[:, :8], second[:, :8]], 1).astype(BF)
    strip_right[ROWS : ROWS + 16] = jnp.concatenate(
        [first[:, COLS - 8 :], second[:, COLS - 8 :]], 1
    ).astype(BF)


def outer(seg, edges, pieces, top, bottom, kernels, weights, begun, extra=()):
    block = sds((ROWS, COLS, CH), BF)
    strip = sds((ROWS + 16, CHALO, CH), BF)
    if seg:
        outs = [block, block, strip, strip, sds((CH, CH), F32)]
        specs = [ANY] + [VMEM] * 4
    else:
        outs = [sds((ROWS, WIDE, CH), BF), block, block]
        specs = [ANY, ANY, ANY]
    shift = len(outs)
    outs = outs + [sds(a.shape, BF) for a in begun[:6]]
    specs = specs + [ANY] * 6
    args = (edges, *pieces, top, bottom, kernels, weights, *extra, *begun[6:], *begun[:6])
    breadth = [b - a for a, b in SPANS[seg]]
    scratch = [pltpu.VMEM((ROWS + 2 * RH, x_wide(seg), CH), F32)] * 4
    heights = [30, 30, 30, ROWS]
    scratch += [pltpu.VMEM((heights[k], breadth[k], CH), BF) for k in range(4)]
    tall = [6 * (5 - DSKIP[k]) for k in range(3)] + [ROWS]
    scratch += [pltpu.VMEM((tall[k], SLOPE_SHAPES[k][1], CH), BF) for k in range(4)]
    scratch += [pltpu.VMEM((30, COLS, CH), BF), pltpu.VMEM((ROWS, breadth[3], CH), BF)]
    scratch += [pltpu.SemaphoreType.DMA((26,))]
    return pl.pallas_call(
        functools.partial(outer_kernel, seg),
        out_shape=outs,
        in_specs=[SMEM] + [VMEM] * (len(args) - 10) + [ANY] * 9,
        out_specs=specs,
        scratch_shapes=scratch,
        input_output_aliases={len(args) - 6 + k: shift + k for k in range(6)},
        compiler_params=pltpu.CompilerParams(vmem_limit_bytes=52 * 2**20),
        cost_estimate=pl.CostEstimate(
            flops=4 * 2 * 5000 * CH * CH, bytes_accessed=12 * 2**20, transcendentals=0
        ),
        name="outer_last" if seg else "outer_first",
    )(*args)


def pool_kernel(feature, cot, weight, weight_t, coarse, back, grad):
    total = None
    for b in range(ROWS // STRIDE):
        rows = slice(STRIDE * b, STRIDE * (b + 1))

        def block_sum(ref):
            value = ref[STRIDE * b].astype(F32)
            for r in range(1, STRIDE):
                value = value + ref[STRIDE * b + r].astype(F32)
            return value.reshape(COLS // STRIDE, STRIDE, CH).sum(axis=1)

        pooled = (block_sum(feature) * (1.0 / (STRIDE * STRIDE))).astype(BF)
        block_cot = block_sum(cot).astype(BF)
        coarse[b] = jnp.dot(pooled, weight[...], preferred_element_type=F32)
        back[b] = jnp.dot(block_cot, weight_t[...], preferred_element_type=F32) * (
            1.0 / (STRIDE * STRIDE)
        )
        part = grad_of(pooled, block_cot)
        total = part if total is None else total + part
    grad[...] = total


def pool(feature, cot, weight):
    small = sds((ROWS // STRIDE, COLS // STRIDE, CH), F32)
    return pl.pallas_call(
        pool_kernel,
        out_shape=[small, small, sds((CH, CH), F32)],
        in_specs=[VMEM] * 4,
        out_specs=[VMEM] * 3,
        compiler_params=pltpu.CompilerParams(vmem_limit_bytes=16 * 2**20),
        cost_estimate=pl.CostEstimate(flops=10**8, bytes_accessed=2 * 2**20, transcendentals=0),
        name="pool",
    )(feature, cot, weight, weight.T)


BASE = 8


def fill_pre(buf, row, pre, from_left, from_right, r):
    buf[row, 0:16] = from_left[r].astype(F32)
    buf[row, 16:144] = pre[r].astype(F32)
    buf[row, 144:160] = from_right[r].astype(F32)


def base_row(base, from_left, from_right, r, half):
    side = slice(8 * half, 8 * half + 8)
    return jnp.concatenate(
        [
            from_left[ROWS + r].astype(F32)[side],
            base[r + 16 * half].astype(F32),
            from_right[ROWS + r].astype(F32)[side],
        ],
        0,
    )


def row_taps(buf, r, taps, which, low=8, high=152):
    parts = []
    for c, width in chunks(low, high, 32):
        parts.append(tap_sum(buf, r, c, width, 8, -1, taps, which).reshape(width, CH))
    return jnp.concatenate(parts, 0)


def ends_kernel(pre, from_left, from_right, base, kernel, up, down, buf):
    taps = rows_of(kernel, 1.0)

    def build(r, _):
        fill_pre(buf, r, pre, from_left, from_right, r)
        fill_pre(buf, 16 + r, pre, from_left, from_right, 16 + r)
        return 0

    lax.fori_loop(0, 16, build, 0)
    zeros = jnp.zeros((8, CH), F32)

    def one(r, half, which):
        value = row_taps(buf, r + 16 * half, taps, which)
        value = value + base_row(base, from_left, from_right, r, half)
        return jnp.concatenate([zeros, value, zeros], 0).astype(BF)

    def body(r, _):
        up[r] = one(r, 0, (-1, 0))
        down[r] = one(ROWS - 23 + r, 1, (0, 1))
        return 0

    lax.fori_loop(0, 7, body, 0)

    def body_pre(r, _):
        up[7 + r] = buf[r].astype(BF)
        down[7 + r] = buf[ROWS - 8 + r].astype(BF)
        return 0

    lax.fori_loop(0, 8, body_pre, 0)


def ends(pre, from_left, from_right, base, kernel):
    strip = sds((RH, WIDE, CH), BF)
    return pl.pallas_call(
        ends_kernel,
        out_shape=[strip, strip],
        in_specs=[VMEM] * 5,
        out_specs=[VMEM] * 2,
        scratch_shapes=[pltpu.VMEM((ROWS, WIDE, CH), F32)],
        compiler_params=pltpu.CompilerParams(vmem_limit_bytes=20 * 2**20),
        cost_estimate=pl.CostEstimate(flops=10**8, bytes_accessed=6 * 2**20, transcendentals=0),
        name="ends",
    )(pre, from_left, from_right, base, kernel)


def own_kernel(pre, from_left, from_right, base, kernel, out, buf):
    taps = rows_of(kernel, 1.0)

    def build(r, _):
        fill_pre(buf, r, pre, from_left, from_right, r)
        fill_pre(buf, 16 + r, pre, from_left, from_right, 16 + r)
        return 0

    lax.fori_loop(0, 16, build, 0)

    def one(r, half, which):
        value = row_taps(buf, r + 16 * half, taps, which)
        out[r + 16 * half] = value + base_row(base, from_left, from_right, r, half)

    def body_edge(r, _):
        one(r, 0, (-1, 0))
        one(r + 8, 1, (0, 1))
        return 0

    def body_middle(r, _):
        one(r + 8, 0, (-1, 0, 1))
        one(r, 1, (-1, 0, 1))
        return 0

    lax.fori_loop(0, 8, body_edge, 0)
    lax.fori_loop(0, 8, body_middle, 0)


def own_part(pre, from_left, from_right, base, kernel):
    return pl.pallas_call(
        own_kernel,
        out_shape=sds((ROWS, UWIDE, CH), F32),
        in_specs=[VMEM] * 5,
        out_specs=VMEM,
        scratch_shapes=[pltpu.VMEM((ROWS, WIDE, CH), F32)],
        compiler_params=pltpu.CompilerParams(vmem_limit_bytes=20 * 2**20),
        cost_estimate=pl.CostEstimate(
            flops=2 * 10**9, bytes_accessed=6 * 2**20, transcendentals=0
        ),
        name="own_part",
    )(pre, from_left, from_right, base, kernel)


UHALO = 7
UWIDE = COLS + 16


def backward_kernel(last, *refs):
    refs = list(refs)
    take = lambda n: [refs.pop(0) for _ in range(n)]
    edges, pre, from_left, from_right, top, bottom = take(6)
    kernels, weights_t = take(2)
    count = 3 if last else 4
    if last:
        back = take(1)[0]
    part_in = take(1)[0]
    slope_in = take(count)
    hid_in = take(count)
    if last:
        out, grads = take(2)
    else:
        up_out, pre_out, strip_left, strip_right, grads = take(5)
    buf, ups = take(2)
    slopes = take(count)
    hids = take(count)
    sem = take(1)[0]

    copies = []
    for k in range(count):
        copies.append(
            (
                pltpu.make_async_copy(slope_in[k], slopes[k], sem.at[2 * k]),
                pltpu.make_async_copy(hid_in[k], hids[k], sem.at[2 * k + 1]),
            )
        )
        copies[-1][0].start()
        copies[-1][1].start()

    part_copy = pltpu.make_async_copy(
        part_in, ups.at[pl.ds(UHALO, ROWS)], sem.at[2 * count]
    )
    part_copy.start()

    def build(r, _):
        fill_pre(buf, BASE + r, pre, from_left, from_right, r)
        fill_pre(buf, BASE + 24 + r, pre, from_left, from_right, 24 + r)
        return 0

    lax.fori_loop(0, 8, build, 0)

    def build_pre(r, _):
        buf[r] = top[7 + r].astype(F32)
        buf[BASE + ROWS + r] = bottom[7 + r].astype(F32)
        return 0

    lax.fori_loop(0, 8, build_pre, 0)

    def build_ups(r, _):
        ups[r] = top[r].astype(F32)[8:152]
        ups[UHALO + ROWS + r] = bottom[r].astype(F32)[8:152]
        return 0

    lax.fori_loop(0, 7, build_ups, 0)

    def add_taps(r, low, high, dilate, taps, which, extra=None):
        for c, width in chunks(low, high, 32):
            start = ups[UHALO + r, c - 8 : c - 8 + width].reshape(width // 8, 8, CH)
            total = tap_sum(buf, BASE + r, c, width, dilate, -1, taps, which, start)
            if extra is not None:
                total = total + extra[(c - low) // 8 : (c - low + width) // 8][:, None, :]
                out[r, c - low : c - low + width] = total.reshape(width, CH).astype(BF)
            else:
                ups[UHALO + r, c - 8 : c - 8 + width] = total.reshape(width, CH)

    taps = rows_of(kernels[3], 1.0)

    part_copy.wait()

    def first_upper(r, _):
        add_taps(r, 8, 152, 8, taps, (1,))
        add_taps(24 + r, 8, 152, 8, taps, (-1,))
        return 0

    lax.fori_loop(0, 8, first_upper, 0)

    def first_ends(r, _):
        add_taps(r - 7, 8, 152, 8, taps, (-1,))
        add_taps(ROWS + r, 8, 152, 8, taps, (1,))
        return 0

    lax.fori_loop(0, 7, first_ends, 0)

    for k, layer in enumerate((2, 1, 0)):
        dilate = 2**layer
        halo = (1, 3, 7)[layer]
        copies[k][0].wait()
        copies[k][1].wait()
        step = (ROWS + 2 * halo) // 2
        skip = DHALO[layer] - halo

        def pull_body(it, _):
            at = it * step
            up = ups[pl.ds(UHALO - halo + at, step)].astype(BF)
            pulled = jnp.dot(
                up.reshape(step * UWIDE, CH), weights_t[layer], preferred_element_type=F32
            ).reshape(step, UWIDE, CH)
            slope = slopes[k][pl.ds(skip + at, step)].astype(F32)
            slope = slope[:, DSIDE[layer] - 8 : DSIDE[layer] - 8 + UWIDE]
            buf[pl.ds(BASE - halo + at, step), 8:152] = pulled * slope
            return 0

        lax.fori_loop(0, 2, pull_body, 0)
        clear_rows(buf, edges, 8)
        zeros = jnp.zeros((ROWS + 16, CHALO, CH), F32)

        @pl.when(edges[2] == 1)
        def _():
            buf[:, 0:CHALO] = zeros

        @pl.when(edges[3] == 1)
        def _():
            buf[:, CHALO + COLS : WIDE] = zeros

        total = jnp.zeros((CH, CH), F32)
        for b in range(2):
            up = ups[UHALO + 16 * b : UHALO + 16 * b + 16, 8:136].astype(BF)
            total = total + grad_of(hids[k][16 * b : 16 * b + 16], up)
        grads[k] = total

        taps = rows_of(kernels[layer], 1.0)
        reach = (0, 1, 3)[layer]
        low, high = ((16, 144), (8, 152), (8, 152))[layer]

        def tap_body(it, _):
            for q in range(2):
                r = 2 * it + q - reach
                if last and layer == 0:
                    add_taps(r, low, high, dilate, taps, (-1, 0, 1), back[r // STRIDE])
                else:
                    add_taps(r, low, high, dilate, taps, (-1, 0, 1))
            return 0

        if layer == 1:
            lax.fori_loop(0, (ROWS + 2) // 2, tap_body, 0)
        else:
            lax.fori_loop(0, (ROWS + 2 * reach) // 2, tap_body, 0)

    if not last:
        copies[3][0].wait()
        copies[3][1].wait()
        total = jnp.zeros((CH, CH), F32)
        edge_cols = []
        for b in range(2):
            rows = slice(16 * b, 16 * b + 16)
            value = ups[UHALO + 16 * b : UHALO + 16 * b + 16, 8:136]
            up_out[rows] = value
            up = value.astype(BF)
            total = total + grad_of(hids[3][rows], up)
            pulled = jnp.dot(up.reshape(-1, CH), weights_t[3], preferred_element_type=F32)
            value = (pulled.reshape(16, COLS, CH) * slopes[3][rows].astype(F32)).astype(BF)
            pre_out[rows] = value
            strip_left[rows] = value[:, :CHALO]
            strip_right[rows] = value[:, COLS - CHALO :]
            edge_cols.append(ups[UHALO + 16 * b : UHALO + 16 * b + 16, 8:136])
        pack_edges(strip_left, strip_right, edge_cols)
        grads[3] = total


def backward(last, edges, pre, sides, part, ends_in, kernels, weights_t, slopes, hids, back=()):
    count = len(slopes)
    block = sds((ROWS, COLS, CH), BF)
    if last:
        outs = [block, sds((count, CH, CH), F32)]
    else:
        strip = sds((ROWS + 16, CHALO, CH), BF)
        outs = [sds((ROWS, COLS, CH), F32), block, strip, strip, sds((count, CH, CH), F32)]
    scratch = [
        pltpu.VMEM((ROWS + 16, WIDE, CH), F32),
        pltpu.VMEM((ROWS + 2 * UHALO, UWIDE, CH), F32),
    ]
    scratch += [pltpu.VMEM(a.shape, BF) for a in slopes]
    scratch += [pltpu.VMEM(a.shape, BF) for a in hids]
    scratch += [pltpu.SemaphoreType.DMA((2 * count + 1,))]
    args = (edges, pre, *sides, *ends_in, kernels, weights_t, *back)
    return pl.pallas_call(
        functools.partial(backward_kernel, last),
        out_shape=outs,
        in_specs=[SMEM] + [VMEM] * (len(args) - 1) + [ANY] * (1 + 2 * count),
        out_specs=[VMEM] * len(outs),
        scratch_shapes=scratch,
        compiler_params=pltpu.CompilerParams(vmem_limit_bytes=30 * 2**20),
        cost_estimate=pl.CostEstimate(
            flops=7 * 2 * 5000 * CH * CH, bytes_accessed=14 * 2**20, transcendentals=0
        ),
        name="backward_last" if last else "backward_first",
    )(*args, part, *slopes, *hids)


def exchange(to_before, to_after, axis):
    ends_at = lax.axis_size(axis) - 1
    forth = [(i, i + 1) for i in range(ends_at)]
    back = [(i + 1, i) for i in range(ends_at)]
    return lax.ppermute(to_after, axis, forth), lax.ppermute(to_before, axis, back)


def local(features_in, cotangent, depth_kernels, point_weights, coarse_weight):
    row, col = lax.axis_index("rows"), lax.axis_index("cols")
    row_end, col_end = lax.axis_size("rows") - 1, lax.axis_size("cols") - 1
    edges = jnp.stack([row == 0, row == row_end, col == 0, col == col_end]).astype(jnp.int32)
    kernels = depth_kernels.astype(F32)
    weights_t = jnp.swapaxes(point_weights, 1, 2)

    left, right = exchange(
        features_in[:, : SIDES[0]], features_in[:, COLS - SIDES[0] :], "cols"
    )
    wide = lambda rows: jnp.concatenate([left[rows], features_in[rows], right[rows]], axis=1)
    top, bottom = exchange(wide(slice(0, RH)), wide(slice(ROWS - RH, ROWS)), "rows")
    coarse, back, coarse_grad = pool(features_in, cotangent, coarse_weight)
    pieces = (left, features_in, right)
    begun = inner(0, edges, pieces, kernels[:3], point_weights[:3])
    x_mid, hid_three, slope_three, *kept = outer(
        0, edges, pieces, top, bottom, kernels[:4], point_weights[:4], begun
    )
    hid_low, slope_low = kept[:3] + [hid_three], kept[3:] + [slope_three]
    top, bottom = exchange(x_mid[:RH], x_mid[ROWS - RH :], "rows")
    begun = inner(1, edges, (x_mid,), kernels[4:7], point_weights[4:7])
    output, pre, strip_left, strip_right, grad_top, *kept = outer(
        1, edges, (x_mid,), top, bottom, kernels[4:], point_weights[4:], begun,
        (coarse, cotangent, weights_t[7]),
    )
    hid_high, slope_high = kept[:3], kept[3:]

    order = lambda things: [things[2], things[1], things[0]]
    sides = exchange(strip_left, strip_right, "cols")
    rows_in = exchange(*ends(pre, *sides, cotangent, kernels[7]), "rows")
    part = own_part(pre, *sides, cotangent, kernels[7])
    upstream, pre, strip_left, strip_right, grad_mid = backward(
        False, edges, pre, sides, part, rows_in,
        kernels[4:], jnp.concatenate([weights_t[4:7], weights_t[3:4]]),
        order(slope_high) + [slope_low[3]], order(hid_high) + [hid_low[3]],
    )
    sides = exchange(strip_left, strip_right, "cols")
    rows_in = exchange(*ends(pre, *sides, upstream, kernels[3]), "rows")
    part = own_part(pre, *sides, upstream, kernels[3])
    input_grad, grad_low = backward(
        True, edges, pre, sides, part, rows_in,
        kernels[:4], weights_t[:3], order(slope_low), order(hid_low), (back,),
    )

    grads = [grad_low[2], grad_low[1], grad_low[0], grad_mid[3], grad_mid[2], grad_mid[1]]
    grads = jnp.stack(grads + [grad_mid[0], grad_top, coarse_grad]).astype(BF)
    shares = lax.all_to_all(grads, "rows", 1, 0, tiled=True)
    summed = shares.reshape(-1, grads.shape[0], CH * 4).astype(F32).sum(axis=0)
    parts = lax.all_gather(summed.astype(BF), "cols", axis=0, tiled=False)
    weight_grads = parts.astype(F32).sum(axis=0).reshape(grads.shape[0], 4, CH)
    return (output, input_grad, weight_grads)


def solution(mesh):
    in_specs = (P("rows", "cols", None), P("rows", "cols", None), P(), P(), P())
    out_specs = (P("rows", "cols", None), P("rows", "cols", None), P(None, "rows", None))
    return jax.shard_map(local, mesh=mesh, in_specs=in_specs, out_specs=out_specs, check_vma=False)
```

time: 228 us -> 212 us (0.930)
  waiting for transfers between devices: 47.5 us -> 36.8 us
  blocking collectives: 30.6 us -> 27.9 us
    ppermute x8 -> x7, waiting for transfers between devices: 30.6 us -> 22.9 us  [exchange(): lax.ppermute(to_before, axis, back)]
    pallas_call x2, Pallas kernels: 31.2 us -> 27 us  [backward(): pl.pallas_call(functools.partial(backward_kernel, last), out_shape=outs,...]
    pallas_call x6 -> x8, Pallas kernels: 56 us -> 59.2 us  [the longest x2 31.7 us: outer(): pl.pallas_call(functools.partial(outer_kernel, seg), out_shape=outs, in_s...]
    ppermute x8 -> x7, waiting for transfers between devices: 16.9 us -> 13.8 us  [exchange(): lax.ppermute(to_after, axis, forth)]
    slice x13 -> x7, local copies, waits for them, and re-layouts: 3.27 us -> 5.11 us  [the longest x1 2.54 us: local(): top, bottom = exchange(x_mid[:RH], x_mid[ROWS - RH:], 'rows')]
    ppermute x8 -> x7, starting transfers between devices: 14.1 us -> 12.8 us  [exchange(): lax.ppermute(to_before, axis, back)]
    unnamed x45 -> x77, local copies, waits for them, and re-layouts: 9.2 us -> 8.75 us
    ppermute x8 -> x7, starting transfers between devices: 29.8 us -> 29.5 us  [exchange(): lax.ppermute(to_after, axis, forth)]
  transfers between devices with their start and end apart: 16 -> 14, of which waited for: 10 -> 10; matrix products, arithmetic and copies ran while one was open for 3% -> 2% of each run, Pallas kernels for 10% -> 13%
where the time goes in v3:
time: 212 us; the launch traced here: 211 us
  Pallas kernels  86.8 us (41%)
  starting transfers between devices  42.3 us (20%)
  waiting for transfers between devices  36.8 us (17%)
  blocking collectives  27.9 us (13%)
  local copies, waits for them, and re-layouts  15.5 us (7%)
    pallas_call x2, Pallas kernels, outer(): pl.pallas_call(functools.partial(outer_kernel, seg), out_shape=outs, in_s...  31.7 us
    ppermute x7, starting transfers between devices, exchange(): lax.ppermute(to_after, axis, forth)  29.5 us
    pallas_call x2, Pallas kernels, backward(): pl.pallas_call(functools.partial(backward_kernel, last), out_shape=outs,...  27 us
    ppermute x7, waiting for transfers between devices, exchange(): lax.ppermute(to_before, axis, back)  22.9 us
    pallas_call x2, Pallas kernels, inner(): pl.pallas_call(functools.partial(inner_kernel, seg), out_shape=outs, in_s...  22.8 us
    all_to_all x1, blocking collectives, local(): shares = lax.all_to_all(grads, 'rows', 1, 0, tiled=True)  21.7 us
    ppermute x7, waiting for transfers between devices, exchange(): lax.ppermute(to_after, axis, forth)  13.8 us
    ppermute x7, starting transfers between devices, exchange(): lax.ppermute(to_before, axis, back)  12.8 us
  transfers between devices with their start and end apart: 14, of which 10 were waited for; matrix products, arithmetic and copies ran while one was open for 2% of the time, Pallas kernels for 13%

profile of v3, /device:TPU:1, one launch (start us, length us, event | category | flops | bytes accessed | tf_op | source)
XLA Modules:
  0.0 211.0 jit_solution(1354980081845089295)
XLA Ops:
  1.8 3.3 %collective-permute-start.1 = (bf16[32,32,128]{2,1,0:T(8,128)(2,1)S(1)}, bf16[32,32,128]{2,1,0:T(8,128)(2,1)S(1)}, u32[]{:S(2)}, u32[]{:S(2)}) collective-permute-start(bf16[32,32,128]{2,1,0:T(8,128)(2,1)S(1)} %get-tuple-element.111), channel_id=1, source_target_pairs={{1,0},{2,1},{3,2},{5,4},{6,5},{7,6},{9,8},{10,9},{11,10},{13,12},{... | collective-permute-start | bytes 786440 | tf_op jit(solution)/shard_map/ppermute | solution.py:805
  5.2 4.6 %collective-permute-start = (bf16[32,32,128]{2,1,0:T(8,128)(2,1)S(1)}, bf16[32,32,128]{2,1,0:T(8,128)(2,1)S(1)}, u32[]{:S(2)}, u32[]{:S(2)}) collective-permute-start(bf16[32,32,128]{2,1,0:T(8,128)(2,1)S(1)} %get-tuple-element.112), channel_id=1, source_target_pairs={{0,1},{1,2},{2,3},{4,5},{5,6},{6,7},{8,9},{9,10},{10,11},{12,13},{... | collective-permute-start | bytes 786440 | tf_op jit(solution)/shard_map/ppermute | solution.py:805
  13.2 3.6 %collective-permute-start.2 = (bf16[15,192,128]{2,1,0:T(8,128)(2,1)S(1)}, bf16[15,192,128]{2,1,0:T(8,128)(2,1)S(1)}, u32[]{:S(2)}, u32[]{:S(2)}) collective-permute-start(bf16[15,192,128]{2,1,0:T(8,128)(2,1)S(1)} %pad_maximum_fusion), channel_id=1, source_target_pairs={{0,4},{4,8},{8,12},{12,16},{16,20},{20,24},{24,28},{28,32},{32,36}... | collective-permute-start | bytes 2211848 | tf_op jit(solution)/shard_map/ppermute | solution.py:805
  18.9 12.0 %inner_first.1 = (bf16[32,128,128]{2,1,0:T(8,128)(2,1)}, bf16[32,128,128]{2,1,0:T(8,128)(2,1)}, bf16[32,128,128]{2,1,0:T(8,128)(2,1)}, bf16[36,160,128]{2,1,0:T(...) custom-call(s32[4]{0:T(128)S(1)} %add_convert_fusion.refs_0_, ...), custom_call_target="tpu_custom_call" | custom-call | flops 393216000 | bytes 12582912 | tf_op jit(solution)/shard_map/inner_first/pallas_call | solution.py:229
  34.3 16.1 %outer_first.1 = (bf16[32,160,128]{2,1,0:T(8,128)(2,1)}, bf16[32,128,128]{2,1,0:T(8,128)(2,1)}, bf16[32,128,128]{2,1,0:T(8,128)(2,1)}, bf16[32,128,128]{2,1,0:T(...) custom-call(s32[4]{0:T(128)S(1)} %add_convert_fusion.refs_0_, ...), custom_call_target="tpu_custom_call", output_to_operand_aliasing={{3}: (11, {}), {4}: (12, {}), {5}: (13, {}), {6}: (14, {}),... | custom-call | flops 655360000 | bytes 12582912 | tf_op jit(solution)/shard_map/outer_first/pallas_call | solution.py:440
  50.5 2.5 %fusion = (bf16[15,160,128]{2,1,0:T(8,128)(2,1)}, bf16[15,160,128]{2,1,0:T(8,128)(2,1)}) fusion(bf16[32,160,128]{2,1,0:T(8,128)(2,1)} %get-tuple-element.64.refs_1_), kind=kLoop, calls=%fused_computation.18 | loop fusion | bytes 2457600 | tf_op jit(solution)/shard_map/slice | solution.py:827
  54.3 4.0 %collective-permute-start.4 = (bf16[15,160,128]{2,1,0:T(8,128)(2,1)}, bf16[15,160,128]{2,1,0:T(8,128)(2,1)S(1)}, u32[]{:S(2)}, u32[]{:S(2)}) collective-permute-start(bf16[15,160,128]{2,1,0:T(8,128)(2,1)} %get-tuple-element.108), channel_id=1, source_target_pairs={{0,4},{4,8},{8,12},{12,16},{16,20},{20,24},{24,28},{28,32},{32,36}... | collective-permute-start | bytes 1843208 | tf_op jit(solution)/shard_map/ppermute | solution.py:805
  62.6 10.8 %inner_last.1 = (bf16[32,128,128]{2,1,0:T(8,128)(2,1)S(1)}, bf16[32,128,128]{2,1,0:T(8,128)(2,1)}, bf16[32,128,128]{2,1,0:T(8,128)(2,1)}, bf16[36,160,128]{2,1,0...) custom-call(s32[4]{0:T(128)S(1)} %copy-done.28, ...), custom_call_target="tpu_custom_call" | custom-call | flops 393216000 | bytes 12582912 | tf_op jit(solution)/shard_map/inner_last/pallas_call | solution.py:229
  75.4 15.6 %outer_last.1 = (bf16[32,128,128]{2,1,0:T(8,128)(2,1)}, bf16[32,128,128]{2,1,0:T(8,128)(2,1)}, bf16[48,16,128]{2,1,0:T(8,128)(2,1)S(1)}, bf16[48,16,128]{2,1,0:T...) custom-call(s32[4]{0:T(128)S(1)} %copy-done.28, ...), custom_call_target="tpu_custom_call", output_to_operand_aliasing={{5}: (12, {}), {6}: (13, {}), {7}: (14, {}), {8}: (15, {}),... | custom-call | flops 655360000 | bytes 12582912 | tf_op jit(solution)/shard_map/outer_last/pallas_call | solution.py:440
  91.0 5.5 %collective-permute-start.6 = (bf16[48,16,128]{2,1,0:T(8,128)(2,1)S(1)}, bf16[48,16,128]{2,1,0:T(8,128)(2,1)S(1)}, u32[]{:S(2)}, u32[]{:S(2)}) collective-permute-start(bf16[48,16,128]{2,1,0:T(8,128)(2,1)S(1)} %get-tuple-element.77), channel_id=1, source_target_pairs={{0,1},{1,2},{2,3},{4,5},{5,6},{6,7},{8,9},{9,10},{10,11},{12,13},{... | collective-permute-start | bytes 589832 | tf_op jit(solution)/shard_map/ppermute | solution.py:805
  99.1 5.8 %collective-permute-done.7.from_right.refs_3_ = bf16[48,16,128]{2,1,0:T(8,128)(2,1)S(1)} collective-permute-done((bf16[48,16,128]{2,1,0:T(8,128)(2,1)S(1)}, bf16[48,16,128]{2,1,0:T(8,128)(2,1)S(1)}, u32[]{:S(2)}, u32[]{:S(2)}) %collective-permute-start.7) | collective-permute-done | bytes 196640 | tf_op jit(solution)/shard_map/ppermute | solution.py:805
  107.0 4.3 %collective-permute-start.8 = (bf16[15,160,128]{2,1,0:T(8,128)(2,1)S(1)}, bf16[15,160,128]{2,1,0:T(8,128)(2,1)S(1)}, u32[]{:S(2)}, u32[]{:S(2)}) collective-permute-start(bf16[15,160,128]{2,1,0:T(8,128)(2,1)S(1)} %get-tuple-element.79), channel_id=1, source_target_pairs={{0,4},{4,8},{8,12},{12,16},{16,20},{20,24},{24,28},{28,32},{32,36}... | collective-permute-start | bytes 1843208 | tf_op jit(solution)/shard_map/ppermute | solution.py:805
  114.3 6.0 %collective-permute-done.8.refs_4_ = bf16[15,160,128]{2,1,0:T(8,128)(2,1)S(1)} collective-permute-done((bf16[15,160,128]{2,1,0:T(8,128)(2,1)S(1)}, bf16[15,160,128]{2,1,0:T(8,128)(2,1)S(1)}, u32[]{:S(2)}, u32[]{:S(2)}) %collective-permute-start.8) | collective-permute-done | bytes 614432 | tf_op jit(solution)/shard_map/ppermute | solution.py:805
  120.2 4.1 %collective-permute-done.9.refs_5_ = bf16[15,160,128]{2,1,0:T(8,128)(2,1)S(1)} collective-permute-done((bf16[15,160,128]{2,1,0:T(8,128)(2,1)S(1)}, bf16[15,160,128]{2,1,0:T(8,128)(2,1)S(1)}, u32[]{:S(2)}, u32[]{:S(2)}) %collective-permute-start.9) | collective-permute-done | bytes 614432 | tf_op jit(solution)/shard_map/ppermute | solution.py:805
  124.4 13.3 %backward_first.1 = (f32[32,128,128]{2,1,0:T(8,128)S(1)}, bf16[32,128,128]{2,1,0:T(8,128)(2,1)S(1)}, bf16[48,16,128]{2,1,0:T(8,128)(2,1)S(1)}, bf16[48,16,128]{2,1,0:T(8,128)(2,1)S(1)}, f32[4,128,128]{2,1,0:T(8,128)S(1)}) custom-call(s32[4]{0:T(128)S(1)} %copy-done.28, bf16[32,128,128]{2,1,0:T(8,128)(2,1)S(1)} %copy-done.14, ...), custom_call_target="tpu_custom_call" | custom-call | flops 1146880000 | bytes 14680064 | tf_op jit(solution)/shard_map/backward_first/pallas_call | solution.py:787
  137.8 1.9 collective-permute-start.10
  139.7 2.4 %collective-permute-start.11 = (bf16[48,16,128]{2,1,0:T(8,128)(2,1)S(1)}, bf16[48,16,128]{2,1,0:T(8,128)(2,1)S(1)}, u32[]{:S(2)}, u32[]{:S(2)}) collective-permute-start(bf16[48,16,128]{2,1,0:T(8,128)(2,1)S(1)} %get-tuple-element.91), channel_id=1, source_target_pairs={{1,0},{2,1},{3,2},{5,4},{6,5},{7,6},{9,8},{10,9},{11,10},{13,12},{... | collective-permute-start | bytes 589832 | tf_op jit(solution)/shard_map/ppermute | solution.py:805
  142.3 5.9 %collective-permute-done.11.from_right.refs_3_ = bf16[48,16,128]{2,1,0:T(8,128)(2,1)S(1)} collective-permute-done((bf16[48,16,128]{2,1,0:T(8,128)(2,1)S(1)}, bf16[48,16,128]{2,1,0:T(8,128)(2,1)S(1)}, u32[]{:S(2)}, u32[]{:S(2)}) %collective-permute-start.11) | collective-permute-done | bytes 196640 | tf_op jit(solution)/shard_map/ppermute | solution.py:805
  149.0 5.6 %collective-permute-start.12 = (bf16[15,160,128]{2,1,0:T(8,128)(2,1)S(1)}, bf16[15,160,128]{2,1,0:T(8,128)(2,1)S(1)}, u32[]{:S(2)}, u32[]{:S(2)}) collective-permute-start(bf16[15,160,128]{2,1,0:T(8,128)(2,1)S(1)} %get-tuple-element.93), channel_id=1, source_target_pairs={{0,4},{4,8},{8,12},{12,16},{16,20},{20,24},{24,28},{28,32},{32,36}... | collective-permute-start | bytes 1843208 | tf_op jit(solution)/shard_map/ppermute | solution.py:805
  157.5 6.5 %collective-permute-done.12.refs_4_ = bf16[15,160,128]{2,1,0:T(8,128)(2,1)S(1)} collective-permute-done((bf16[15,160,128]{2,1,0:T(8,128)(2,1)S(1)}, bf16[15,160,128]{2,1,0:T(8,128)(2,1)S(1)}, u32[]{:S(2)}, u32[]{:S(2)}) %collective-permute-start.12) | collective-permute-done | bytes 614432 | tf_op jit(solution)/shard_map/ppermute | solution.py:805
  164.0 4.1 %collective-permute-done.13.refs_5_ = bf16[15,160,128]{2,1,0:T(8,128)(2,1)S(1)} collective-permute-done((bf16[15,160,128]{2,1,0:T(8,128)(2,1)S(1)}, bf16[15,160,128]{2,1,0:T(8,128)(2,1)S(1)}, u32[]{:S(2)}, u32[]{:S(2)}) %collective-permute-start.13) | collective-permute-done | bytes 614432 | tf_op jit(solution)/shard_map/ppermute | solution.py:805
  168.2 13.7 %backward_last.1 = (bf16[32,128,128]{2,1,0:T(8,128)(2,1)}, f32[3,128,128]{2,1,0:T(8,128)S(1)}) custom-call(s32[4]{0:T(128)S(1)} %copy-done.28, bf16[32,128,128]{2,1,0:T(8,128)(2,1)S(1)} %get-tuple-element.89.pre.refs_1_, bf16[48,16,128]{2,1,0:T(8,128)(2,1)S(1)} %collective-permute-done.10.from_left.refs_2_, ...), custom_call_target="tpu_custom_call" | custom-call | flops 1146880000 | bytes 14680064 | tf_op jit(solution)/shard_map/backward_last/pallas_call | solution.py:787
  182.3 21.7 %all_to_all.12 = bf16[9,128,128]{2,0,1:T(8,128)(2,1)S(1)} all-to-all(bf16[9,128,128]{2,0,1:T(8,128)(2,1)S(1)} %copy.34), channel_id=1, replica_groups=mesh['rows'=32,'cols'=4] {'rows'}, dimensions={1} | all-to-all | bytes 589824 | tf_op jit(solution)/shard_map/all_to_all | solution.py:854
  204.1 6.3 %all_gather.7 = bf16[4,9,512]{2,1,0:T(8,128)(2,1)S(1)} all-gather(bf16[1,9,512]{2,1,0:T(8,128)(2,1)S(1)} %all_gather.6), channel_id=1, replica_groups=mesh['rows'=32,'cols'=4] {'cols'}, dimensions={0}, use_global_device_ids=true | all-gather | bytes 46080 | tf_op jit(solution)/shard_map/all_gather | solution.py:856
  (121 shorter events, 29.9 us)
Async XLA Ops:
  1.8 10.1 %collective-permute-start.1 = (bf16[32,32,128]{2,1,0:T(8,128)(2,1)S(1)}, bf16[32,32,128]{2,1,0:T(8,128)(2,1)S(1)}, u32[]{:S(2)}, u32[]{:S(2)}) collective-permute-start(bf16[32,32,128]{2,1,0:T(8,128)(2,1)S(1)} %get-tuple-element.111), channel_id=1, source_target_pairs={{1,0},{2,1},{3,2},{5,4},{6,5},{7,6},{9,8},{10,9},{11,10},{13,12},{... | collective-permute-start | bytes 786440 | tf_op jit(solution)/shard_map/ppermute | solution.py:805
  5.2 7.9 %collective-permute-start = (bf16[32,32,128]{2,1,0:T(8,128)(2,1)S(1)}, bf16[32,32,128]{2,1,0:T(8,128)(2,1)S(1)}, u32[]{:S(2)}, u32[]{:S(2)}) collective-permute-start(bf16[32,32,128]{2,1,0:T(8,128)(2,1)S(1)} %get-tuple-element.112), channel_id=1, source_target_pairs={{0,1},{1,2},{2,3},{4,5},{5,6},{6,7},{8,9},{9,10},{10,11},{12,13},{... | collective-permute-start | bytes 786440 | tf_op jit(solution)/shard_map/ppermute | solution.py:805
  13.2 18.6 %collective-permute-start.2 = (bf16[15,192,128]{2,1,0:T(8,128)(2,1)S(1)}, bf16[15,192,128]{2,1,0:T(8,128)(2,1)S(1)}, u32[]{:S(2)}, u32[]{:S(2)}) collective-permute-start(bf16[15,192,128]{2,1,0:T(8,128)(2,1)S(1)} %pad_maximum_fusion), channel_id=1, source_target_pairs={{0,4},{4,8},{8,12},{12,16},{16,20},{20,24},{24,28},{28,32},{32,36}... | collective-permute-start | bytes 2211848 | tf_op jit(solution)/shard_map/ppermute | solution.py:805
  16.8 16.6 %collective-permute-start.3 = (bf16[15,192,128]{2,1,0:T(8,128)(2,1)S(1)}, bf16[15,192,128]{2,1,0:T(8,128)(2,1)S(1)}, u32[]{:S(2)}, u32[]{:S(2)}) collective-permute-start(bf16[15,192,128]{2,1,0:T(8,128)(2,1)S(1)} %pad_maximum_fusion.1), channel_id=1, source_target_pairs={{4,0},{8,4},{12,8},{16,12},{20,16},{24,20},{28,24},{32,28},{36,32}... | collective-permute-start | bytes 2211848 | tf_op jit(solution)/shard_map/ppermute | solution.py:805
  18.2 32.2 %copy-start.27 = (s32[4]{0:T(128)}, s32[4]{0:T(128)S(1)}, u32[]{:S(2)}) copy-start(s32[4]{0:T(128)S(1)} %add_convert_fusion.refs_0_) | copy-start | bytes 52
  53.0 22.3 %collective-permute-start.5 = (bf16[15,160,128]{2,1,0:T(8,128)(2,1)}, bf16[15,160,128]{2,1,0:T(8,128)(2,1)S(1)}, u32[]{:S(2)}, u32[]{:S(2)}) collective-permute-start(bf16[15,160,128]{2,1,0:T(8,128)(2,1)} %get-tuple-element.107), channel_id=1, source_target_pairs={{4,0},{8,4},{12,8},{16,12},{20,16},{24,20},{28,24},{32,28},{36,32}... | collective-permute-start | bytes 1843208 | tf_op jit(solution)/shard_map/ppermute | solution.py:805
  54.3 21.1 %collective-permute-start.4 = (bf16[15,160,128]{2,1,0:T(8,128)(2,1)}, bf16[15,160,128]{2,1,0:T(8,128)(2,1)S(1)}, u32[]{:S(2)}, u32[]{:S(2)}) collective-permute-start(bf16[15,160,128]{2,1,0:T(8,128)(2,1)} %get-tuple-element.108), channel_id=1, source_target_pairs={{0,4},{4,8},{8,12},{12,16},{16,20},{20,24},{24,28},{28,32},{32,36}... | collective-permute-start | bytes 1843208 | tf_op jit(solution)/shard_map/ppermute | solution.py:805
  75.3 29.6 %copy-start.3 = (bf16[32,128,128]{2,1,0:T(8,128)(2,1)S(1)}, bf16[32,128,128]{2,1,0:T(8,128)(2,1)}, u32[]{:S(2)}) copy-start(bf16[32,128,128]{2,1,0:T(8,128)(2,1)} %base.3) | copy-start | bytes 3145732
  75.3 49.0 %copy-start.20 = (bf16[32,128,128]{2,1,0:T(8,128)(2,1)S(1)}, bf16[32,128,128]{2,1,0:T(8,128)(2,1)}, u32[]{:S(2)}) copy-start(bf16[32,128,128]{2,1,0:T(8,128)(2,1)} %get-tuple-element.84.refs_12_) | copy-start | bytes 3145732
  91.0 8.1 %collective-permute-start.6 = (bf16[48,16,128]{2,1,0:T(8,128)(2,1)S(1)}, bf16[48,16,128]{2,1,0:T(8,128)(2,1)S(1)}, u32[]{:S(2)}, u32[]{:S(2)}) collective-permute-start(bf16[48,16,128]{2,1,0:T(8,128)(2,1)S(1)} %get-tuple-element.77), channel_id=1, source_target_pairs={{0,1},{1,2},{2,3},{4,5},{5,6},{6,7},{8,9},{9,10},{10,11},{12,13},{... | collective-permute-start | bytes 589832 | tf_op jit(solution)/shard_map/ppermute | solution.py:805
  96.4 8.5 %collective-permute-start.7 = (bf16[48,16,128]{2,1,0:T(8,128)(2,1)S(1)}, bf16[48,16,128]{2,1,0:T(8,128)(2,1)S(1)}, u32[]{:S(2)}, u32[]{:S(2)}) collective-permute-start(bf16[48,16,128]{2,1,0:T(8,128)(2,1)S(1)} %get-tuple-element.78), channel_id=1, source_target_pairs={{1,0},{2,1},{3,2},{5,4},{6,5},{7,6},{9,8},{10,9},{11,10},{13,12},{... | collective-permute-start | bytes 589832 | tf_op jit(solution)/shard_map/ppermute | solution.py:805
  106.2 18.2 %copy-start.18 = (bf16[32,128,128]{2,1,0:T(8,128)(2,1)S(1)}, bf16[32,128,128]{2,1,0:T(8,128)(2,1)}, u32[]{:S(2)}) copy-start(bf16[32,128,128]{2,1,0:T(8,128)(2,1)} %get-tuple-element.85.refs_13_) | copy-start | bytes 3145732
  106.2 18.2 %copy-start.19 = (bf16[32,128,128]{2,1,0:T(8,128)(2,1)S(1)}, bf16[32,128,128]{2,1,0:T(8,128)(2,1)}, u32[]{:S(2)}) copy-start(bf16[32,128,128]{2,1,0:T(8,128)(2,1)} %get-tuple-element.88.refs_16_) | copy-start | bytes 3145732
  107.0 13.2 %collective-permute-start.8 = (bf16[15,160,128]{2,1,0:T(8,128)(2,1)S(1)}, bf16[15,160,128]{2,1,0:T(8,128)(2,1)S(1)}, u32[]{:S(2)}, u32[]{:S(2)}) collective-permute-start(bf16[15,160,128]{2,1,0:T(8,128)(2,1)S(1)} %get-tuple-element.79), channel_id=1, source_target_pairs={{0,4},{4,8},{8,12},{12,16},{16,20},{20,24},{24,28},{28,32},{32,36}... | collective-permute-start | bytes 1843208 | tf_op jit(solution)/shard_map/ppermute | solution.py:805
  111.3 13.1 %collective-permute-start.9 = (bf16[15,160,128]{2,1,0:T(8,128)(2,1)S(1)}, bf16[15,160,128]{2,1,0:T(8,128)(2,1)S(1)}, u32[]{:S(2)}, u32[]{:S(2)}) collective-permute-start(bf16[15,160,128]{2,1,0:T(8,128)(2,1)S(1)} %get-tuple-element.80), channel_id=1, source_target_pairs={{4,0},{8,4},{12,8},{16,12},{20,16},{24,20},{28,24},{32,28},{36,32}... | collective-permute-start | bytes 1843208 | tf_op jit(solution)/shard_map/ppermute | solution.py:805
  137.8 4.5 %collective-permute-start.10 = (bf16[48,16,128]{2,1,0:T(8,128)(2,1)S(1)}, bf16[48,16,128]{2,1,0:T(8,128)(2,1)S(1)}, u32[]{:S(2)}, u32[]{:S(2)}) collective-permute-start(bf16[48,16,128]{2,1,0:T(8,128)(2,1)S(1)} %get-tuple-element.90), channel_id=1, source_target_pairs={{0,1},{1,2},{2,3},{4,5},{5,6},{6,7},{8,9},{9,10},{10,11},{12,13},{... | collective-permute-start | bytes 589832 | tf_op jit(solution)/shard_map/ppermute | solution.py:805
  139.7 8.5 %collective-permute-start.11 = (bf16[48,16,128]{2,1,0:T(8,128)(2,1)S(1)}, bf16[48,16,128]{2,1,0:T(8,128)(2,1)S(1)}, u32[]{:S(2)}, u32[]{:S(2)}) collective-permute-start(bf16[48,16,128]{2,1,0:T(8,128)(2,1)S(1)} %get-tuple-element.91), channel_id=1, source_target_pairs={{1,0},{2,1},{3,2},{5,4},{6,5},{7,6},{9,8},{10,9},{11,10},{13,12},{... | collective-permute-start | bytes 589832 | tf_op jit(solution)/shard_map/ppermute | solution.py:805
  148.2 20.0 %copy-start.12 = (bf16[32,128,128]{2,1,0:T(8,128)(2,1)S(1)}, bf16[32,128,128]{2,1,0:T(8,128)(2,1)}, u32[]{:S(2)}) copy-start(bf16[32,128,128]{2,1,0:T(8,128)(2,1)} %get-tuple-element.99.refs_13_) | copy-start | bytes 3145732
  149.0 15.0 %collective-permute-start.12 = (bf16[15,160,128]{2,1,0:T(8,128)(2,1)S(1)}, bf16[15,160,128]{2,1,0:T(8,128)(2,1)S(1)}, u32[]{:S(2)}, u32[]{:S(2)}) collective-permute-start(bf16[15,160,128]{2,1,0:T(8,128)(2,1)S(1)} %get-tuple-element.93), channel_id=1, source_target_pairs={{0,4},{4,8},{8,12},{12,16},{16,20},{20,24},{24,28},{28,32},{32,36}... | collective-permute-start | bytes 1843208 | tf_op jit(solution)/shard_map/ppermute | solution.py:805
  154.6 13.6 %collective-permute-start.13 = (bf16[15,160,128]{2,1,0:T(8,128)(2,1)S(1)}, bf16[15,160,128]{2,1,0:T(8,128)(2,1)S(1)}, u32[]{:S(2)}, u32[]{:S(2)}) collective-permute-start(bf16[15,160,128]{2,1,0:T(8,128)(2,1)S(1)} %get-tuple-element.94), channel_id=1, source_target_pairs={{4,0},{8,4},{12,8},{16,12},{20,16},{24,20},{28,24},{32,28},{36,32}... | collective-permute-start | bytes 1843208 | tf_op jit(solution)/shard_map/ppermute | solution.py:805
  155.9 12.2 %copy-start.4 = (bf16[48,144,128]{2,1,0:T(8,128)(2,1)S(1)}, bf16[48,144,128]{2,1,0:T(8,128)(2,1)}, u32[]{:S(2)}) copy-start(bf16[48,144,128]{2,1,0:T(8,128)(2,1)} %get-tuple-element.96.refs_10_) | copy-start | bytes 5308420
  155.9 12.2 %copy-start.7 = (bf16[38,160,128]{2,1,0:T(8,128)(2,1)S(1)}, bf16[38,160,128]{2,1,0:T(8,128)(2,1)}, u32[]{:S(2)}) copy-start(bf16[38,160,128]{2,1,0:T(8,128)(2,1)} %get-tuple-element.97.refs_11_) | copy-start | bytes 4669444
  155.9 12.2 %copy-start.8 = (bf16[36,160,128]{2,1,0:T(8,128)(2,1)S(1)}, bf16[36,160,128]{2,1,0:T(8,128)(2,1)}, u32[]{:S(2)}) copy-start(bf16[36,160,128]{2,1,0:T(8,128)(2,1)} %get-tuple-element.98.refs_12_) | copy-start | bytes 4423684
  155.9 12.2 %copy-start.10 = (bf16[32,128,128]{2,1,0:T(8,128)(2,1)S(1)}, bf16[32,128,128]{2,1,0:T(8,128)(2,1)}, u32[]{:S(2)}) copy-start(bf16[32,128,128]{2,1,0:T(8,128)(2,1)} %get-tuple-element.101.refs_15_) | copy-start | bytes 3145732
  (24 other events, 155.4 us)

commit v4 on v3

--- a/solution.py
+++ b/solution.py
@@ -68,6 +68,12 @@
         out.append((low, min(size, high - low)))
         low += size
     return out
+
+
+def pull_back(upstream, weight):
+    return lax.dot_general(
+        upstream.reshape(-1, CH), weight, (((1,), (1,)), ((), ())), preferred_element_type=F32
+    )
 
 
 def grad_of(hidden, upstream):
@@ -247,13 +253,13 @@
     pieces = take(1 if seg else 3)
     top, bottom, kernels, weights = take(4)
     if seg:
-        coarse, cot, back_weight = take(3)
+        cot = take(1)[0]
     x_in = take(3)
     take(6)
     if seg:
         out, pre, strip_left, strip_right, grad = take(5)
     else:
-        x_out, hid_three, slope_three = take(3)
+        x_out, up_out, down_out, hid_three, slope_three = take(5)
     hid_out, slope_out = take(3), take(3)
     x_bufs, h_bufs, slopes = take(4), take(4), take(4)
     hid_two, own_buf, sem = take(3)
@@ -364,14 +370,7 @@
     def last_mix(it, _):
         at = 16 * it
         value = mixed_rows(h_bufs[3], at, x_bufs[3], at, 16, seg, 3, weights)
-        if seg:
-            for q in range(2):
-                extra = coarse[2 * it + q][:, None, :]
-                part = value[q * STRIDE : (q + 1) * STRIDE].reshape(STRIDE, -1, STRIDE, CH)
-                part = (part + extra[None]).reshape(STRIDE, COLS, CH)
-                own_buf[pl.ds(at + q * STRIDE, STRIDE)] = part.astype(BF)
-        else:
-            own_buf[pl.ds(at, 16)] = value.astype(BF)
+        own_buf[pl.ds(at, 16)] = value.astype(BF)
         return 0
 
     lax.fori_loop(0, 2, last_mix, 0)
@@ -383,7 +382,7 @@
             rows = slice(16 * b, 16 * b + 16)
             up = cot[rows]
             total = total + grad_of(h_bufs[3][rows], up)
-            pulled = jnp.dot(up.reshape(-1, CH), back_weight[...], preferred_element_type=F32)
+            pulled = pull_back(up, weights[3])
             value = pulled.reshape(16, COLS, CH) * slopes[3][rows].astype(F32)
             value = value.astype(BF)
             pre[rows] = value
@@ -404,6 +403,8 @@
             own_buf[:, CHALO + COLS : WIDE] = zeros
 
         send(own_buf, x_out, 14)
+        send(own_buf.at[pl.ds(0, RH)], up_out, 15)
+        send(own_buf.at[pl.ds(ROWS - RH, RH)], down_out, 16)
     for copy in copies:
         copy.wait()
 
@@ -423,8 +424,9 @@
         outs = [block, block, strip, strip, sds((CH, CH), F32)]
         specs = [ANY] + [VMEM] * 4
     else:
-        outs = [sds((ROWS, WIDE, CH), BF), block, block]
-        specs = [ANY, ANY, ANY]
+        ends_shape = sds((RH, WIDE, CH), BF)
+        outs = [sds((ROWS, WIDE, CH), BF), ends_shape, ends_shape, block, block]
+        specs = [ANY] * 5
     shift = len(outs)
     outs = outs + [sds(a.shape, BF) for a in begun[:6]]
     specs = specs + [ANY] * 6
@@ -452,7 +454,7 @@
     )(*args)
 
 
-def pool_kernel(feature, cot, weight, weight_t, coarse, back, grad):
+def pool_kernel(feature, cot, x_last, weight, out, back, grad):
     total = None
     for b in range(ROWS // STRIDE):
         rows = slice(STRIDE * b, STRIDE * (b + 1))
@@ -465,26 +467,27 @@
 
         pooled = (block_sum(feature) * (1.0 / (STRIDE * STRIDE))).astype(BF)
         block_cot = block_sum(cot).astype(BF)
-        coarse[b] = jnp.dot(pooled, weight[...], preferred_element_type=F32)
-        back[b] = jnp.dot(block_cot, weight_t[...], preferred_element_type=F32) * (
-            1.0 / (STRIDE * STRIDE)
-        )
+        coarse = jnp.dot(pooled, weight[...], preferred_element_type=F32)
+        value = x_last[rows].astype(F32).reshape(STRIDE, COLS // STRIDE, STRIDE, CH)
+        value = value + coarse[:, None, :][None]
+        out[rows] = value.reshape(STRIDE, COLS, CH).astype(BF)
+        back[b] = pull_back(block_cot, weight[...]) * (1.0 / (STRIDE * STRIDE))
         part = grad_of(pooled, block_cot)
         total = part if total is None else total + part
     grad[...] = total
 
 
-def pool(feature, cot, weight):
+def pool(feature, cot, x_last, weight):
     small = sds((ROWS // STRIDE, COLS // STRIDE, CH), F32)
     return pl.pallas_call(
         pool_kernel,
-        out_shape=[small, small, sds((CH, CH), F32)],
+        out_shape=[sds((ROWS, COLS, CH), BF), small, sds((CH, CH), F32)],
         in_specs=[VMEM] * 4,
         out_specs=[VMEM] * 3,
         compiler_params=pltpu.CompilerParams(vmem_limit_bytes=16 * 2**20),
-        cost_estimate=pl.CostEstimate(flops=10**8, bytes_accessed=2 * 2**20, transcendentals=0),
+        cost_estimate=pl.CostEstimate(flops=10**9, bytes_accessed=4 * 2**20, transcendentals=0),
         name="pool",
-    )(feature, cot, weight, weight.T)
+    )(feature, cot, x_last, weight)
 
 
 BASE = 8
@@ -611,7 +614,7 @@
     refs = list(refs)
     take = lambda n: [refs.pop(0) for _ in range(n)]
     edges, pre, from_left, from_right, top, bottom = take(6)
-    kernels, weights_t = take(2)
+    kernels, weights = take(2)
     count = 3 if last else 4
     if last:
         back = take(1)[0]
@@ -703,9 +706,7 @@
         def pull_body(it, _):
             at = it * step
             up = ups[pl.ds(UHALO - halo + at, step)].astype(BF)
-            pulled = jnp.dot(
-                up.reshape(step * UWIDE, CH), weights_t[layer], preferred_element_type=F32
-            ).reshape(step, UWIDE, CH)
+            pulled = pull_back(up, weights[layer]).reshape(step, UWIDE, CH)
             slope = slopes[k][pl.ds(skip + at, step)].astype(F32)
             slope = slope[:, DSIDE[layer] - 8 : DSIDE[layer] - 8 + UWIDE]
             buf[pl.ds(BASE - halo + at, step), 8:152] = pulled * slope
@@ -758,7 +759,7 @@
             up_out[rows] = value
             up = value.astype(BF)
             total = total + grad_of(hids[3][rows], up)
-            pulled = jnp.dot(up.reshape(-1, CH), weights_t[3], preferred_element_type=F32)
+            pulled = pull_back(up, weights[3])
             value = (pulled.reshape(16, COLS, CH) * slopes[3][rows].astype(F32)).astype(BF)
             pre_out[rows] = value
             strip_left[rows] = value[:, :CHALO]
@@ -768,7 +769,7 @@
         grads[3] = total
 
 
-def backward(last, edges, pre, sides, part, ends_in, kernels, weights_t, slopes, hids, back=()):
+def backward(last, edges, pre, sides, part, ends_in, kernels, weights, slopes, hids, back=()):
     count = len(slopes)
     block = sds((ROWS, COLS, CH), BF)
     if last:
@@ -783,7 +784,7 @@
     scratch += [pltpu.VMEM(a.shape, BF) for a in slopes]
     scratch += [pltpu.VMEM(a.shape, BF) for a in hids]
     scratch += [pltpu.SemaphoreType.DMA((2 * count + 1,))]
-    args = (edges, pre, *sides, *ends_in, kernels, weights_t, *back)
+    args = (edges, pre, *sides, *ends_in, kernels, weights, *back)
     return pl.pallas_call(
         functools.partial(backward_kernel, last),
         out_shape=outs,
@@ -810,25 +811,23 @@
     row_end, col_end = lax.axis_size("rows") - 1, lax.axis_size("cols") - 1
     edges = jnp.stack([row == 0, row == row_end, col == 0, col == col_end]).astype(jnp.int32)
     kernels = depth_kernels.astype(F32)
-    weights_t = jnp.swapaxes(point_weights, 1, 2)
 
     left, right = exchange(
         features_in[:, : SIDES[0]], features_in[:, COLS - SIDES[0] :], "cols"
     )
     wide = lambda rows: jnp.concatenate([left[rows], features_in[rows], right[rows]], axis=1)
     top, bottom = exchange(wide(slice(0, RH)), wide(slice(ROWS - RH, ROWS)), "rows")
-    coarse, back, coarse_grad = pool(features_in, cotangent, coarse_weight)
     pieces = (left, features_in, right)
     begun = inner(0, edges, pieces, kernels[:3], point_weights[:3])
-    x_mid, hid_three, slope_three, *kept = outer(
+    x_mid, x_up, x_down, hid_three, slope_three, *kept = outer(
         0, edges, pieces, top, bottom, kernels[:4], point_weights[:4], begun
     )
     hid_low, slope_low = kept[:3] + [hid_three], kept[3:] + [slope_three]
-    top, bottom = exchange(x_mid[:RH], x_mid[ROWS - RH :], "rows")
+    top, bottom = exchange(x_up, x_down, "rows")
     begun = inner(1, edges, (x_mid,), kernels[4:7], point_weights[4:7])
-    output, pre, strip_left, strip_right, grad_top, *kept = outer(
+    x_last, pre, strip_left, strip_right, grad_top, *kept = outer(
         1, edges, (x_mid,), top, bottom, kernels[4:], point_weights[4:], begun,
-        (coarse, cotangent, weights_t[7]),
+        (cotangent,),
     )
     hid_high, slope_high = kept[:3], kept[3:]
 
@@ -838,15 +837,17 @@
     part = own_part(pre, *sides, cotangent, kernels[7])
     upstream, pre, strip_left, strip_right, grad_mid = backward(
         False, edges, pre, sides, part, rows_in,
-        kernels[4:], jnp.concatenate([weights_t[4:7], weights_t[3:4]]),
+        kernels[4:], jnp.concatenate([point_weights[4:7], point_weights[3:4]]),
         order(slope_high) + [slope_low[3]], order(hid_high) + [hid_low[3]],
     )
     sides = exchange(strip_left, strip_right, "cols")
     rows_in = exchange(*ends(pre, *sides, upstream, kernels[3]), "rows")
-    part = own_part(pre, *sides, upstream, kernels[3])
+    output, back, coarse_grad = pool(features_in, cotangent, x_last, coarse_weight)
+    later, back = lax.optimization_barrier((upstream, back))
+    part = own_part(pre, *sides, later, kernels[3])
     input_grad, grad_low = backward(
         True, edges, pre, sides, part, rows_in,
-        kernels[:4], weights_t[:3], order(slope_low), order(hid_low), (back,),
+        kernels[:4], point_weights[:3], order(slope_low), order(hid_low), (back,),
     )
 
     grads = [grad_low[2], grad_low[1], grad_low[0], grad_mid[3], grad_mid[2], grad_mid[1]]

time: 212 us -> 208 us (0.981)
  local copies, waits for them, and re-layouts: 15.5 us -> 7.22 us
  blocking collectives: 27.9 us -> 31.5 us
  starting transfers between devices: 42.3 us -> 39.8 us
    unnamed x77 -> x63, local copies, waits for them, and re-layouts: 8.75 us -> 5.01 us
    all_to_all x1, blocking collectives: 21.7 us -> 25.2 us  [local(): shares = lax.all_to_all(grads, 'rows', 1, 0, tiled=True)]
    ppermute x7, waiting for transfers between devices: 22.9 us -> 26 us  [exchange(): lax.ppermute(to_before, axis, back)]
    slice x3 -> x2, local copies, waits for them, and re-layouts: 2.56 us -> 0.01 us  [local(): point_weights[3:4]]
    ppermute x7, starting transfers between devices: 29.5 us -> 27 us  [exchange(): lax.ppermute(to_after, axis, forth)]
  transfers between devices with their start and end apart: 14 -> 14, of which waited for: 10 -> 12; matrix products, arithmetic and copies ran while one was open for 2% -> 0% of each run, Pallas kernels for 13% -> 13%
where the time goes in v4:
time: 208 us; the launch traced here: 207 us
  Pallas kernels  88.2 us (42%)
  starting transfers between devices  39.8 us (19%)
  waiting for transfers between devices  38.8 us (19%)
  blocking collectives  31.5 us (15%)
  local copies, waits for them, and re-layouts  7.22 us (3%)
    pallas_call x2, Pallas kernels, outer(): pl.pallas_call(functools.partial(outer_kernel, seg), out_shape=outs, in_s...  31.9 us
    pallas_call x2, Pallas kernels, backward(): pl.pallas_call(functools.partial(backward_kernel, last), out_shape=outs,...  27.2 us
    ppermute x7, starting transfers between devices, exchange(): lax.ppermute(to_after, axis, forth)  27 us
    ppermute x7, waiting for transfers between devices, exchange(): lax.ppermute(to_before, axis, back)  26 us
    all_to_all x1, blocking collectives, local(): shares = lax.all_to_all(grads, 'rows', 1, 0, tiled=True)  25.2 us
    pallas_call x2, Pallas kernels, inner(): pl.pallas_call(functools.partial(inner_kernel, seg), out_shape=outs, in_s...  22.7 us
    ppermute x7, starting transfers between devices, exchange(): lax.ppermute(to_before, axis, back)  12.8 us
    ppermute x7, waiting for transfers between devices, exchange(): lax.ppermute(to_after, axis, forth)  12.8 us
  transfers between devices with their start and end apart: 14, of which 12 were waited for; matrix products, arithmetic and copies ran while one was open for 0% of the time, Pallas kernels for 13%

profile of v4, /device:TPU:1, one launch (start us, length us, event | category | flops | bytes accessed | tf_op | source)
XLA Modules:
  0.0 207.2 jit_solution(7827634482741979971)
XLA Ops:
  1.8 3.3 %collective-permute-start.1 = (bf16[32,32,128]{2,1,0:T(8,128)(2,1)S(1)}, bf16[32,32,128]{2,1,0:T(8,128)(2,1)S(1)}, u32[]{:S(2)}, u32[]{:S(2)}) collective-permute-start(bf16[32,32,128]{2,1,0:T(8,128)(2,1)S(1)} %get-tuple-element.117), channel_id=1, source_target_pairs={{1,0},{2,1},{3,2},{5,4},{6,5},{7,6},{9,8},{10,9},{11,10},{13,12},{... | collective-permute-start | bytes 786440 | tf_op jit(solution)/shard_map/ppermute | solution.py:806
  5.2 4.6 %collective-permute-start = (bf16[32,32,128]{2,1,0:T(8,128)(2,1)S(1)}, bf16[32,32,128]{2,1,0:T(8,128)(2,1)S(1)}, u32[]{:S(2)}, u32[]{:S(2)}) collective-permute-start(bf16[32,32,128]{2,1,0:T(8,128)(2,1)S(1)} %get-tuple-element.118), channel_id=1, source_target_pairs={{0,1},{1,2},{2,3},{4,5},{5,6},{6,7},{8,9},{9,10},{10,11},{12,13},{... | collective-permute-start | bytes 786440 | tf_op jit(solution)/shard_map/ppermute | solution.py:806
  10.0 2.0 collective-permute-done.1.refs_3_
  13.2 3.6 %collective-permute-start.2 = (bf16[15,192,128]{2,1,0:T(8,128)(2,1)S(1)}, bf16[15,192,128]{2,1,0:T(8,128)(2,1)S(1)}, u32[]{:S(2)}, u32[]{:S(2)}) collective-permute-start(bf16[15,192,128]{2,1,0:T(8,128)(2,1)S(1)} %pad_maximum_fusion), channel_id=1, source_target_pairs={{0,4},{4,8},{8,12},{12,16},{16,20},{20,24},{24,28},{28,32},{32,36}... | collective-permute-start | bytes 2211848 | tf_op jit(solution)/shard_map/ppermute | solution.py:806
  18.3 11.9 %inner_first.1 = (bf16[32,128,128]{2,1,0:T(8,128)(2,1)}, bf16[32,128,128]{2,1,0:T(8,128)(2,1)}, bf16[32,128,128]{2,1,0:T(8,128)(2,1)}, bf16[36,160,128]{2,1,0:T(...) custom-call(s32[4]{0:T(128)S(1)} %add_convert_fusion.refs_0_, ...), custom_call_target="tpu_custom_call" | custom-call | flops 393216000 | bytes 12582912 | tf_op jit(solution)/shard_map/inner_first/pallas_call | solution.py:235
  31.1 2.3 %collective-permute-done.3.refs_5_ = bf16[15,192,128]{2,1,0:T(8,128)(2,1)S(1)} collective-permute-done((bf16[15,192,128]{2,1,0:T(8,128)(2,1)S(1)}, bf16[15,192,128]{2,1,0:T(8,128)(2,1)S(1)}, u32[]{:S(2)}, u32[]{:S(2)}) %collective-permute-start.3) | collective-permute-done | bytes 737312 | tf_op jit(solution)/shard_map/ppermute | solution.py:806
  34.3 16.3 %outer_first.1 = (bf16[32,160,128]{2,1,0:T(8,128)(2,1)}, bf16[15,160,128]{2,1,0:T(8,128)(2,1)S(1)}, bf16[15,160,128]{2,1,0:T(8,128)(2,1)S(1)}, bf16[32,128,128]{...) custom-call(s32[4]{0:T(128)S(1)} %add_convert_fusion.refs_0_, ...), custom_call_target="tpu_custom_call", output_to_operand_aliasing={{5}: (11, {}), {6}: (12, {}), {7}: (13, {}), {8}: (14, {}),... | custom-call | flops 655360000 | bytes 12582912 | tf_op jit(solution)/shard_map/outer_first/pallas_call | solution.py:442
  50.6 3.2 %collective-permute-start.4 = (bf16[15,160,128]{2,1,0:T(8,128)(2,1)S(1)}, bf16[15,160,128]{2,1,0:T(8,128)(2,1)S(1)}, u32[]{:S(2)}, u32[]{:S(2)}) collective-permute-start(bf16[15,160,128]{2,1,0:T(8,128)(2,1)S(1)} %get-tuple-element.69), channel_id=1, source_target_pairs={{0,4},{4,8},{8,12},{12,16},{16,20},{20,24},{24,28},{28,32},{32,36}... | collective-permute-start | bytes 1843208 | tf_op jit(solution)/shard_map/ppermute | solution.py:806
  55.1 10.8 %inner_last.1 = (bf16[32,128,128]{2,1,0:T(8,128)(2,1)S(1)}, bf16[32,128,128]{2,1,0:T(8,128)(2,1)}, bf16[32,128,128]{2,1,0:T(8,128)(2,1)}, bf16[36,160,128]{2,1,0...) custom-call(s32[4]{0:T(128)S(1)} %add_convert_fusion.refs_0_, ...), custom_call_target="tpu_custom_call" | custom-call | flops 393216000 | bytes 12582912 | tf_op jit(solution)/shard_map/inner_last/pallas_call | solution.py:235
  68.0 15.6 %outer_last.1 = (bf16[32,128,128]{2,1,0:T(8,128)(2,1)}, bf16[32,128,128]{2,1,0:T(8,128)(2,1)}, bf16[48,16,128]{2,1,0:T(8,128)(2,1)S(1)}, bf16[48,16,128]{2,1,0:T...) custom-call(s32[4]{0:T(128)S(1)} %add_convert_fusion.refs_0_, ...), custom_call_target="tpu_custom_call", output_to_operand_aliasing={{5}: (10, {}), {6}: (11, {}), {7}: (12, {}), {8}: (13, {}),... | custom-call | flops 655360000 | bytes 12582912 | tf_op jit(solution)/shard_map/outer_last/pallas_call | solution.py:442
  83.6 4.9 %collective-permute-start.6 = (bf16[48,16,128]{2,1,0:T(8,128)(2,1)S(1)}, bf16[48,16,128]{2,1,0:T(8,128)(2,1)S(1)}, u32[]{:S(2)}, u32[]{:S(2)}) collective-permute-start(bf16[48,16,128]{2,1,0:T(8,128)(2,1)S(1)} %get-tuple-element.83), channel_id=1, source_target_pairs={{0,1},{1,2},{2,3},{4,5},{5,6},{6,7},{8,9},{9,10},{10,11},{12,13},{... | collective-permute-start | bytes 589832 | tf_op jit(solution)/shard_map/ppermute | solution.py:806
  91.2 5.9 %collective-permute-done.7.from_right.refs_3_ = bf16[48,16,128]{2,1,0:T(8,128)(2,1)S(1)} collective-permute-done((bf16[48,16,128]{2,1,0:T(8,128)(2,1)S(1)}, bf16[48,16,128]{2,1,0:T(8,128)(2,1)S(1)}, u32[]{:S(2)}, u32[]{:S(2)}) %collective-permute-start.7) | collective-permute-done | bytes 196640 | tf_op jit(solution)/shard_map/ppermute | solution.py:806
  99.1 5.0 %collective-permute-start.8 = (bf16[15,160,128]{2,1,0:T(8,128)(2,1)S(1)}, bf16[15,160,128]{2,1,0:T(8,128)(2,1)S(1)}, u32[]{:S(2)}, u32[]{:S(2)}) collective-permute-start(bf16[15,160,128]{2,1,0:T(8,128)(2,1)S(1)} %get-tuple-element.85), channel_id=1, source_target_pairs={{0,4},{4,8},{8,12},{12,16},{16,20},{20,24},{24,28},{28,32},{32,36}... | collective-permute-start | bytes 1843208 | tf_op jit(solution)/shard_map/ppermute | solution.py:806
  107.1 6.0 %collective-permute-done.8.refs_4_ = bf16[15,160,128]{2,1,0:T(8,128)(2,1)S(1)} collective-permute-done((bf16[15,160,128]{2,1,0:T(8,128)(2,1)S(1)}, bf16[15,160,128]{2,1,0:T(8,128)(2,1)S(1)}, u32[]{:S(2)}, u32[]{:S(2)}) %collective-permute-start.8) | collective-permute-done | bytes 614432 | tf_op jit(solution)/shard_map/ppermute | solution.py:806
  113.1 4.1 %collective-permute-done.9.refs_5_ = bf16[15,160,128]{2,1,0:T(8,128)(2,1)S(1)} collective-permute-done((bf16[15,160,128]{2,1,0:T(8,128)(2,1)S(1)}, bf16[15,160,128]{2,1,0:T(8,128)(2,1)S(1)}, u32[]{:S(2)}, u32[]{:S(2)}) %collective-permute-start.9) | collective-permute-done | bytes 614432 | tf_op jit(solution)/shard_map/ppermute | solution.py:806
  117.3 13.5 %backward_first.1 = (f32[32,128,128]{2,1,0:T(8,128)S(1)}, bf16[32,128,128]{2,1,0:T(8,128)(2,1)S(1)}, bf16[48,16,128]{2,1,0:T(8,128)(2,1)S(1)}, bf16[48,16,128]{2,1,0:T(8,128)(2,1)S(1)}, f32[4,128,128]{2,1,0:T(8,128)S(1)}) custom-call(s32[4]{0:T(128)S(1)} %add_convert_fusion.refs_0_, bf16[32,128,128]{2,1,0:T(8,128)(2,1)S(1)} %copy-done.12, ...), custom_call_target="tpu_custom_call" | custom-call | flops 1146880000 | bytes 14680064 | tf_op jit(solution)/shard_map/backward_first/pallas_call | solution.py:788
  132.7 2.4 %collective-permute-start.11 = (bf16[48,16,128]{2,1,0:T(8,128)(2,1)S(1)}, bf16[48,16,128]{2,1,0:T(8,128)(2,1)S(1)}, u32[]{:S(2)}, u32[]{:S(2)}) collective-permute-start(bf16[48,16,128]{2,1,0:T(8,128)(2,1)S(1)} %get-tuple-element.97), channel_id=1, source_target_pairs={{1,0},{2,1},{3,2},{5,4},{6,5},{7,6},{9,8},{10,9},{11,10},{13,12},{... | collective-permute-start | bytes 589832 | tf_op jit(solution)/shard_map/ppermute | solution.py:806
  135.3 5.9 %collective-permute-done.11.from_right.refs_3_ = bf16[48,16,128]{2,1,0:T(8,128)(2,1)S(1)} collective-permute-done((bf16[48,16,128]{2,1,0:T(8,128)(2,1)S(1)}, bf16[48,16,128]{2,1,0:T(8,128)(2,1)S(1)}, u32[]{:S(2)}, u32[]{:S(2)}) %collective-permute-start.11) | collective-permute-done | bytes 196640 | tf_op jit(solution)/shard_map/ppermute | solution.py:806
  142.0 3.6 %collective-permute-start.12 = (bf16[15,160,128]{2,1,0:T(8,128)(2,1)S(1)}, bf16[15,160,128]{2,1,0:T(8,128)(2,1)S(1)}, u32[]{:S(2)}, u32[]{:S(2)}) collective-permute-start(bf16[15,160,128]{2,1,0:T(8,128)(2,1)S(1)} %get-tuple-element.99), channel_id=1, source_target_pairs={{0,4},{4,8},{8,12},{12,16},{16,20},{20,24},{24,28},{28,32},{32,36}... | collective-permute-start | bytes 1843208 | tf_op jit(solution)/shard_map/ppermute | solution.py:806
  150.2 4.8 %collective-permute-done.12.refs_4_ = bf16[15,160,128]{2,1,0:T(8,128)(2,1)S(1)} collective-permute-done((bf16[15,160,128]{2,1,0:T(8,128)(2,1)S(1)}, bf16[15,160,128]{2,1,0:T(8,128)(2,1)S(1)}, u32[]{:S(2)}, u32[]{:S(2)}) %collective-permute-start.12) | collective-permute-done | bytes 614432 | tf_op jit(solution)/shard_map/ppermute | solution.py:806
  155.1 5.6 %collective-permute-done.13.refs_5_ = bf16[15,160,128]{2,1,0:T(8,128)(2,1)S(1)} collective-permute-done((bf16[15,160,128]{2,1,0:T(8,128)(2,1)S(1)}, bf16[15,160,128]{2,1,0:T(8,128)(2,1)S(1)}, u32[]{:S(2)}, u32[]{:S(2)}) %collective-permute-start.13) | collective-permute-done | bytes 614432 | tf_op jit(solution)/shard_map/ppermute | solution.py:806
  160.7 13.8 %backward_last.1 = (bf16[32,128,128]{2,1,0:T(8,128)(2,1)}, f32[3,128,128]{2,1,0:T(8,128)S(1)}) custom-call(s32[4]{0:T(128)S(1)} %add_convert_fusion.refs_0_, bf16[32,128,128]{2,1,0:T(8,128)(2,1)S(1)} %get-tuple-element.95.pre.refs_1_, bf16[48,16,128]{2,1,0:T(8,128)(2,1)S(1)} %collective-permute-done.10.from_left.refs_2_, ...), custom_call_target="tpu_custom_call" | custom-call | flops 1146880000 | bytes 14680064 | tf_op jit(solution)/shard_map/backward_last/pallas_call | solution.py:788
  174.8 25.2 %all_to_all.12 = bf16[9,128,128]{2,0,1:T(8,128)(2,1)S(1)} all-to-all(bf16[9,128,128]{2,0,1:T(8,128)(2,1)S(1)} %copy.26), channel_id=1, replica_groups=mesh['rows'=32,'cols'=4] {'rows'}, dimensions={1} | all-to-all | bytes 589824 | tf_op jit(solution)/shard_map/all_to_all | solution.py:855
  200.2 6.3 %all_gather.7 = bf16[4,9,512]{2,1,0:T(8,128)(2,1)S(1)} all-gather(bf16[1,9,512]{2,1,0:T(8,128)(2,1)S(1)} %all_gather.6), channel_id=1, replica_groups=mesh['rows'=32,'cols'=4] {'cols'}, dimensions={0}, use_global_device_ids=true | all-gather | bytes 46080 | tf_op jit(solution)/shard_map/all_gather | solution.py:857
  (106 shorter events, 25.2 us)
Async XLA Ops:
  1.8 10.1 %collective-permute-start.1 = (bf16[32,32,128]{2,1,0:T(8,128)(2,1)S(1)}, bf16[32,32,128]{2,1,0:T(8,128)(2,1)S(1)}, u32[]{:S(2)}, u32[]{:S(2)}) collective-permute-start(bf16[32,32,128]{2,1,0:T(8,128)(2,1)S(1)} %get-tuple-element.117), channel_id=1, source_target_pairs={{1,0},{2,1},{3,2},{5,4},{6,5},{7,6},{9,8},{10,9},{11,10},{13,12},{... | collective-permute-start | bytes 786440 | tf_op jit(solution)/shard_map/ppermute | solution.py:806
  5.2 7.9 %collective-permute-start = (bf16[32,32,128]{2,1,0:T(8,128)(2,1)S(1)}, bf16[32,32,128]{2,1,0:T(8,128)(2,1)S(1)}, u32[]{:S(2)}, u32[]{:S(2)}) collective-permute-start(bf16[32,32,128]{2,1,0:T(8,128)(2,1)S(1)} %get-tuple-element.118), channel_id=1, source_target_pairs={{0,1},{1,2},{2,3},{4,5},{5,6},{6,7},{8,9},{9,10},{10,11},{12,13},{... | collective-permute-start | bytes 786440 | tf_op jit(solution)/shard_map/ppermute | solution.py:806
  13.2 17.9 %collective-permute-start.2 = (bf16[15,192,128]{2,1,0:T(8,128)(2,1)S(1)}, bf16[15,192,128]{2,1,0:T(8,128)(2,1)S(1)}, u32[]{:S(2)}, u32[]{:S(2)}) collective-permute-start(bf16[15,192,128]{2,1,0:T(8,128)(2,1)S(1)} %pad_maximum_fusion), channel_id=1, source_target_pairs={{0,4},{4,8},{8,12},{12,16},{16,20},{20,24},{24,28},{28,32},{32,36}... | collective-permute-start | bytes 2211848 | tf_op jit(solution)/shard_map/ppermute | solution.py:806
  16.8 16.6 %collective-permute-start.3 = (bf16[15,192,128]{2,1,0:T(8,128)(2,1)S(1)}, bf16[15,192,128]{2,1,0:T(8,128)(2,1)S(1)}, u32[]{:S(2)}, u32[]{:S(2)}) collective-permute-start(bf16[15,192,128]{2,1,0:T(8,128)(2,1)S(1)} %pad_maximum_fusion.1), channel_id=1, source_target_pairs={{4,0},{8,4},{12,8},{16,12},{20,16},{24,20},{28,24},{32,28},{36,32}... | collective-permute-start | bytes 2211848 | tf_op jit(solution)/shard_map/ppermute | solution.py:806
  50.6 17.2 %collective-permute-start.4 = (bf16[15,160,128]{2,1,0:T(8,128)(2,1)S(1)}, bf16[15,160,128]{2,1,0:T(8,128)(2,1)S(1)}, u32[]{:S(2)}, u32[]{:S(2)}) collective-permute-start(bf16[15,160,128]{2,1,0:T(8,128)(2,1)S(1)} %get-tuple-element.69), channel_id=1, source_target_pairs={{0,4},{4,8},{8,12},{12,16},{16,20},{20,24},{24,28},{28,32},{32,36}... | collective-permute-start | bytes 1843208 | tf_op jit(solution)/shard_map/ppermute | solution.py:806
  53.8 14.2 %collective-permute-start.5 = (bf16[15,160,128]{2,1,0:T(8,128)(2,1)S(1)}, bf16[15,160,128]{2,1,0:T(8,128)(2,1)S(1)}, u32[]{:S(2)}, u32[]{:S(2)}) collective-permute-start(bf16[15,160,128]{2,1,0:T(8,128)(2,1)S(1)} %get-tuple-element.70), channel_id=1, source_target_pairs={{4,0},{8,4},{12,8},{16,12},{20,16},{24,20},{28,24},{32,28},{36,32}... | collective-permute-start | bytes 1843208 | tf_op jit(solution)/shard_map/ppermute | solution.py:806
  68.0 29.1 %copy-start.17 = (bf16[32,128,128]{2,1,0:T(8,128)(2,1)S(1)}, bf16[32,128,128]{2,1,0:T(8,128)(2,1)}, u32[]{:S(2)}) copy-start(bf16[32,128,128]{2,1,0:T(8,128)(2,1)} %base.3) | copy-start | bytes 3145732
  68.0 49.3 %copy-start.19 = (bf16[32,128,128]{2,1,0:T(8,128)(2,1)S(1)}, bf16[32,128,128]{2,1,0:T(8,128)(2,1)}, u32[]{:S(2)}) copy-start(bf16[32,128,128]{2,1,0:T(8,128)(2,1)} %get-tuple-element.90.refs_12_) | copy-start | bytes 3145732
  83.6 21.9 %slice-start = ((bf16[8,128,128]{2,1,0:T(8,128)(2,1)}), bf16[1,128,128]{2,1,0:T(8,128)(2,1)S(1)}, s32[]{:S(2)}) async-start(bf16[8,128,128]{2,1,0:T(8,128)(2,1)} %param.8), calls=%async_computation.1 | async-start | bytes 65536 | tf_op jit(solution)/shard_map/slice | solution.py:840
  83.6 7.5 %collective-permute-start.6 = (bf16[48,16,128]{2,1,0:T(8,128)(2,1)S(1)}, bf16[48,16,128]{2,1,0:T(8,128)(2,1)S(1)}, u32[]{:S(2)}, u32[]{:S(2)}) collective-permute-start(bf16[48,16,128]{2,1,0:T(8,128)(2,1)S(1)} %get-tuple-element.83), channel_id=1, source_target_pairs={{0,1},{1,2},{2,3},{4,5},{5,6},{6,7},{8,9},{9,10},{10,11},{12,13},{... | collective-permute-start | bytes 589832 | tf_op jit(solution)/shard_map/ppermute | solution.py:806
  88.6 8.5 %collective-permute-start.7 = (bf16[48,16,128]{2,1,0:T(8,128)(2,1)S(1)}, bf16[48,16,128]{2,1,0:T(8,128)(2,1)S(1)}, u32[]{:S(2)}, u32[]{:S(2)}) collective-permute-start(bf16[48,16,128]{2,1,0:T(8,128)(2,1)S(1)} %get-tuple-element.84), channel_id=1, source_target_pairs={{1,0},{2,1},{3,2},{5,4},{6,5},{7,6},{9,8},{10,9},{11,10},{13,12},{... | collective-permute-start | bytes 589832 | tf_op jit(solution)/shard_map/ppermute | solution.py:806
  98.3 19.0 %copy-start.15 = (bf16[32,128,128]{2,1,0:T(8,128)(2,1)S(1)}, bf16[32,128,128]{2,1,0:T(8,128)(2,1)}, u32[]{:S(2)}) copy-start(bf16[32,128,128]{2,1,0:T(8,128)(2,1)} %get-tuple-element.92.refs_14_) | copy-start | bytes 3145732
  98.3 19.0 %copy-start.16 = (bf16[32,128,128]{2,1,0:T(8,128)(2,1)S(1)}, bf16[32,128,128]{2,1,0:T(8,128)(2,1)}, u32[]{:S(2)}) copy-start(bf16[32,128,128]{2,1,0:T(8,128)(2,1)} %get-tuple-element.91.refs_13_) | copy-start | bytes 3145732
  98.3 19.0 %copy-start.18 = (bf16[32,128,128]{2,1,0:T(8,128)(2,1)S(1)}, bf16[32,128,128]{2,1,0:T(8,128)(2,1)}, u32[]{:S(2)}) copy-start(bf16[32,128,128]{2,1,0:T(8,128)(2,1)} %get-tuple-element.94.refs_16_) | copy-start | bytes 3145732
  99.1 14.0 %collective-permute-start.8 = (bf16[15,160,128]{2,1,0:T(8,128)(2,1)S(1)}, bf16[15,160,128]{2,1,0:T(8,128)(2,1)S(1)}, u32[]{:S(2)}, u32[]{:S(2)}) collective-permute-start(bf16[15,160,128]{2,1,0:T(8,128)(2,1)S(1)} %get-tuple-element.85), channel_id=1, source_target_pairs={{0,4},{4,8},{8,12},{12,16},{16,20},{20,24},{24,28},{28,32},{32,36}... | collective-permute-start | bytes 1843208 | tf_op jit(solution)/shard_map/ppermute | solution.py:806
  104.2 13.1 %collective-permute-start.9 = (bf16[15,160,128]{2,1,0:T(8,128)(2,1)S(1)}, bf16[15,160,128]{2,1,0:T(8,128)(2,1)S(1)}, u32[]{:S(2)}, u32[]{:S(2)}) collective-permute-start(bf16[15,160,128]{2,1,0:T(8,128)(2,1)S(1)} %get-tuple-element.86), channel_id=1, source_target_pairs={{4,0},{8,4},{12,8},{16,12},{20,16},{24,20},{28,24},{32,28},{36,32}... | collective-permute-start | bytes 1843208 | tf_op jit(solution)/shard_map/ppermute | solution.py:806
  130.8 4.5 %collective-permute-start.10 = (bf16[48,16,128]{2,1,0:T(8,128)(2,1)S(1)}, bf16[48,16,128]{2,1,0:T(8,128)(2,1)S(1)}, u32[]{:S(2)}, u32[]{:S(2)}) collective-permute-start(bf16[48,16,128]{2,1,0:T(8,128)(2,1)S(1)} %get-tuple-element.96), channel_id=1, source_target_pairs={{0,1},{1,2},{2,3},{4,5},{5,6},{6,7},{8,9},{9,10},{10,11},{12,13},{... | collective-permute-start | bytes 589832 | tf_op jit(solution)/shard_map/ppermute | solution.py:806
  132.7 8.5 %collective-permute-start.11 = (bf16[48,16,128]{2,1,0:T(8,128)(2,1)S(1)}, bf16[48,16,128]{2,1,0:T(8,128)(2,1)S(1)}, u32[]{:S(2)}, u32[]{:S(2)}) collective-permute-start(bf16[48,16,128]{2,1,0:T(8,128)(2,1)S(1)} %get-tuple-element.97), channel_id=1, source_target_pairs={{1,0},{2,1},{3,2},{5,4},{6,5},{7,6},{9,8},{10,9},{11,10},{13,12},{... | collective-permute-start | bytes 589832 | tf_op jit(solution)/shard_map/ppermute | solution.py:806
  142.0 13.0 %collective-permute-start.12 = (bf16[15,160,128]{2,1,0:T(8,128)(2,1)S(1)}, bf16[15,160,128]{2,1,0:T(8,128)(2,1)S(1)}, u32[]{:S(2)}, u32[]{:S(2)}) collective-permute-start(bf16[15,160,128]{2,1,0:T(8,128)(2,1)S(1)} %get-tuple-element.99), channel_id=1, source_target_pairs={{0,4},{4,8},{8,12},{12,16},{16,20},{20,24},{24,28},{28,32},{32,36}... | collective-permute-start | bytes 1843208 | tf_op jit(solution)/shard_map/ppermute | solution.py:806
  145.6 15.0 %collective-permute-start.13 = (bf16[15,160,128]{2,1,0:T(8,128)(2,1)S(1)}, bf16[15,160,128]{2,1,0:T(8,128)(2,1)S(1)}, u32[]{:S(2)}, u32[]{:S(2)}) collective-permute-start(bf16[15,160,128]{2,1,0:T(8,128)(2,1)S(1)} %get-tuple-element.100), channel_id=1, source_target_pairs={{4,0},{8,4},{12,8},{16,12},{20,16},{24,20},{28,24},{32,28},{36,32}... | collective-permute-start | bytes 1843208 | tf_op jit(solution)/shard_map/ppermute | solution.py:806
  147.0 13.7 %copy-start.10 = (bf16[32,128,128]{2,1,0:T(8,128)(2,1)S(1)}, bf16[32,128,128]{2,1,0:T(8,128)(2,1)}, u32[]{:S(2)}) copy-start(bf16[32,128,128]{2,1,0:T(8,128)(2,1)} %get-tuple-element.107.refs_13_) | copy-start | bytes 3145732
  148.7 12.0 %copy-start.2 = (bf16[48,144,128]{2,1,0:T(8,128)(2,1)S(1)}, bf16[48,144,128]{2,1,0:T(8,128)(2,1)}, u32[]{:S(2)}) copy-start(bf16[48,144,128]{2,1,0:T(8,128)(2,1)} %get-tuple-element.104.refs_10_) | copy-start | bytes 5308420
  148.7 11.9 %copy-start.5 = (bf16[38,160,128]{2,1,0:T(8,128)(2,1)S(1)}, bf16[38,160,128]{2,1,0:T(8,128)(2,1)}, u32[]{:S(2)}) copy-start(bf16[38,160,128]{2,1,0:T(8,128)(2,1)} %get-tuple-element.105.refs_11_) | copy-start | bytes 4669444
  148.7 11.9 %copy-start.6 = (bf16[36,160,128]{2,1,0:T(8,128)(2,1)S(1)}, bf16[36,160,128]{2,1,0:T(8,128)(2,1)}, u32[]{:S(2)}) copy-start(bf16[36,160,128]{2,1,0:T(8,128)(2,1)} %get-tuple-element.106.refs_12_) | copy-start | bytes 4423684
  (19 other events, 130.6 us)

commit v5 on v4

--- a/solution.py
+++ b/solution.py
@@ -155,7 +155,8 @@
     edges = take(1)[0]
     pieces = take(1 if seg else 3)
     kernels, weights = take(2)
-    hid_out, slope_out, x_out = take(3), take(3), take(3)
+    hid_out, slope_out, x_all = take(3), take(3), take(1)[0]
+    x_out = [x_all.at[pl.ds(o, n)] for o, n in ((0, 8), (8, 16), (24, 18))]
     x_bufs, h_bufs, slopes = take(4), take(3), take(3)
     hid_two, sem = take(2)
 
@@ -176,17 +177,18 @@
         low, high = SPANS[seg][layer]
         edge = INNER[layer]
         first, number = edge + 1, ROWS - 2 - 2 * edge
+        group = (5, 2, 6)[layer]
         taps = rows_of(kernels[layer], 0.5)
         hid_own = hid_two if layer == 2 else None
 
         def body(it, _):
+            at = group * it
             act_rows(
-                src, taps, seg, layer, first + 2 * it, 2, True,
-                h_buf, 2 * it, slope_buf, 2 * it, hid_own,
+                src, taps, seg, layer, first + at, group, True, h_buf, at, slope_buf, at, hid_own
             )
             return 0
 
-        lax.fori_loop(0, number // 2, body, 0)
+        lax.fori_loop(0, number // group, body, 0)
         rows = pl.ds(first, number)
         hid_src = hid_two if layer == 2 else h_buf.at[:, pl.ds(SIDES[seg] - low, COLS)]
         send(hid_src, hid_out[layer].at[rows], layer)
@@ -225,7 +227,7 @@
 def inner(seg, edges, pieces, kernels, weights):
     outs = [sds((ROWS, COLS, CH), BF)] * 3
     outs += [sds(s, BF) for s in SLOPE_SHAPES[:3]]
-    outs += [sds((n, x_wide(seg), CH), F32) for n in (8, 16, 18)]
+    outs += [sds((42, x_wide(seg), CH), F32)]
     numbers = [ROWS - 2 - 2 * e for e in INNER]
     breadth = [b - a for a, b in SPANS[seg]]
     scratch = [pltpu.VMEM((ROWS + 2 * RH, x_wide(seg), CH), F32)] * 4
@@ -236,7 +238,7 @@
         functools.partial(inner_kernel, seg),
         out_shape=outs,
         in_specs=[SMEM] + [VMEM] * (2 + len(pieces)),
-        out_specs=[ANY] * 9,
+        out_specs=[ANY] * 7,
         scratch_shapes=scratch,
         compiler_params=pltpu.CompilerParams(vmem_limit_bytes=52 * 2**20),
         cost_estimate=pl.CostEstimate(
@@ -254,7 +256,8 @@
     top, bottom, kernels, weights = take(4)
     if seg:
         cot = take(1)[0]
-    x_in = take(3)
+    x_all = take(1)[0]
+    x_in = [x_all.at[pl.ds(o, n)] for o, n in ((0, 8), (8, 16), (24, 18))]
     take(6)
     if seg:
         out, pre, strip_left, strip_right, grad = take(5)
@@ -442,7 +445,7 @@
     return pl.pallas_call(
         functools.partial(outer_kernel, seg),
         out_shape=outs,
-        in_specs=[SMEM] + [VMEM] * (len(args) - 10) + [ANY] * 9,
+        in_specs=[SMEM] + [VMEM] * (len(args) - 8) + [ANY] * 7,
         out_specs=specs,
         scratch_shapes=scratch,
         input_output_aliases={len(args) - 6 + k: shift + k for k in range(6)},
@@ -620,11 +623,12 @@
         back = take(1)[0]
     part_in = take(1)[0]
     slope_in = take(count)
-    hid_in = take(count)
     if last:
+        hid_in = take(count)
         out, grads = take(2)
     else:
-        up_out, pre_out, strip_left, strip_right, grads = take(5)
+        up_out, pre_out, strip_left, strip_right = take(4)
+        held_out = take(count)
     buf, ups = take(2)
     slopes = take(count)
     hids = take(count)
@@ -632,14 +636,14 @@
 
     copies = []
     for k in range(count):
-        copies.append(
-            (
-                pltpu.make_async_copy(slope_in[k], slopes[k], sem.at[2 * k]),
-                pltpu.make_async_copy(hid_in[k], hids[k], sem.at[2 * k + 1]),
-            )
-        )
+        copies.append([pltpu.make_async_copy(slope_in[k], slopes[k], sem.at[2 * k])])
+        if last:
+            copies[-1].append(pltpu.make_async_copy(hid_in[k], hids[k], sem.at[2 * k + 1]))
+        else:
+            copies[-1].append(pltpu.make_async_copy(hids[k], held_out[k], sem.at[2 * k + 1]))
         copies[-1][0].start()
-        copies[-1][1].start()
+        if last:
+            copies[-1][1].start()
 
     part_copy = pltpu.make_async_copy(
         part_in, ups.at[pl.ds(UHALO, ROWS)], sem.at[2 * count]
@@ -699,7 +703,8 @@
         dilate = 2**layer
         halo = (1, 3, 7)[layer]
         copies[k][0].wait()
-        copies[k][1].wait()
+        if last:
+            copies[k][1].wait()
         step = (ROWS + 2 * halo) // 2
         skip = DHALO[layer] - halo
 
@@ -727,8 +732,14 @@
         total = jnp.zeros((CH, CH), F32)
         for b in range(2):
             up = ups[UHALO + 16 * b : UHALO + 16 * b + 16, 8:136].astype(BF)
-            total = total + grad_of(hids[k][16 * b : 16 * b + 16], up)
-        grads[k] = total
+            if last:
+                total = total + grad_of(hids[k][16 * b : 16 * b + 16], up)
+            else:
+                hids[k][16 * b : 16 * b + 16] = up
+        if last:
+            grads[k] = total
+        else:
+            copies[k][1].start()
 
         taps = rows_of(kernels[layer], 1.0)
         reach = (0, 1, 3)[layer]
@@ -750,15 +761,13 @@
 
     if not last:
         copies[3][0].wait()
-        copies[3][1].wait()
-        total = jnp.zeros((CH, CH), F32)
         edge_cols = []
         for b in range(2):
             rows = slice(16 * b, 16 * b + 16)
             value = ups[UHALO + 16 * b : UHALO + 16 * b + 16, 8:136]
             up_out[rows] = value
             up = value.astype(BF)
-            total = total + grad_of(hids[3][rows], up)
+            hids[3][rows] = up
             pulled = pull_back(up, weights[3])
             value = (pulled.reshape(16, COLS, CH) * slopes[3][rows].astype(F32)).astype(BF)
             pre_out[rows] = value
@@ -766,30 +775,32 @@
             strip_right[rows] = value[:, COLS - CHALO :]
             edge_cols.append(ups[UHALO + 16 * b : UHALO + 16 * b + 16, 8:136])
         pack_edges(strip_left, strip_right, edge_cols)
-        grads[3] = total
-
-
-def backward(last, edges, pre, sides, part, ends_in, kernels, weights, slopes, hids, back=()):
+        copies[3][1].start()
+        for k in range(count):
+            copies[k][1].wait()
+
+
+def backward(last, edges, pre, sides, part, ends_in, kernels, weights, slopes, hids=(), back=()):
     count = len(slopes)
     block = sds((ROWS, COLS, CH), BF)
     if last:
         outs = [block, sds((count, CH, CH), F32)]
     else:
         strip = sds((ROWS + 16, CHALO, CH), BF)
-        outs = [sds((ROWS, COLS, CH), F32), block, strip, strip, sds((count, CH, CH), F32)]
+        outs = [sds((ROWS, COLS, CH), F32), block, strip, strip] + [block] * count
     scratch = [
         pltpu.VMEM((ROWS + 16, WIDE, CH), F32),
         pltpu.VMEM((ROWS + 2 * UHALO, UWIDE, CH), F32),
     ]
     scratch += [pltpu.VMEM(a.shape, BF) for a in slopes]
-    scratch += [pltpu.VMEM(a.shape, BF) for a in hids]
+    scratch += [pltpu.VMEM((ROWS, COLS, CH), BF)] * count
     scratch += [pltpu.SemaphoreType.DMA((2 * count + 1,))]
     args = (edges, pre, *sides, *ends_in, kernels, weights, *back)
     return pl.pallas_call(
         functools.partial(backward_kernel, last),
         out_shape=outs,
-        in_specs=[SMEM] + [VMEM] * (len(args) - 1) + [ANY] * (1 + 2 * count),
-        out_specs=[VMEM] * len(outs),
+        in_specs=[SMEM] + [VMEM] * (len(args) - 1) + [ANY] * (1 + count + len(hids)),
+        out_specs=[VMEM] * len(outs) if last else [VMEM] * 4 + [ANY] * count,
         scratch_shapes=scratch,
         compiler_params=pltpu.CompilerParams(vmem_limit_bytes=30 * 2**20),
         cost_estimate=pl.CostEstimate(
@@ -797,6 +808,40 @@
         ),
         name="backward_last" if last else "backward_first",
     )(*args, part, *slopes, *hids)
+
+
+def late_kernel(*refs):
+    count = (len(refs) - 2) // 4
+    ins, grads = refs[: 2 * count], refs[2 * count]
+    bufs, sem = refs[2 * count + 1 : -1], refs[-1]
+    copies = [pltpu.make_async_copy(a, b, sem.at[k]) for k, (a, b) in enumerate(zip(ins, bufs))]
+    for copy in copies:
+        copy.start()
+    for k in range(count):
+        copies[2 * k].wait()
+        copies[2 * k + 1].wait()
+        total = jnp.zeros((CH, CH), F32)
+        for b in range(2):
+            rows = slice(16 * b, 16 * b + 16)
+            total = total + grad_of(bufs[2 * k][rows], bufs[2 * k + 1][rows])
+        grads[k] = total
+
+
+def late_grads(hids, held):
+    args = [a for pair in zip(hids, held) for a in pair]
+    return pl.pallas_call(
+        late_kernel,
+        out_shape=sds((len(hids), CH, CH), F32),
+        in_specs=[ANY] * len(args),
+        out_specs=VMEM,
+        scratch_shapes=[pltpu.VMEM((ROWS, COLS, CH), BF)] * len(args)
+        + [pltpu.SemaphoreType.DMA((len(args),))],
+        compiler_params=pltpu.CompilerParams(vmem_limit_bytes=20 * 2**20),
+        cost_estimate=pl.CostEstimate(
+            flops=4 * 2 * 4096 * CH * CH, bytes_accessed=8 * 2**20, transcendentals=0
+        ),
+        name="late_grads",
+    )(*args)
 
 
 def exchange(to_before, to_after, axis):
@@ -835,15 +880,16 @@
     sides = exchange(strip_left, strip_right, "cols")
     rows_in = exchange(*ends(pre, *sides, cotangent, kernels[7]), "rows")
     part = own_part(pre, *sides, cotangent, kernels[7])
-    upstream, pre, strip_left, strip_right, grad_mid = backward(
+    upstream, pre, strip_left, strip_right, *held = backward(
         False, edges, pre, sides, part, rows_in,
         kernels[4:], jnp.concatenate([point_weights[4:7], point_weights[3:4]]),
-        order(slope_high) + [slope_low[3]], order(hid_high) + [hid_low[3]],
+        order(slope_high) + [slope_low[3]],
     )
     sides = exchange(strip_left, strip_right, "cols")
     rows_in = exchange(*ends(pre, *sides, upstream, kernels[3]), "rows")
     output, back, coarse_grad = pool(features_in, cotangent, x_last, coarse_weight)
-    later, back = lax.optimization_barrier((upstream, back))
+    grad_mid = late_grads(order(hid_high) + [hid_low[3]], held)
+    later, back, grad_mid = lax.optimization_barrier((upstream, back, grad_mid))
     part = own_part(pre, *sides, later, kernels[3])
     input_grad, grad_low = backward(
         True, edges, pre, sides, part, rows_in,

time: 208 us -> 205 us (0.986)
  waiting for transfers between devices: 38.8 us -> 36.5 us
    ppermute x7, waiting for transfers between devices: 12.8 us -> 9.68 us  [exchange(): lax.ppermute(to_after, axis, forth)]
    pallas_call x0 -> x1, Pallas kernels: none -> 2.55 us  [late_grads(): pl.pallas_call(late_kernel, out_shape=sds((len(hids), CH, CH), F32), in_s...]
    unnamed x63 -> x61, local copies, waits for them, and re-layouts: 5.01 us -> 4.68 us
  transfers between devices with their start and end apart: 14 -> 14, of which waited for: 12 -> 12; matrix products, arithmetic and copies ran while one was open for 0% -> 0% of each run, Pallas kernels for 13% -> 14%
where the time goes in v5:
time: 205 us; the launch traced here: 204 us
  Pallas kernels  88.3 us (43%)
  starting transfers between devices  39 us (19%)
  waiting for transfers between devices  36.5 us (18%)
  blocking collectives  31.5 us (15%)
  local copies, waits for them, and re-layouts  6.89 us (3%)
    pallas_call x2, Pallas kernels, outer(): pl.pallas_call(functools.partial(outer_kernel, seg), out_shape=outs, in_s...  31.8 us
    ppermute x7, waiting for transfers between devices, exchange(): lax.ppermute(to_before, axis, back)  26.9 us
    ppermute x7, starting transfers between devices, exchange(): lax.ppermute(to_after, axis, forth)  26.2 us
    pallas_call x2, Pallas kernels, backward(): pl.pallas_call(functools.partial(backward_kernel, last), out_shape=outs,...  25.9 us
    all_to_all x1, blocking collectives, local(): shares = lax.all_to_all(grads, 'rows', 1, 0, tiled=True)  25.3 us
    pallas_call x2, Pallas kernels, inner(): pl.pallas_call(functools.partial(inner_kernel, seg), out_shape=outs, in_s...  21.7 us
    ppermute x7, starting transfers between devices, exchange(): lax.ppermute(to_before, axis, back)  12.8 us
    ppermute x7, waiting for transfers between devices, exchange(): lax.ppermute(to_after, axis, forth)  9.68 us
  transfers between devices with their start and end apart: 14, of which 12 were waited for; matrix products, arithmetic and copies ran while one was open for 0% of the time, Pallas kernels for 14%

profile of v5, /device:TPU:1, one launch (start us, length us, event | category | flops | bytes accessed | tf_op | source)
XLA Modules:
  0.0 203.8 jit_solution(12754980552306841281)
XLA Ops:
  1.8 3.3 %collective-permute-start.1 = (bf16[32,32,128]{2,1,0:T(8,128)(2,1)S(1)}, bf16[32,32,128]{2,1,0:T(8,128)(2,1)S(1)}, u32[]{:S(2)}, u32[]{:S(2)}) collective-permute-start(bf16[32,32,128]{2,1,0:T(8,128)(2,1)S(1)} %get-tuple-element.117), channel_id=1, source_target_pairs={{1,0},{2,1},{3,2},{5,4},{6,5},{7,6},{9,8},{10,9},{11,10},{13,12},{... | collective-permute-start | bytes 786440 | tf_op jit(solution)/shard_map/ppermute | solution.py:851
  5.2 4.6 %collective-permute-start = (bf16[32,32,128]{2,1,0:T(8,128)(2,1)S(1)}, bf16[32,32,128]{2,1,0:T(8,128)(2,1)S(1)}, u32[]{:S(2)}, u32[]{:S(2)}) collective-permute-start(bf16[32,32,128]{2,1,0:T(8,128)(2,1)S(1)} %get-tuple-element.118), channel_id=1, source_target_pairs={{0,1},{1,2},{2,3},{4,5},{5,6},{6,7},{8,9},{9,10},{10,11},{12,13},{... | collective-permute-start | bytes 786440 | tf_op jit(solution)/shard_map/ppermute | solution.py:851
  10.0 2.0 collective-permute-done.1.refs_3_
  13.2 3.6 %collective-permute-start.2 = (bf16[15,192,128]{2,1,0:T(8,128)(2,1)S(1)}, bf16[15,192,128]{2,1,0:T(8,128)(2,1)S(1)}, u32[]{:S(2)}, u32[]{:S(2)}) collective-permute-start(bf16[15,192,128]{2,1,0:T(8,128)(2,1)S(1)} %pad_maximum_fusion), channel_id=1, source_target_pairs={{0,4},{4,8},{8,12},{12,16},{16,20},{20,24},{24,28},{28,32},{32,36}... | collective-permute-start | bytes 2211848 | tf_op jit(solution)/shard_map/ppermute | solution.py:851
  18.3 11.4 %inner_first.1 = (bf16[32,128,128]{2,1,0:T(8,128)(2,1)S(1)}, bf16[32,128,128]{2,1,0:T(8,128)(2,1)}, bf16[32,128,128]{2,1,0:T(8,128)(2,1)}, bf16[36,160,128]{2,1,...) custom-call(s32[4]{0:T(128)S(1)} %add_convert_fusion.refs_0_, ...), custom_call_target="tpu_custom_call" | custom-call | flops 393216000 | bytes 12582912 | tf_op jit(solution)/shard_map/inner_first/pallas_call | solution.py:237
  30.7 2.7 %collective-permute-done.3.refs_5_ = bf16[15,192,128]{2,1,0:T(8,128)(2,1)S(1)} collective-permute-done((bf16[15,192,128]{2,1,0:T(8,128)(2,1)S(1)}, bf16[15,192,128]{2,1,0:T(8,128)(2,1)S(1)}, u32[]{:S(2)}, u32[]{:S(2)}) %collective-permute-start.3) | collective-permute-done | bytes 737312 | tf_op jit(solution)/shard_map/ppermute | solution.py:851
  34.3 16.2 %outer_first.1 = (bf16[32,160,128]{2,1,0:T(8,128)(2,1)}, bf16[15,160,128]{2,1,0:T(8,128)(2,1)S(1)}, bf16[15,160,128]{2,1,0:T(8,128)(2,1)S(1)}, bf16[32,128,128]{...) custom-call(s32[4]{0:T(128)S(1)} %add_convert_fusion.refs_0_, ...), custom_call_target="tpu_custom_call", output_to_operand_aliasing={{5}: (9, {}), {6}: (10, {}), {7}: (11, {}), {8}: (12, {}), ... | custom-call | flops 655360000 | bytes 12582912 | tf_op jit(solution)/shard_map/outer_first/pallas_call | solution.py:445
  50.5 3.2 %collective-permute-start.4 = (bf16[15,160,128]{2,1,0:T(8,128)(2,1)S(1)}, bf16[15,160,128]{2,1,0:T(8,128)(2,1)S(1)}, u32[]{:S(2)}, u32[]{:S(2)}) collective-permute-start(bf16[15,160,128]{2,1,0:T(8,128)(2,1)S(1)} %get-tuple-element.67), channel_id=1, source_target_pairs={{0,4},{4,8},{8,12},{12,16},{16,20},{20,24},{24,28},{28,32},{32,36}... | collective-permute-start | bytes 1843208 | tf_op jit(solution)/shard_map/ppermute | solution.py:851
  55.0 10.3 %inner_last.1 = (bf16[32,128,128]{2,1,0:T(8,128)(2,1)S(1)}, bf16[32,128,128]{2,1,0:T(8,128)(2,1)}, bf16[32,128,128]{2,1,0:T(8,128)(2,1)}, bf16[36,160,128]{2,1,0...) custom-call(s32[4]{0:T(128)S(1)} %add_convert_fusion.refs_0_, ...), custom_call_target="tpu_custom_call" | custom-call | flops 393216000 | bytes 12582912 | tf_op jit(solution)/shard_map/inner_last/pallas_call | solution.py:237
  67.9 15.5 %outer_last.1 = (bf16[32,128,128]{2,1,0:T(8,128)(2,1)}, bf16[32,128,128]{2,1,0:T(8,128)(2,1)}, bf16[48,16,128]{2,1,0:T(8,128)(2,1)S(1)}, bf16[48,16,128]{2,1,0:T...) custom-call(s32[4]{0:T(128)S(1)} %add_convert_fusion.refs_0_, ...), custom_call_target="tpu_custom_call", output_to_operand_aliasing={{5}: (8, {}), {6}: (9, {}), {7}: (10, {}), {8}: (11, {}), {... | custom-call | flops 655360000 | bytes 12582912 | tf_op jit(solution)/shard_map/outer_last/pallas_call | solution.py:445
  83.4 3.5 %collective-permute-start.6 = (bf16[48,16,128]{2,1,0:T(8,128)(2,1)S(1)}, bf16[48,16,128]{2,1,0:T(8,128)(2,1)S(1)}, u32[]{:S(2)}, u32[]{:S(2)}) collective-permute-start(bf16[48,16,128]{2,1,0:T(8,128)(2,1)S(1)} %get-tuple-element.79), channel_id=1, source_target_pairs={{0,1},{1,2},{2,3},{4,5},{5,6},{6,7},{8,9},{9,10},{10,11},{12,13},{... | collective-permute-start | bytes 589832 | tf_op jit(solution)/shard_map/ppermute | solution.py:851
  89.5 5.9 %collective-permute-done.7.from_right.refs_3_ = bf16[48,16,128]{2,1,0:T(8,128)(2,1)S(1)} collective-permute-done((bf16[48,16,128]{2,1,0:T(8,128)(2,1)S(1)}, bf16[48,16,128]{2,1,0:T(8,128)(2,1)S(1)}, u32[]{:S(2)}, u32[]{:S(2)}) %collective-permute-start.7) | collective-permute-done | bytes 196640 | tf_op jit(solution)/shard_map/ppermute | solution.py:851
  97.5 4.7 %collective-permute-start.8 = (bf16[15,160,128]{2,1,0:T(8,128)(2,1)S(1)}, bf16[15,160,128]{2,1,0:T(8,128)(2,1)S(1)}, u32[]{:S(2)}, u32[]{:S(2)}) collective-permute-start(bf16[15,160,128]{2,1,0:T(8,128)(2,1)S(1)} %get-tuple-element.81), channel_id=1, source_target_pairs={{0,4},{4,8},{8,12},{12,16},{16,20},{20,24},{24,28},{28,32},{32,36}... | collective-permute-start | bytes 1843208 | tf_op jit(solution)/shard_map/ppermute | solution.py:851
  105.1 6.0 %collective-permute-done.8.refs_4_ = bf16[15,160,128]{2,1,0:T(8,128)(2,1)S(1)} collective-permute-done((bf16[15,160,128]{2,1,0:T(8,128)(2,1)S(1)}, bf16[15,160,128]{2,1,0:T(8,128)(2,1)S(1)}, u32[]{:S(2)}, u32[]{:S(2)}) %collective-permute-start.8) | collective-permute-done | bytes 614432 | tf_op jit(solution)/shard_map/ppermute | solution.py:851
  111.1 4.1 %collective-permute-done.9.refs_5_ = bf16[15,160,128]{2,1,0:T(8,128)(2,1)S(1)} collective-permute-done((bf16[15,160,128]{2,1,0:T(8,128)(2,1)S(1)}, bf16[15,160,128]{2,1,0:T(8,128)(2,1)S(1)}, u32[]{:S(2)}, u32[]{:S(2)}) %collective-permute-start.9) | collective-permute-done | bytes 614432 | tf_op jit(solution)/shard_map/ppermute | solution.py:851
  115.3 12.1 %backward_first.1 = (f32[32,128,128]{2,1,0:T(8,128)S(1)}, bf16[32,128,128]{2,1,0:T(8,128)(2,1)S(1)}, bf16[48,16,128]{2,1,0:T(8,128)(2,1)S(1)}, bf16[48,16,128]{2...) custom-call(s32[4]{0:T(128)S(1)} %add_convert_fusion.refs_0_, ...), custom_call_target="tpu_custom_call" | custom-call | flops 1146880000 | bytes 14680064 | tf_op jit(solution)/shard_map/backward_first/pallas_call | solution.py:799
  129.3 2.4 %collective-permute-start.11 = (bf16[48,16,128]{2,1,0:T(8,128)(2,1)S(1)}, bf16[48,16,128]{2,1,0:T(8,128)(2,1)S(1)}, u32[]{:S(2)}, u32[]{:S(2)}) collective-permute-start(bf16[48,16,128]{2,1,0:T(8,128)(2,1)S(1)} %get-tuple-element.89), channel_id=1, source_target_pairs={{1,0},{2,1},{3,2},{5,4},{6,5},{7,6},{9,8},{10,9},{11,10},{13,12},{... | collective-permute-start | bytes 589832 | tf_op jit(solution)/shard_map/ppermute | solution.py:851
  131.9 5.9 %collective-permute-done.11.from_right.refs_3_ = bf16[48,16,128]{2,1,0:T(8,128)(2,1)S(1)} collective-permute-done((bf16[48,16,128]{2,1,0:T(8,128)(2,1)S(1)}, bf16[48,16,128]{2,1,0:T(8,128)(2,1)S(1)}, u32[]{:S(2)}, u32[]{:S(2)}) %collective-permute-start.11) | collective-permute-done | bytes 196640 | tf_op jit(solution)/shard_map/ppermute | solution.py:851
  138.6 4.7 %collective-permute-start.12 = (bf16[15,160,128]{2,1,0:T(8,128)(2,1)S(1)}, bf16[15,160,128]{2,1,0:T(8,128)(2,1)S(1)}, u32[]{:S(2)}, u32[]{:S(2)}) collective-permute-start(bf16[15,160,128]{2,1,0:T(8,128)(2,1)S(1)} %get-tuple-element.91), channel_id=1, source_target_pairs={{0,4},{4,8},{8,12},{12,16},{16,20},{20,24},{24,28},{28,32},{32,36}... | collective-permute-start | bytes 1843208 | tf_op jit(solution)/shard_map/ppermute | solution.py:851
  146.8 2.6 %late_grads.1 = f32[4,128,128]{2,1,0:T(8,128)S(1)} custom-call(bf16[32,128,128]{2,1,0:T(8,128)(2,1)S(1)} %copy-done.17, bf16[32,128,128]{2,1,0:T(8,128)(2,1)S(1)} %get-tuple-element.95.refs_1_, bf16[32,128,128]{2,1,0:T(8,128)(2,1)S(1)} %copy-done.16, bf16[32,128,128]{2,1,0:T(8,128)(2,1)S(1)} %get-tuple-element.97.refs_3_, ...), custom_call_target="tpu_custom_call" | custom-call | flops 536870912 | bytes 8388608 | tf_op jit(solution)/shard_map/late_grads/pallas_call | solution.py:832
  152.7 4.7 %collective-permute-done.13.refs_5_ = bf16[15,160,128]{2,1,0:T(8,128)(2,1)S(1)} collective-permute-done((bf16[15,160,128]{2,1,0:T(8,128)(2,1)S(1)}, bf16[15,160,128]{2,1,0:T(8,128)(2,1)S(1)}, u32[]{:S(2)}, u32[]{:S(2)}) %collective-permute-start.13) | collective-permute-done | bytes 614432 | tf_op jit(solution)/shard_map/ppermute | solution.py:851
  157.4 13.8 %backward_last.1 = (bf16[32,128,128]{2,1,0:T(8,128)(2,1)}, f32[3,128,128]{2,1,0:T(8,128)S(1)}) custom-call(s32[4]{0:T(128)S(1)} %add_convert_fusion.refs_0_, bf16[32,128,128]{2,1,0:T(8,128)(2,1)S(1)} %get-tuple-element.87.pre.refs_1_, bf16[48,16,128]{2,1,0:T(8,128)(2,1)S(1)} %collective-permute-done.10.from_left.refs_2_, ...), custom_call_target="tpu_custom_call" | custom-call | flops 1146880000 | bytes 14680064 | tf_op jit(solution)/shard_map/backward_last/pallas_call | solution.py:799
  171.6 25.3 %all_to_all.12 = bf16[9,128,128]{2,0,1:T(8,128)(2,1)S(1)} all-to-all(bf16[9,128,128]{2,0,1:T(8,128)(2,1)S(1)} %copy.26), channel_id=1, replica_groups=mesh['rows'=32,'cols'=4] {'rows'}, dimensions={1} | all-to-all | bytes 589824 | tf_op jit(solution)/shard_map/all_to_all | solution.py:901
  197.0 6.2 %all_gather.7 = bf16[4,9,512]{2,1,0:T(8,128)(2,1)S(1)} all-gather(bf16[1,9,512]{2,1,0:T(8,128)(2,1)S(1)} %all_gather.6), channel_id=1, replica_groups=mesh['rows'=32,'cols'=4] {'cols'}, dimensions={0}, use_global_device_ids=true | all-gather | bytes 46080 | tf_op jit(solution)/shard_map/all_gather | solution.py:903
  (105 shorter events, 27.9 us)
Async XLA Ops:
  0.6 9.2 %copy-start = (bf16[32,128,128]{2,1,0:T(8,128)(2,1)S(1)}, bf16[32,128,128]{2,1,0:T(8,128)(2,1)}, u32[]{:S(2)}) copy-start(bf16[32,128,128]{2,1,0:T(8,128)(2,1)} %feature.1) | copy-start | bytes 3145732
  0.6 9.3 %copy-start.26 = (bf16[8,9,128]{2,0,1:T(8,128)(2,1)S(1)}, bf16[8,9,128]{2,0,1:T(8,128)(2,1)}, u32[]{:S(2)}) copy-start(bf16[8,9,128]{2,0,1:T(8,128)(2,1)} %param.7) | copy-start | bytes 55300
  1.8 10.1 %collective-permute-start.1 = (bf16[32,32,128]{2,1,0:T(8,128)(2,1)S(1)}, bf16[32,32,128]{2,1,0:T(8,128)(2,1)S(1)}, u32[]{:S(2)}, u32[]{:S(2)}) collective-permute-start(bf16[32,32,128]{2,1,0:T(8,128)(2,1)S(1)} %get-tuple-element.117), channel_id=1, source_target_pairs={{1,0},{2,1},{3,2},{5,4},{6,5},{7,6},{9,8},{10,9},{11,10},{13,12},{... | collective-permute-start | bytes 786440 | tf_op jit(solution)/shard_map/ppermute | solution.py:851
  5.2 7.9 %collective-permute-start = (bf16[32,32,128]{2,1,0:T(8,128)(2,1)S(1)}, bf16[32,32,128]{2,1,0:T(8,128)(2,1)S(1)}, u32[]{:S(2)}, u32[]{:S(2)}) collective-permute-start(bf16[32,32,128]{2,1,0:T(8,128)(2,1)S(1)} %get-tuple-element.118), channel_id=1, source_target_pairs={{0,1},{1,2},{2,3},{4,5},{5,6},{6,7},{8,9},{9,10},{10,11},{12,13},{... | collective-permute-start | bytes 786440 | tf_op jit(solution)/shard_map/ppermute | solution.py:851
  13.2 17.5 %collective-permute-start.2 = (bf16[15,192,128]{2,1,0:T(8,128)(2,1)S(1)}, bf16[15,192,128]{2,1,0:T(8,128)(2,1)S(1)}, u32[]{:S(2)}, u32[]{:S(2)}) collective-permute-start(bf16[15,192,128]{2,1,0:T(8,128)(2,1)S(1)} %pad_maximum_fusion), channel_id=1, source_target_pairs={{0,4},{4,8},{8,12},{12,16},{16,20},{20,24},{24,28},{28,32},{32,36}... | collective-permute-start | bytes 2211848 | tf_op jit(solution)/shard_map/ppermute | solution.py:851
  16.8 16.6 %collective-permute-start.3 = (bf16[15,192,128]{2,1,0:T(8,128)(2,1)S(1)}, bf16[15,192,128]{2,1,0:T(8,128)(2,1)S(1)}, u32[]{:S(2)}, u32[]{:S(2)}) collective-permute-start(bf16[15,192,128]{2,1,0:T(8,128)(2,1)S(1)} %pad_maximum_fusion.1), channel_id=1, source_target_pairs={{4,0},{8,4},{12,8},{16,12},{20,16},{24,20},{28,24},{32,28},{36,32}... | collective-permute-start | bytes 2211848 | tf_op jit(solution)/shard_map/ppermute | solution.py:851
  50.5 15.8 %collective-permute-start.4 = (bf16[15,160,128]{2,1,0:T(8,128)(2,1)S(1)}, bf16[15,160,128]{2,1,0:T(8,128)(2,1)S(1)}, u32[]{:S(2)}, u32[]{:S(2)}) collective-permute-start(bf16[15,160,128]{2,1,0:T(8,128)(2,1)S(1)} %get-tuple-element.67), channel_id=1, source_target_pairs={{0,4},{4,8},{8,12},{12,16},{16,20},{20,24},{24,28},{28,32},{32,36}... | collective-permute-start | bytes 1843208 | tf_op jit(solution)/shard_map/ppermute | solution.py:851
  53.7 14.2 %collective-permute-start.5 = (bf16[15,160,128]{2,1,0:T(8,128)(2,1)S(1)}, bf16[15,160,128]{2,1,0:T(8,128)(2,1)S(1)}, u32[]{:S(2)}, u32[]{:S(2)}) collective-permute-start(bf16[15,160,128]{2,1,0:T(8,128)(2,1)S(1)} %get-tuple-element.68), channel_id=1, source_target_pairs={{4,0},{8,4},{12,8},{16,12},{20,16},{24,20},{28,24},{32,28},{36,32}... | collective-permute-start | bytes 1843208 | tf_op jit(solution)/shard_map/ppermute | solution.py:851
  67.9 27.5 %copy-start.18 = (bf16[32,128,128]{2,1,0:T(8,128)(2,1)S(1)}, bf16[32,128,128]{2,1,0:T(8,128)(2,1)}, u32[]{:S(2)}) copy-start(bf16[32,128,128]{2,1,0:T(8,128)(2,1)} %base.3) | copy-start | bytes 3145732
  83.4 20.0 %slice-start = ((bf16[8,128,128]{2,1,0:T(8,128)(2,1)}), bf16[1,128,128]{2,1,0:T(8,128)(2,1)S(1)}, s32[]{:S(2)}) async-start(bf16[8,128,128]{2,1,0:T(8,128)(2,1)} %param.8), calls=%async_computation.1 | async-start | bytes 65536 | tf_op jit(solution)/shard_map/slice | solution.py:885
  83.4 6.1 %collective-permute-start.6 = (bf16[48,16,128]{2,1,0:T(8,128)(2,1)S(1)}, bf16[48,16,128]{2,1,0:T(8,128)(2,1)S(1)}, u32[]{:S(2)}, u32[]{:S(2)}) collective-permute-start(bf16[48,16,128]{2,1,0:T(8,128)(2,1)S(1)} %get-tuple-element.79), channel_id=1, source_target_pairs={{0,1},{1,2},{2,3},{4,5},{5,6},{6,7},{8,9},{9,10},{10,11},{12,13},{... | collective-permute-start | bytes 589832 | tf_op jit(solution)/shard_map/ppermute | solution.py:851
  86.9 8.5 %collective-permute-start.7 = (bf16[48,16,128]{2,1,0:T(8,128)(2,1)S(1)}, bf16[48,16,128]{2,1,0:T(8,128)(2,1)S(1)}, u32[]{:S(2)}, u32[]{:S(2)}) collective-permute-start(bf16[48,16,128]{2,1,0:T(8,128)(2,1)S(1)} %get-tuple-element.80), channel_id=1, source_target_pairs={{1,0},{2,1},{3,2},{5,4},{6,5},{7,6},{9,8},{10,9},{11,10},{13,12},{... | collective-permute-start | bytes 589832 | tf_op jit(solution)/shard_map/ppermute | solution.py:851
  97.5 13.6 %collective-permute-start.8 = (bf16[15,160,128]{2,1,0:T(8,128)(2,1)S(1)}, bf16[15,160,128]{2,1,0:T(8,128)(2,1)S(1)}, u32[]{:S(2)}, u32[]{:S(2)}) collective-permute-start(bf16[15,160,128]{2,1,0:T(8,128)(2,1)S(1)} %get-tuple-element.81), channel_id=1, source_target_pairs={{0,4},{4,8},{8,12},{12,16},{16,20},{20,24},{24,28},{28,32},{32,36}... | collective-permute-start | bytes 1843208 | tf_op jit(solution)/shard_map/ppermute | solution.py:851
  102.2 13.1 %collective-permute-start.9 = (bf16[15,160,128]{2,1,0:T(8,128)(2,1)S(1)}, bf16[15,160,128]{2,1,0:T(8,128)(2,1)S(1)}, u32[]{:S(2)}, u32[]{:S(2)}) collective-permute-start(bf16[15,160,128]{2,1,0:T(8,128)(2,1)S(1)} %get-tuple-element.82), channel_id=1, source_target_pairs={{4,0},{8,4},{12,8},{16,12},{20,16},{24,20},{28,24},{32,28},{36,32}... | collective-permute-start | bytes 1843208 | tf_op jit(solution)/shard_map/ppermute | solution.py:851
  103.5 11.7 %copy-start.3 = (bf16[48,144,128]{2,1,0:T(8,128)(2,1)S(1)}, bf16[48,144,128]{2,1,0:T(8,128)(2,1)}, u32[]{:S(2)}) copy-start(bf16[48,144,128]{2,1,0:T(8,128)(2,1)} %get-tuple-element.83.refs_9_) | copy-start | bytes 5308420
  103.5 11.7 %copy-start.5 = (bf16[38,160,128]{2,1,0:T(8,128)(2,1)S(1)}, bf16[38,160,128]{2,1,0:T(8,128)(2,1)}, u32[]{:S(2)}) copy-start(bf16[38,160,128]{2,1,0:T(8,128)(2,1)} %get-tuple-element.84.refs_10_) | copy-start | bytes 4669444
  103.5 11.7 %copy-start.7 = (bf16[36,160,128]{2,1,0:T(8,128)(2,1)S(1)}, bf16[36,160,128]{2,1,0:T(8,128)(2,1)}, u32[]{:S(2)}) copy-start(bf16[36,160,128]{2,1,0:T(8,128)(2,1)} %get-tuple-element.85.refs_11_) | copy-start | bytes 4423684
  103.5 11.7 %copy-start.13 = (bf16[32,128,128]{2,1,0:T(8,128)(2,1)S(1)}, bf16[32,128,128]{2,1,0:T(8,128)(2,1)}, u32[]{:S(2)}) copy-start(bf16[32,128,128]{2,1,0:T(8,128)(2,1)} %get-tuple-element.78.pre.refs_1_) | copy-start | bytes 3145732
  103.5 11.7 %copy-start.20 = (bf16[32,128,128]{2,1,0:T(8,128)(2,1)S(1)}, bf16[32,128,128]{2,1,0:T(8,128)(2,1)}, u32[]{:S(2)}) copy-start(bf16[32,128,128]{2,1,0:T(8,128)(2,1)} %get-tuple-element.86.refs_12_) | copy-start | bytes 3145732
  127.3 4.5 %collective-permute-start.10 = (bf16[48,16,128]{2,1,0:T(8,128)(2,1)S(1)}, bf16[48,16,128]{2,1,0:T(8,128)(2,1)S(1)}, u32[]{:S(2)}, u32[]{:S(2)}) collective-permute-start(bf16[48,16,128]{2,1,0:T(8,128)(2,1)S(1)} %get-tuple-element.88), channel_id=1, source_target_pairs={{0,1},{1,2},{2,3},{4,5},{5,6},{6,7},{8,9},{9,10},{10,11},{12,13},{... | collective-permute-start | bytes 589832 | tf_op jit(solution)/shard_map/ppermute | solution.py:851
  129.3 8.5 %collective-permute-start.11 = (bf16[48,16,128]{2,1,0:T(8,128)(2,1)S(1)}, bf16[48,16,128]{2,1,0:T(8,128)(2,1)S(1)}, u32[]{:S(2)}, u32[]{:S(2)}) collective-permute-start(bf16[48,16,128]{2,1,0:T(8,128)(2,1)S(1)} %get-tuple-element.89), channel_id=1, source_target_pairs={{1,0},{2,1},{3,2},{5,4},{6,5},{7,6},{9,8},{10,9},{11,10},{13,12},{... | collective-permute-start | bytes 589832 | tf_op jit(solution)/shard_map/ppermute | solution.py:851
  138.6 14.1 %collective-permute-start.12 = (bf16[15,160,128]{2,1,0:T(8,128)(2,1)S(1)}, bf16[15,160,128]{2,1,0:T(8,128)(2,1)S(1)}, u32[]{:S(2)}, u32[]{:S(2)}) collective-permute-start(bf16[15,160,128]{2,1,0:T(8,128)(2,1)S(1)} %get-tuple-element.91), channel_id=1, source_target_pairs={{0,4},{4,8},{8,12},{12,16},{16,20},{20,24},{24,28},{28,32},{32,36}... | collective-permute-start | bytes 1843208 | tf_op jit(solution)/shard_map/ppermute | solution.py:851
  143.2 14.1 %collective-permute-start.13 = (bf16[15,160,128]{2,1,0:T(8,128)(2,1)S(1)}, bf16[15,160,128]{2,1,0:T(8,128)(2,1)S(1)}, u32[]{:S(2)}, u32[]{:S(2)}) collective-permute-start(bf16[15,160,128]{2,1,0:T(8,128)(2,1)S(1)} %get-tuple-element.92), channel_id=1, source_target_pairs={{4,0},{8,4},{12,8},{16,12},{20,16},{24,20},{28,24},{32,28},{36,32}... | collective-permute-start | bytes 1843208 | tf_op jit(solution)/shard_map/ppermute | solution.py:851
  146.8 10.6 %copy-start.11 = (bf16[32,128,128]{2,1,0:T(8,128)(2,1)S(1)}, bf16[32,128,128]{2,1,0:T(8,128)(2,1)}, u32[]{:S(2)}) copy-start(bf16[32,128,128]{2,1,0:T(8,128)(2,1)} %get-tuple-element.107.refs_13_) | copy-start | bytes 3145732
  (18 other events, 86.3 us)

commit v6 on v5

--- a/solution.py
+++ b/solution.py
@@ -260,7 +260,7 @@
     x_in = [x_all.at[pl.ds(o, n)] for o, n in ((0, 8), (8, 16), (24, 18))]
     take(6)
     if seg:
-        out, pre, strip_left, strip_right, grad = take(5)
+        out, pre, strip_left, strip_right, hid_three = take(5)
     else:
         x_out, up_out, down_out, hid_three, slope_three = take(5)
     hid_out, slope_out = take(3), take(3)
@@ -366,7 +366,9 @@
         return 0
 
     lax.fori_loop(0, ROWS // 4, last_body, 0)
-    if not seg:
+    if seg:
+        send(h_bufs[3], hid_three, 12)
+    else:
         send(h_bufs[3].at[:, pl.ds(CHALO, COLS)], hid_three, 12)
         send(slopes[3], slope_three, 13)
 
@@ -379,12 +381,10 @@
     lax.fori_loop(0, 2, last_mix, 0)
     if seg:
         send(own_buf, out, 14)
-        total = jnp.zeros((CH, CH), F32)
         edge_cols = []
         for b in range(2):
             rows = slice(16 * b, 16 * b + 16)
             up = cot[rows]
-            total = total + grad_of(h_bufs[3][rows], up)
             pulled = pull_back(up, weights[3])
             value = pulled.reshape(16, COLS, CH) * slopes[3][rows].astype(F32)
             value = value.astype(BF)
@@ -393,7 +393,6 @@
             strip_right[rows] = value[:, COLS - CHALO :]
             edge_cols.append(up.astype(F32))
         pack_edges(strip_left, strip_right, edge_cols)
-        grad[...] = total
     else:
         zeros = jnp.zeros((ROWS, CHALO, CH), BF)
 
@@ -424,8 +423,8 @@
     block = sds((ROWS, COLS, CH), BF)
     strip = sds((ROWS + 16, CHALO, CH), BF)
     if seg:
-        outs = [block, block, strip, strip, sds((CH, CH), F32)]
-        specs = [ANY] + [VMEM] * 4
+        outs = [block, block, strip, strip, block]
+        specs = [ANY] + [VMEM] * 3 + [ANY]
     else:
         ends_shape = sds((RH, WIDE, CH), BF)
         outs = [sds((ROWS, WIDE, CH), BF), ends_shape, ends_shape, block, block]
@@ -838,7 +837,7 @@
         + [pltpu.SemaphoreType.DMA((len(args),))],
         compiler_params=pltpu.CompilerParams(vmem_limit_bytes=20 * 2**20),
         cost_estimate=pl.CostEstimate(
-            flops=4 * 2 * 4096 * CH * CH, bytes_accessed=8 * 2**20, transcendentals=0
+            flops=5 * 2 * 4096 * CH * CH, bytes_accessed=8 * 2**20, transcendentals=0
         ),
         name="late_grads",
     )(*args)
@@ -870,7 +869,7 @@
     hid_low, slope_low = kept[:3] + [hid_three], kept[3:] + [slope_three]
     top, bottom = exchange(x_up, x_down, "rows")
     begun = inner(1, edges, (x_mid,), kernels[4:7], point_weights[4:7])
-    x_last, pre, strip_left, strip_right, grad_top, *kept = outer(
+    x_last, pre, strip_left, strip_right, hid_top, *kept = outer(
         1, edges, (x_mid,), top, bottom, kernels[4:], point_weights[4:], begun,
         (cotangent,),
     )
@@ -888,7 +887,9 @@
     sides = exchange(strip_left, strip_right, "cols")
     rows_in = exchange(*ends(pre, *sides, upstream, kernels[3]), "rows")
     output, back, coarse_grad = pool(features_in, cotangent, x_last, coarse_weight)
-    grad_mid = late_grads(order(hid_high) + [hid_low[3]], held)
+    grad_mid = late_grads(
+        order(hid_high) + [hid_low[3], hid_top], list(held) + [cotangent]
+    )
     later, back, grad_mid = lax.optimization_barrier((upstream, back, grad_mid))
     part = own_part(pre, *sides, later, kernels[3])
     input_grad, grad_low = backward(
@@ -897,7 +898,7 @@
     )
 
     grads = [grad_low[2], grad_low[1], grad_low[0], grad_mid[3], grad_mid[2], grad_mid[1]]
-    grads = jnp.stack(grads + [grad_mid[0], grad_top, coarse_grad]).astype(BF)
+    grads = jnp.stack(grads + [grad_mid[0], grad_mid[4], coarse_grad]).astype(BF)
     shares = lax.all_to_all(grads, "rows", 1, 0, tiled=True)
     summed = shares.reshape(-1, grads.shape[0], CH * 4).astype(F32).sum(axis=0)
     parts = lax.all_gather(summed.astype(BF), "cols", axis=0, tiled=False)

time: 205 us -> 205 us (level)
    unnamed x61 -> x64, local copies, waits for them, and re-layouts: 4.68 us -> 4.7 us
  transfers between devices with their start and end apart: 14 -> 14, of which waited for: 12 -> 12; matrix products, arithmetic and copies ran while one was open for 0% -> 0% of each run, Pallas kernels for 14% -> 15%
where the time goes in v6:
time: 205 us; the launch traced here: 204 us
  Pallas kernels  88.9 us (43%)
  starting transfers between devices  39 us (19%)
  waiting for transfers between devices  35.9 us (18%)
  blocking collectives  31.5 us (15%)
  local copies, waits for them, and re-layouts  6.91 us (3%)
    pallas_call x2, Pallas kernels, outer(): pl.pallas_call(functools.partial(outer_kernel, seg), out_shape=outs, in_s...  31.8 us
    ppermute x7, waiting for transfers between devices, exchange(): lax.ppermute(to_before, axis, back)  26.9 us
    ppermute x7, starting transfers between devices, exchange(): lax.ppermute(to_after, axis, forth)  26.2 us
    pallas_call x2, Pallas kernels, backward(): pl.pallas_call(functools.partial(backward_kernel, last), out_shape=outs,...  25.8 us
    all_to_all x1, blocking collectives, local(): shares = lax.all_to_all(grads, 'rows', 1, 0, tiled=True)  25.2 us
    pallas_call x2, Pallas kernels, inner(): pl.pallas_call(functools.partial(inner_kernel, seg), out_shape=outs, in_s...  21.7 us
    ppermute x7, starting transfers between devices, exchange(): lax.ppermute(to_before, axis, back)  12.8 us
    ppermute x7, waiting for transfers between devices, exchange(): lax.ppermute(to_after, axis, forth)  9.04 us
  transfers between devices with their start and end apart: 14, of which 12 were waited for; matrix products, arithmetic and copies ran while one was open for 0% of the time, Pallas kernels for 15%

profile of v6, /device:TPU:1, one launch (start us, length us, event | category | flops | bytes accessed | tf_op | source)
XLA Modules:
  0.0 203.9 jit_solution(3047385616759320372)
XLA Ops:
  1.8 3.3 %collective-permute-start.1 = (bf16[32,32,128]{2,1,0:T(8,128)(2,1)S(1)}, bf16[32,32,128]{2,1,0:T(8,128)(2,1)S(1)}, u32[]{:S(2)}, u32[]{:S(2)}) collective-permute-start(bf16[32,32,128]{2,1,0:T(8,128)(2,1)S(1)} %get-tuple-element.117), channel_id=1, source_target_pairs={{1,0},{2,1},{3,2},{5,4},{6,5},{7,6},{9,8},{10,9},{11,10},{13,12},{... | collective-permute-start | bytes 786440 | tf_op jit(solution)/shard_map/ppermute | solution.py:850
  5.2 4.6 %collective-permute-start = (bf16[32,32,128]{2,1,0:T(8,128)(2,1)S(1)}, bf16[32,32,128]{2,1,0:T(8,128)(2,1)S(1)}, u32[]{:S(2)}, u32[]{:S(2)}) collective-permute-start(bf16[32,32,128]{2,1,0:T(8,128)(2,1)S(1)} %get-tuple-element.118), channel_id=1, source_target_pairs={{0,1},{1,2},{2,3},{4,5},{5,6},{6,7},{8,9},{9,10},{10,11},{12,13},{... | collective-permute-start | bytes 786440 | tf_op jit(solution)/shard_map/ppermute | solution.py:850
  10.0 2.0 collective-permute-done.1.refs_3_
  13.2 3.6 %collective-permute-start.2 = (bf16[15,192,128]{2,1,0:T(8,128)(2,1)S(1)}, bf16[15,192,128]{2,1,0:T(8,128)(2,1)S(1)}, u32[]{:S(2)}, u32[]{:S(2)}) collective-permute-start(bf16[15,192,128]{2,1,0:T(8,128)(2,1)S(1)} %pad_maximum_fusion), channel_id=1, source_target_pairs={{0,4},{4,8},{8,12},{12,16},{16,20},{20,24},{24,28},{28,32},{32,36}... | collective-permute-start | bytes 2211848 | tf_op jit(solution)/shard_map/ppermute | solution.py:850
  18.3 11.4 %inner_first.1 = (bf16[32,128,128]{2,1,0:T(8,128)(2,1)S(1)}, bf16[32,128,128]{2,1,0:T(8,128)(2,1)}, bf16[32,128,128]{2,1,0:T(8,128)(2,1)}, bf16[36,160,128]{2,1,...) custom-call(s32[4]{0:T(128)S(1)} %add_convert_fusion.refs_0_, ...), custom_call_target="tpu_custom_call" | custom-call | flops 393216000 | bytes 12582912 | tf_op jit(solution)/shard_map/inner_first/pallas_call | solution.py:237
  30.7 2.7 %collective-permute-done.3.refs_5_ = bf16[15,192,128]{2,1,0:T(8,128)(2,1)S(1)} collective-permute-done((bf16[15,192,128]{2,1,0:T(8,128)(2,1)S(1)}, bf16[15,192,128]{2,1,0:T(8,128)(2,1)S(1)}, u32[]{:S(2)}, u32[]{:S(2)}) %collective-permute-start.3) | collective-permute-done | bytes 737312 | tf_op jit(solution)/shard_map/ppermute | solution.py:850
  34.3 16.2 %outer_first.1 = (bf16[32,160,128]{2,1,0:T(8,128)(2,1)}, bf16[15,160,128]{2,1,0:T(8,128)(2,1)S(1)}, bf16[15,160,128]{2,1,0:T(8,128)(2,1)S(1)}, bf16[32,128,128]{...) custom-call(s32[4]{0:T(128)S(1)} %add_convert_fusion.refs_0_, ...), custom_call_target="tpu_custom_call", output_to_operand_aliasing={{5}: (9, {}), {6}: (10, {}), {7}: (11, {}), {8}: (12, {}), ... | custom-call | flops 655360000 | bytes 12582912 | tf_op jit(solution)/shard_map/outer_first/pallas_call | solution.py:444
  50.5 3.2 %collective-permute-start.4 = (bf16[15,160,128]{2,1,0:T(8,128)(2,1)S(1)}, bf16[15,160,128]{2,1,0:T(8,128)(2,1)S(1)}, u32[]{:S(2)}, u32[]{:S(2)}) collective-permute-start(bf16[15,160,128]{2,1,0:T(8,128)(2,1)S(1)} %get-tuple-element.67), channel_id=1, source_target_pairs={{0,4},{4,8},{8,12},{12,16},{16,20},{20,24},{24,28},{28,32},{32,36}... | collective-permute-start | bytes 1843208 | tf_op jit(solution)/shard_map/ppermute | solution.py:850
  55.0 10.3 %inner_last.1 = (bf16[32,128,128]{2,1,0:T(8,128)(2,1)S(1)}, bf16[32,128,128]{2,1,0:T(8,128)(2,1)}, bf16[32,128,128]{2,1,0:T(8,128)(2,1)}, bf16[36,160,128]{2,1,0...) custom-call(s32[4]{0:T(128)S(1)} %add_convert_fusion.refs_0_, ...), custom_call_target="tpu_custom_call" | custom-call | flops 393216000 | bytes 12582912 | tf_op jit(solution)/shard_map/inner_last/pallas_call | solution.py:237
  67.9 15.5 %outer_last.1 = (bf16[32,128,128]{2,1,0:T(8,128)(2,1)}, bf16[32,128,128]{2,1,0:T(8,128)(2,1)}, bf16[48,16,128]{2,1,0:T(8,128)(2,1)S(1)}, bf16[48,16,128]{2,1,0:T...) custom-call(s32[4]{0:T(128)S(1)} %add_convert_fusion.refs_0_, ...), custom_call_target="tpu_custom_call", output_to_operand_aliasing={{5}: (8, {}), {6}: (9, {}), {7}: (10, {}), {8}: (11, {}), {... | custom-call | flops 655360000 | bytes 12582912 | tf_op jit(solution)/shard_map/outer_last/pallas_call | solution.py:444
  83.4 3.5 %collective-permute-start.6 = (bf16[48,16,128]{2,1,0:T(8,128)(2,1)S(1)}, bf16[48,16,128]{2,1,0:T(8,128)(2,1)S(1)}, u32[]{:S(2)}, u32[]{:S(2)}) collective-permute-start(bf16[48,16,128]{2,1,0:T(8,128)(2,1)S(1)} %get-tuple-element.79), channel_id=1, source_target_pairs={{0,1},{1,2},{2,3},{4,5},{5,6},{6,7},{8,9},{9,10},{10,11},{12,13},{... | collective-permute-start | bytes 589832 | tf_op jit(solution)/shard_map/ppermute | solution.py:850
  89.5 5.9 %collective-permute-done.7.from_right.refs_3_ = bf16[48,16,128]{2,1,0:T(8,128)(2,1)S(1)} collective-permute-done((bf16[48,16,128]{2,1,0:T(8,128)(2,1)S(1)}, bf16[48,16,128]{2,1,0:T(8,128)(2,1)S(1)}, u32[]{:S(2)}, u32[]{:S(2)}) %collective-permute-start.7) | collective-permute-done | bytes 196640 | tf_op jit(solution)/shard_map/ppermute | solution.py:850
  97.5 4.7 %collective-permute-start.8 = (bf16[15,160,128]{2,1,0:T(8,128)(2,1)S(1)}, bf16[15,160,128]{2,1,0:T(8,128)(2,1)S(1)}, u32[]{:S(2)}, u32[]{:S(2)}) collective-permute-start(bf16[15,160,128]{2,1,0:T(8,128)(2,1)S(1)} %get-tuple-element.81), channel_id=1, source_target_pairs={{0,4},{4,8},{8,12},{12,16},{16,20},{20,24},{24,28},{28,32},{32,36}... | collective-permute-start | bytes 1843208 | tf_op jit(solution)/shard_map/ppermute | solution.py:850
  105.1 6.0 %collective-permute-done.8.refs_4_ = bf16[15,160,128]{2,1,0:T(8,128)(2,1)S(1)} collective-permute-done((bf16[15,160,128]{2,1,0:T(8,128)(2,1)S(1)}, bf16[15,160,128]{2,1,0:T(8,128)(2,1)S(1)}, u32[]{:S(2)}, u32[]{:S(2)}) %collective-permute-start.8) | collective-permute-done | bytes 614432 | tf_op jit(solution)/shard_map/ppermute | solution.py:850
  111.1 4.1 %collective-permute-done.9.refs_5_ = bf16[15,160,128]{2,1,0:T(8,128)(2,1)S(1)} collective-permute-done((bf16[15,160,128]{2,1,0:T(8,128)(2,1)S(1)}, bf16[15,160,128]{2,1,0:T(8,128)(2,1)S(1)}, u32[]{:S(2)}, u32[]{:S(2)}) %collective-permute-start.9) | collective-permute-done | bytes 614432 | tf_op jit(solution)/shard_map/ppermute | solution.py:850
  115.3 12.1 %backward_first.1 = (f32[32,128,128]{2,1,0:T(8,128)S(1)}, bf16[32,128,128]{2,1,0:T(8,128)(2,1)S(1)}, bf16[48,16,128]{2,1,0:T(8,128)(2,1)S(1)}, bf16[48,16,128]{2...) custom-call(s32[4]{0:T(128)S(1)} %add_convert_fusion.refs_0_, ...), custom_call_target="tpu_custom_call" | custom-call | flops 1146880000 | bytes 14680064 | tf_op jit(solution)/shard_map/backward_first/pallas_call | solution.py:798
  129.3 2.4 %collective-permute-start.11 = (bf16[48,16,128]{2,1,0:T(8,128)(2,1)S(1)}, bf16[48,16,128]{2,1,0:T(8,128)(2,1)S(1)}, u32[]{:S(2)}, u32[]{:S(2)}) collective-permute-start(bf16[48,16,128]{2,1,0:T(8,128)(2,1)S(1)} %get-tuple-element.89), channel_id=1, source_target_pairs={{1,0},{2,1},{3,2},{5,4},{6,5},{7,6},{9,8},{10,9},{11,10},{13,12},{... | collective-permute-start | bytes 589832 | tf_op jit(solution)/shard_map/ppermute | solution.py:850
  131.9 5.9 %collective-permute-done.11.from_right.refs_3_ = bf16[48,16,128]{2,1,0:T(8,128)(2,1)S(1)} collective-permute-done((bf16[48,16,128]{2,1,0:T(8,128)(2,1)S(1)}, bf16[48,16,128]{2,1,0:T(8,128)(2,1)S(1)}, u32[]{:S(2)}, u32[]{:S(2)}) %collective-permute-start.11) | collective-permute-done | bytes 196640 | tf_op jit(solution)/shard_map/ppermute | solution.py:850
  138.6 4.7 %collective-permute-start.12 = (bf16[15,160,128]{2,1,0:T(8,128)(2,1)S(1)}, bf16[15,160,128]{2,1,0:T(8,128)(2,1)S(1)}, u32[]{:S(2)}, u32[]{:S(2)}) collective-permute-start(bf16[15,160,128]{2,1,0:T(8,128)(2,1)S(1)} %get-tuple-element.91), channel_id=1, source_target_pairs={{0,4},{4,8},{8,12},{12,16},{16,20},{20,24},{24,28},{28,32},{32,36}... | collective-permute-start | bytes 1843208 | tf_op jit(solution)/shard_map/ppermute | solution.py:850
  146.8 3.2 %late_grads.1 = f32[5,128,128]{2,1,0:T(8,128)S(1)} custom-call(bf16[32,128,128]{2,1,0:T(8,128)(2,1)S(1)} %copy-done.18, bf16[32,128,128]{2,1,0:T(8,128)(2,1)S(1)} %get-tuple-element.95.refs_1_, bf16[32,128,128]{2,1,0:T(8,128)(2,1)S(1)} %copy-done.17, bf16[32,128,128]{2,1,0:T(8,128)(2,1)S(1)} %get-tuple-element.97.refs_3_, ...), custom_call_target="tpu_custom_call" | custom-call | flops 671088640 | bytes 8388608 | tf_op jit(solution)/shard_map/late_grads/pallas_call | solution.py:831
  152.7 4.7 %collective-permute-done.13.refs_5_ = bf16[15,160,128]{2,1,0:T(8,128)(2,1)S(1)} collective-permute-done((bf16[15,160,128]{2,1,0:T(8,128)(2,1)S(1)}, bf16[15,160,128]{2,1,0:T(8,128)(2,1)S(1)}, u32[]{:S(2)}, u32[]{:S(2)}) %collective-permute-start.13) | collective-permute-done | bytes 614432 | tf_op jit(solution)/shard_map/ppermute | solution.py:850
  157.5 13.8 %backward_last.1 = (bf16[32,128,128]{2,1,0:T(8,128)(2,1)}, f32[3,128,128]{2,1,0:T(8,128)S(1)}) custom-call(s32[4]{0:T(128)S(1)} %add_convert_fusion.refs_0_, bf16[32,128,128]{2,1,0:T(8,128)(2,1)S(1)} %get-tuple-element.87.pre.refs_1_, bf16[48,16,128]{2,1,0:T(8,128)(2,1)S(1)} %collective-permute-done.10.from_left.refs_2_, ...), custom_call_target="tpu_custom_call" | custom-call | flops 1146880000 | bytes 14680064 | tf_op jit(solution)/shard_map/backward_last/pallas_call | solution.py:798
  171.7 25.2 %all_to_all.12 = bf16[9,128,128]{2,0,1:T(8,128)(2,1)S(1)} all-to-all(bf16[9,128,128]{2,0,1:T(8,128)(2,1)S(1)} %copy.26), channel_id=1, replica_groups=mesh['rows'=32,'cols'=4] {'rows'}, dimensions={1} | all-to-all | bytes 589824 | tf_op jit(solution)/shard_map/all_to_all | solution.py:902
  197.0 6.2 %all_gather.7 = bf16[4,9,512]{2,1,0:T(8,128)(2,1)S(1)} all-gather(bf16[1,9,512]{2,1,0:T(8,128)(2,1)S(1)} %all_gather.6), channel_id=1, replica_groups=mesh['rows'=32,'cols'=4] {'cols'}, dimensions={0}, use_global_device_ids=true | all-gather | bytes 46080 | tf_op jit(solution)/shard_map/all_gather | solution.py:904
  (107 shorter events, 27.3 us)
Async XLA Ops:
  0.6 9.3 %copy-start.27 = (bf16[8,9,128]{2,0,1:T(8,128)(2,1)S(1)}, bf16[8,9,128]{2,0,1:T(8,128)(2,1)}, u32[]{:S(2)}) copy-start(bf16[8,9,128]{2,0,1:T(8,128)(2,1)} %param.7) | copy-start | bytes 55300
  1.8 10.1 %collective-permute-start.1 = (bf16[32,32,128]{2,1,0:T(8,128)(2,1)S(1)}, bf16[32,32,128]{2,1,0:T(8,128)(2,1)S(1)}, u32[]{:S(2)}, u32[]{:S(2)}) collective-permute-start(bf16[32,32,128]{2,1,0:T(8,128)(2,1)S(1)} %get-tuple-element.117), channel_id=1, source_target_pairs={{1,0},{2,1},{3,2},{5,4},{6,5},{7,6},{9,8},{10,9},{11,10},{13,12},{... | collective-permute-start | bytes 786440 | tf_op jit(solution)/shard_map/ppermute | solution.py:850
  5.2 7.9 %collective-permute-start = (bf16[32,32,128]{2,1,0:T(8,128)(2,1)S(1)}, bf16[32,32,128]{2,1,0:T(8,128)(2,1)S(1)}, u32[]{:S(2)}, u32[]{:S(2)}) collective-permute-start(bf16[32,32,128]{2,1,0:T(8,128)(2,1)S(1)} %get-tuple-element.118), channel_id=1, source_target_pairs={{0,1},{1,2},{2,3},{4,5},{5,6},{6,7},{8,9},{9,10},{10,11},{12,13},{... | collective-permute-start | bytes 786440 | tf_op jit(solution)/shard_map/ppermute | solution.py:850
  13.2 17.5 %collective-permute-start.2 = (bf16[15,192,128]{2,1,0:T(8,128)(2,1)S(1)}, bf16[15,192,128]{2,1,0:T(8,128)(2,1)S(1)}, u32[]{:S(2)}, u32[]{:S(2)}) collective-permute-start(bf16[15,192,128]{2,1,0:T(8,128)(2,1)S(1)} %pad_maximum_fusion), channel_id=1, source_target_pairs={{0,4},{4,8},{8,12},{12,16},{16,20},{20,24},{24,28},{28,32},{32,36}... | collective-permute-start | bytes 2211848 | tf_op jit(solution)/shard_map/ppermute | solution.py:850
  16.8 16.6 %collective-permute-start.3 = (bf16[15,192,128]{2,1,0:T(8,128)(2,1)S(1)}, bf16[15,192,128]{2,1,0:T(8,128)(2,1)S(1)}, u32[]{:S(2)}, u32[]{:S(2)}) collective-permute-start(bf16[15,192,128]{2,1,0:T(8,128)(2,1)S(1)} %pad_maximum_fusion.1), channel_id=1, source_target_pairs={{4,0},{8,4},{12,8},{16,12},{20,16},{24,20},{28,24},{32,28},{36,32}... | collective-permute-start | bytes 2211848 | tf_op jit(solution)/shard_map/ppermute | solution.py:850
  50.5 15.9 %collective-permute-start.4 = (bf16[15,160,128]{2,1,0:T(8,128)(2,1)S(1)}, bf16[15,160,128]{2,1,0:T(8,128)(2,1)S(1)}, u32[]{:S(2)}, u32[]{:S(2)}) collective-permute-start(bf16[15,160,128]{2,1,0:T(8,128)(2,1)S(1)} %get-tuple-element.67), channel_id=1, source_target_pairs={{0,4},{4,8},{8,12},{12,16},{16,20},{20,24},{24,28},{28,32},{32,36}... | collective-permute-start | bytes 1843208 | tf_op jit(solution)/shard_map/ppermute | solution.py:850
  53.7 14.2 %collective-permute-start.5 = (bf16[15,160,128]{2,1,0:T(8,128)(2,1)S(1)}, bf16[15,160,128]{2,1,0:T(8,128)(2,1)S(1)}, u32[]{:S(2)}, u32[]{:S(2)}) collective-permute-start(bf16[15,160,128]{2,1,0:T(8,128)(2,1)S(1)} %get-tuple-element.68), channel_id=1, source_target_pairs={{4,0},{8,4},{12,8},{16,12},{20,16},{24,20},{28,24},{32,28},{36,32}... | collective-permute-start | bytes 1843208 | tf_op jit(solution)/shard_map/ppermute | solution.py:850
  67.9 27.5 %copy-start.2 = (bf16[32,128,128]{2,1,0:T(8,128)(2,1)S(1)}, bf16[32,128,128]{2,1,0:T(8,128)(2,1)}, u32[]{:S(2)}) copy-start(bf16[32,128,128]{2,1,0:T(8,128)(2,1)} %refs_9_.1) | copy-start | bytes 3145732
  83.4 20.0 %slice-start = ((bf16[8,128,128]{2,1,0:T(8,128)(2,1)}), bf16[1,128,128]{2,1,0:T(8,128)(2,1)S(1)}, s32[]{:S(2)}) async-start(bf16[8,128,128]{2,1,0:T(8,128)(2,1)} %param.8), calls=%async_computation.1 | async-start | bytes 65536 | tf_op jit(solution)/shard_map/slice | solution.py:884
  83.4 6.1 %collective-permute-start.6 = (bf16[48,16,128]{2,1,0:T(8,128)(2,1)S(1)}, bf16[48,16,128]{2,1,0:T(8,128)(2,1)S(1)}, u32[]{:S(2)}, u32[]{:S(2)}) collective-permute-start(bf16[48,16,128]{2,1,0:T(8,128)(2,1)S(1)} %get-tuple-element.79), channel_id=1, source_target_pairs={{0,1},{1,2},{2,3},{4,5},{5,6},{6,7},{8,9},{9,10},{10,11},{12,13},{... | collective-permute-start | bytes 589832 | tf_op jit(solution)/shard_map/ppermute | solution.py:850
  86.9 8.5 %collective-permute-start.7 = (bf16[48,16,128]{2,1,0:T(8,128)(2,1)S(1)}, bf16[48,16,128]{2,1,0:T(8,128)(2,1)S(1)}, u32[]{:S(2)}, u32[]{:S(2)}) collective-permute-start(bf16[48,16,128]{2,1,0:T(8,128)(2,1)S(1)} %get-tuple-element.80), channel_id=1, source_target_pairs={{1,0},{2,1},{3,2},{5,4},{6,5},{7,6},{9,8},{10,9},{11,10},{13,12},{... | collective-permute-start | bytes 589832 | tf_op jit(solution)/shard_map/ppermute | solution.py:850
  97.5 13.6 %collective-permute-start.8 = (bf16[15,160,128]{2,1,0:T(8,128)(2,1)S(1)}, bf16[15,160,128]{2,1,0:T(8,128)(2,1)S(1)}, u32[]{:S(2)}, u32[]{:S(2)}) collective-permute-start(bf16[15,160,128]{2,1,0:T(8,128)(2,1)S(1)} %get-tuple-element.81), channel_id=1, source_target_pairs={{0,4},{4,8},{8,12},{12,16},{16,20},{20,24},{24,28},{28,32},{32,36}... | collective-permute-start | bytes 1843208 | tf_op jit(solution)/shard_map/ppermute | solution.py:850
  102.2 13.1 %collective-permute-start.9 = (bf16[15,160,128]{2,1,0:T(8,128)(2,1)S(1)}, bf16[15,160,128]{2,1,0:T(8,128)(2,1)S(1)}, u32[]{:S(2)}, u32[]{:S(2)}) collective-permute-start(bf16[15,160,128]{2,1,0:T(8,128)(2,1)S(1)} %get-tuple-element.82), channel_id=1, source_target_pairs={{4,0},{8,4},{12,8},{16,12},{20,16},{24,20},{28,24},{32,28},{36,32}... | collective-permute-start | bytes 1843208 | tf_op jit(solution)/shard_map/ppermute | solution.py:850
  103.5 11.7 %copy-start.4 = (bf16[48,144,128]{2,1,0:T(8,128)(2,1)S(1)}, bf16[48,144,128]{2,1,0:T(8,128)(2,1)}, u32[]{:S(2)}) copy-start(bf16[48,144,128]{2,1,0:T(8,128)(2,1)} %get-tuple-element.83.refs_9_) | copy-start | bytes 5308420
  103.5 11.7 %copy-start.6 = (bf16[38,160,128]{2,1,0:T(8,128)(2,1)S(1)}, bf16[38,160,128]{2,1,0:T(8,128)(2,1)}, u32[]{:S(2)}) copy-start(bf16[38,160,128]{2,1,0:T(8,128)(2,1)} %get-tuple-element.84.refs_10_) | copy-start | bytes 4669444
  103.5 11.7 %copy-start.8 = (bf16[36,160,128]{2,1,0:T(8,128)(2,1)S(1)}, bf16[36,160,128]{2,1,0:T(8,128)(2,1)}, u32[]{:S(2)}) copy-start(bf16[36,160,128]{2,1,0:T(8,128)(2,1)} %get-tuple-element.85.refs_11_) | copy-start | bytes 4423684
  103.5 11.7 %copy-start.14 = (bf16[32,128,128]{2,1,0:T(8,128)(2,1)S(1)}, bf16[32,128,128]{2,1,0:T(8,128)(2,1)}, u32[]{:S(2)}) copy-start(bf16[32,128,128]{2,1,0:T(8,128)(2,1)} %get-tuple-element.78.pre.refs_1_) | copy-start | bytes 3145732
  103.5 11.7 %copy-start.20 = (bf16[32,128,128]{2,1,0:T(8,128)(2,1)S(1)}, bf16[32,128,128]{2,1,0:T(8,128)(2,1)}, u32[]{:S(2)}) copy-start(bf16[32,128,128]{2,1,0:T(8,128)(2,1)} %get-tuple-element.86.refs_12_) | copy-start | bytes 3145732
  115.3 29.3 %copy-start.22 = (bf16[32,128,128]{2,1,0:T(8,128)(2,1)S(1)}, bf16[32,128,128]{2,1,0:T(8,128)(2,1)}, u32[]{:S(2)}) copy-start(bf16[32,128,128]{2,1,0:T(8,128)(2,1)} %get-tuple-element.76.x_last) | copy-start | bytes 3145732
  127.3 4.5 %collective-permute-start.10 = (bf16[48,16,128]{2,1,0:T(8,128)(2,1)S(1)}, bf16[48,16,128]{2,1,0:T(8,128)(2,1)S(1)}, u32[]{:S(2)}, u32[]{:S(2)}) collective-permute-start(bf16[48,16,128]{2,1,0:T(8,128)(2,1)S(1)} %get-tuple-element.88), channel_id=1, source_target_pairs={{0,1},{1,2},{2,3},{4,5},{5,6},{6,7},{8,9},{9,10},{10,11},{12,13},{... | collective-permute-start | bytes 589832 | tf_op jit(solution)/shard_map/ppermute | solution.py:850
  129.3 8.5 %collective-permute-start.11 = (bf16[48,16,128]{2,1,0:T(8,128)(2,1)S(1)}, bf16[48,16,128]{2,1,0:T(8,128)(2,1)S(1)}, u32[]{:S(2)}, u32[]{:S(2)}) collective-permute-start(bf16[48,16,128]{2,1,0:T(8,128)(2,1)S(1)} %get-tuple-element.89), channel_id=1, source_target_pairs={{1,0},{2,1},{3,2},{5,4},{6,5},{7,6},{9,8},{10,9},{11,10},{13,12},{... | collective-permute-start | bytes 589832 | tf_op jit(solution)/shard_map/ppermute | solution.py:850
  138.6 14.1 %collective-permute-start.12 = (bf16[15,160,128]{2,1,0:T(8,128)(2,1)S(1)}, bf16[15,160,128]{2,1,0:T(8,128)(2,1)S(1)}, u32[]{:S(2)}, u32[]{:S(2)}) collective-permute-start(bf16[15,160,128]{2,1,0:T(8,128)(2,1)S(1)} %get-tuple-element.91), channel_id=1, source_target_pairs={{0,4},{4,8},{8,12},{12,16},{16,20},{20,24},{24,28},{28,32},{32,36}... | collective-permute-start | bytes 1843208 | tf_op jit(solution)/shard_map/ppermute | solution.py:850
  143.2 14.2 %collective-permute-start.13 = (bf16[15,160,128]{2,1,0:T(8,128)(2,1)S(1)}, bf16[15,160,128]{2,1,0:T(8,128)(2,1)S(1)}, u32[]{:S(2)}, u32[]{:S(2)}) collective-permute-start(bf16[15,160,128]{2,1,0:T(8,128)(2,1)S(1)} %get-tuple-element.92), channel_id=1, source_target_pairs={{4,0},{8,4},{12,8},{16,12},{20,16},{24,20},{28,24},{32,28},{36,32}... | collective-permute-start | bytes 1843208 | tf_op jit(solution)/shard_map/ppermute | solution.py:850
  146.8 10.6 %copy-start.12 = (bf16[32,128,128]{2,1,0:T(8,128)(2,1)S(1)}, bf16[32,128,128]{2,1,0:T(8,128)(2,1)}, u32[]{:S(2)}) copy-start(bf16[32,128,128]{2,1,0:T(8,128)(2,1)} %get-tuple-element.108.refs_13_) | copy-start | bytes 3145732
  (19 other events, 94.3 us)
